TPU v7x, 128 devices: a whole 4x4x4 slice. The times are simulated.
128 devices in a mesh: lat: 8 (over z, x_lo), lon: 16 (over y, x_hi, core).
Axes of the slice: x: 4 (x_hi: 2, x_lo: 2; x = x_hi * 2 + x_lo), y: 4, z: 4, core: 2. Of those that a mesh axis runs over, the one named last changes fastest.
Arguments:
- latents: bfloat16 [2, 96, 576, 1024], P(None, 'lat', None, 'lon'), may hold values from -6 to 6
- land_mask: int32 [2, 96, 576], P(None, 'lat'), may hold values 0 or 1
- norm_gain: float32 [1024], replicated, may hold values from 0.5 to 5
- qkv_weight: bfloat16 [1024, 3072], replicated, may hold values from -0.1875 to 0.1875
- out_weight: bfloat16 [1024, 1024], replicated, may hold values from -0.1875 to 0.1875
- out_cotangent: bfloat16 [2, 96, 576, 1024], P(None, 'lat', 'lon'), may hold values from -6 to 6
Outputs:
- block_out: bfloat16 [2, 96, 576, 1024], P(None, 'lat', 'lon')
- latent_grad: bfloat16 [2, 96, 576, 1024], P(None, 'lat', None, 'lon')
- qkv_weight_grad: float32 [1024, 3072], P(('lat', 'lon'))
- out_weight_grad: float32 [1024, 1024], P(('lat', 'lon'))
- gain_grad: float32 [1024], P(('lat', 'lon'))
Inputs may be any that keep to these rules, and one draw needn't show every extreme that they name: `land_mask`: 1 marks land.
All inputs are finite; a program needn't handle non-finite values. No bound on the sum of `land_mask` on one device may be relied on, other than what follows from the above.
Results may differ from a plain program's by a relative error of at most 0.0085.
The roundings to bfloat16 on the way count: a program that leaves them out, or rounds other values in their place, can miss the bound.
Values may be sent and summed in bfloat16 or wider, within the bound.
No kernel may reach another device: no remote copies, remote signals or barrier semaphores. Data moves between devices by JAX's collectives and lax.ppermute only.
A program may use at most 192 MiB of HBM per device.

v0:
```python
import jax
import jax.numpy as jnp
from jax import lax
from jax.sharding import PartitionSpec as P

HEADS = 16
WLAT = 6
WLON = 12
SHIFT = 6


def from_behind(x, axis, by):
    devices = lax.axis_size(axis)
    return lax.ppermute(x, axis, [(i, (i + by) % devices) for i in range(devices)])


def layer_norm(flat):
    values_f = flat.astype(jnp.float32)
    centred = values_f - jnp.mean(values_f, axis=-1, keepdims=True)
    variance = jnp.mean(centred * centred, axis=-1, keepdims=True)
    inv_scale = lax.rsqrt(variance + 1e-05)
    return (centred * inv_scale, inv_scale)


def to_windows(grid):
    levels, lat_rows, lon_cols, feat_dim = grid.shape
    grid = grid.reshape(levels, lat_rows // WLAT, WLAT, lon_cols // WLON, WLON, feat_dim)
    grid = grid.transpose(1, 3, 0, 2, 4, 5)
    return grid.reshape(-1, levels * WLAT * WLON, feat_dim)


def from_windows(windows, levels, lat_rows, lon_cols):
    feat_dim = windows.shape[-1]
    grid = windows.reshape(lat_rows // WLAT, lon_cols // WLON, levels, WLAT, WLON, feat_dim)
    return grid.transpose(2, 0, 3, 1, 4, 5).reshape(levels, lat_rows, lon_cols, feat_dim)


def window_pass(projected, upstream, mask_win):
    batch, win_tokens, triple = projected.shape
    feat_dim = triple // 3
    head_dim = feat_dim // HEADS
    factor = head_dim ** (-0.5)
    queries = projected[..., :feat_dim].reshape(batch, win_tokens, HEADS, head_dim)
    key_rows = projected[..., feat_dim : 2 * feat_dim].reshape(batch, win_tokens, HEADS, head_dim)
    value_rows = projected[..., 2 * feat_dim :].reshape(batch, win_tokens, HEADS, head_dim)
    scores = (
        jnp.einsum("bqhe,bkhe->bhqk", queries, key_rows, preferred_element_type=jnp.float32)
        * factor
    )
    allowed = (mask_win[:, None, None, :] == 1) | jnp.eye(win_tokens, dtype=bool)[None, None]
    scores = jnp.where(allowed, scores, -jnp.inf)
    highest = jnp.max(scores, axis=-1, keepdims=True)
    raised = jnp.exp(scores - highest)
    prob_full = raised / jnp.sum(raised, axis=-1, keepdims=True)
    prob_half = prob_full.astype(jnp.bfloat16)
    attended = jnp.einsum(
        "bhqk,bkhe->bqhe", prob_half, value_rows, preferred_element_type=jnp.float32
    )
    attended = attended.reshape(batch, win_tokens, feat_dim).astype(jnp.bfloat16)
    grad_heads = upstream.reshape(batch, win_tokens, HEADS, head_dim)
    prob_grad = jnp.einsum(
        "bqhe,bkhe->bhqk", grad_heads, value_rows, preferred_element_type=jnp.float32
    )
    inner = jnp.sum(prob_full * prob_grad, axis=-1, keepdims=True)
    score_grad = (prob_full * (prob_grad - inner) * factor).astype(jnp.bfloat16)
    query_grad = jnp.einsum(
        "bhqk,bkhe->bqhe", score_grad, key_rows, preferred_element_type=jnp.float32
    )
    key_grad = jnp.einsum(
        "bhqk,bqhe->bkhe", score_grad, queries, preferred_element_type=jnp.float32
    )
    value_grad = jnp.einsum(
        "bhqk,bqhe->bkhe", prob_half, grad_heads, preferred_element_type=jnp.float32
    )
    qkv_grad = jnp.concatenate(
        [
            query_grad.reshape(batch, win_tokens, feat_dim),
            key_grad.reshape(batch, win_tokens, feat_dim),
            value_grad.reshape(batch, win_tokens, feat_dim),
        ],
        axis=-1,
    )
    return (attended, qkv_grad.astype(jnp.bfloat16))


def per_device(latents, land_mask, norm_gain, qkv_weight, out_weight, out_cotangent):
    lon_index = lax.axis_index("lon")
    tile_cols = out_cotangent.shape[2]
    tile = lax.all_to_all(latents, "lon", split_axis=2, concat_axis=3, tiled=True)
    border = from_behind(tile[:, :, :SHIFT], "lon", -1)
    rolled = jnp.concatenate([tile[:, :, SHIFT:], border], axis=2)
    mask_whole = jnp.roll(land_mask, -SHIFT, axis=2)
    mask_rolled = lax.dynamic_slice_in_dim(mask_whole, lon_index * tile_cols, tile_cols, 2)
    levels, lat_rows, lon_cols, feat_dim = rolled.shape
    flat = rolled.reshape(-1, feat_dim)
    normed, inv_scale = layer_norm(flat)
    scaled = (normed * norm_gain).astype(jnp.bfloat16)
    projected = jnp.dot(scaled, qkv_weight, preferred_element_type=jnp.float32).astype(jnp.bfloat16)
    upstream_flat = out_cotangent.reshape(-1, feat_dim)
    out_grad = jnp.dot(upstream_flat, out_weight.T, preferred_element_type=jnp.float32).astype(
        jnp.bfloat16
    )
    qkv_win = to_windows(projected.reshape(levels, lat_rows, lon_cols, 3 * feat_dim))
    grad_win = to_windows(out_grad.reshape(levels, lat_rows, lon_cols, feat_dim))
    mask_win = to_windows(mask_rolled[..., None])[..., 0]
    attended, qkv_grad = window_pass(qkv_win, grad_win, mask_win)
    attended = from_windows(attended, levels, lat_rows, lon_cols).reshape(-1, feat_dim)
    qkv_grad = from_windows(qkv_grad, levels, lat_rows, lon_cols).reshape(-1, 3 * feat_dim)
    block_out = (
        flat.astype(jnp.float32) + jnp.dot(attended, out_weight, preferred_element_type=jnp.float32)
    ).astype(jnp.bfloat16)
    block_out = block_out.reshape(levels, lat_rows, lon_cols, feat_dim)
    norm_grad = jnp.dot(qkv_grad, qkv_weight.T, preferred_element_type=jnp.float32)
    gain_grad = jnp.sum(norm_grad * normed, axis=0)
    out_weight_grad = jnp.dot(attended.T, upstream_flat, preferred_element_type=jnp.float32)
    qkv_weight_grad = jnp.dot(scaled.T, qkv_grad, preferred_element_type=jnp.float32)
    qkv_weight_part, out_weight_part, gain_part = (
        lax.psum_scatter(qkv_weight_grad, ("lat", "lon"), scatter_dimension=0, tiled=True),
        lax.psum_scatter(out_weight_grad, ("lat", "lon"), scatter_dimension=0, tiled=True),
        lax.psum_scatter(gain_grad, ("lat", "lon"), scatter_dimension=0, tiled=True),
    )
    scaled_grad = norm_grad * norm_gain
    input_grad = inv_scale * (
        scaled_grad
        - jnp.mean(scaled_grad, axis=-1, keepdims=True)
        - normed * jnp.mean(scaled_grad * normed, axis=-1, keepdims=True)
    )
    rolled_grad = (upstream_flat.astype(jnp.float32) + input_grad).astype(jnp.bfloat16)
    rolled_grad = rolled_grad.reshape(levels, lat_rows, lon_cols, feat_dim)
    carried = from_behind(rolled_grad[:, :, lon_cols - SHIFT :], "lon", 1)
    tile_grad = jnp.concatenate([carried, rolled_grad[:, :, : lon_cols - SHIFT]], axis=2)
    returned = lax.all_to_all(tile_grad, "lon", split_axis=3, concat_axis=2, tiled=True)
    return (block_out, returned, qkv_weight_part, out_weight_part, gain_part)


def solution(mesh):
    return jax.shard_map(
        per_device,
        mesh=mesh,
        in_specs=(
            P(None, "lat", None, "lon"),
            P(None, "lat", None),
            P(),
            P(),
            P(),
            P(None, "lat", "lon", None),
        ),
        out_specs=(
            P(None, "lat", "lon", None),
            P(None, "lat", None, "lon"),
            P(("lat", "lon"), None),
            P(("lat", "lon"), None),
            P(("lat", "lon")),
        ),
        check_vma=False,
    )
```

profile of v0, /device:TPU:0, one launch (start us, length us, event | category | flops | bytes accessed | tf_op | source)
XLA Modules:
  0.0 1527.1 jit_solution(17001084574198316804)
XLA Ops:
  7.2 8.7 copy.111
  15.9 7.4 reshape.196
  23.3 7.2 all-to-all-start
  38.0 18.3 %all-to-all-done = bf16[16,2,27648]{2,1,0:T(2,128)(2,1)} async-done(((bf16[16,2,27648]{2,1,0:T(2,128)(2,1)}), bf16[16,2,27648]{2,1,0:T(2,128)(2,1)}, u32[]{:S(2)}, u32[]{:S(2)}) %all-to-all-start) | async-done | bytes 1769504 | tf_op jit(solution)/shard_map/all_to_all | solution.py:89
  56.3 7.1 reshape.197
  71.3 6.7 all_to_all.29
  97.1 10.9 convolution_convert_fusion
  108.0 8.3 reshape_reshape.15
  116.3 6.9 copy.120
  123.3 8.5 reshape.188
  150.7 13.1 fusion.43
  163.8 8.8 convert_bitcast_fusion.3
  223.7 10.1 fusion.44
  233.7 24.1 %convert_bitcast_fusion.2 = bf16[6,144,16,64]{1,3,2,0:T(8,128)(2,1)} fusion(bf16[6,144,16,64]{1,3,2,0:T(8,128)(2,1)} %bitcast.79, f32[6,16,144,144]{2,3,1,0:T(8,128)} %fusion.44, f32[6,16,144,144]{2,3,1,0:T(8,128)} %get-tuple-element.39, f32[6,16,144]{2,1,0:T(8,128)S(1)} %get-tuple-element.38), kind=kOutput, calls=%fused_computation.32 | convolution fusion | flops 269637248 | bytes 19519488 | tf_op jit(solution)/shard_map/bhqk,bkhe->bqhe/dot_general | solution.py:66
  257.8 6.5 copy.132
  270.5 24.3 %convert_bitcast_fusion.1 = bf16[6,144,16,64]{1,3,2,0:T(8,128)(2,1)} fusion(bf16[6,144,16,64]{1,3,2,0:T(8,128)(2,1)} %bitcast.77, f32[6,16,144,144]{2,3,1,0:T(8,128)} %fusion.44, f32[6,16,144,144]{2,3,1,0:T(8,128)} %get-tuple-element.39, f32[6,16,144]{2,1,0:T(8,128)S(1)} %get-tuple-element.38), kind=kOutput, calls=%fused_computation.31 | convolution fusion | flops 269637248 | bytes 19519488 | tf_op jit(solution)/shard_map/bhqk,bqhe->bkhe/dot_general | solution.py:69
  294.7 6.5 copy.134
  307.4 10.2 convert_bitcast_fusion
  317.6 6.5 copy.137
  338.0 8.5 reshape_reshape.19
  355.8 11.9 fusion.45
  368.4 10.9 multiply_reduce_fusion.1
  389.7 8.1 collective-permute-done.1
  399.9 16.0 %copy.139 = bf16[2,12,36,1024]{2,0,1,3:T(2,128)(2,1)} copy(bf16[2,12,36,1024]{3,2,1,0:T(8,128)(2,1)} %pad_maximum_fusion) | data formatting | bytes 3538944 | tf_op jit(solution)/shard_map/concatenate | solution.py:131
  416.0 14.9 reshape.198
  449.3 69.9 %all-reduce = f32[1024]{0:T(1024)S(1)} all-reduce(f32[1024]{0:T(1024)S(1)} %get-tuple-element.30), channel_id=4, replica_groups=mesh['lat'=8,'lon'=16] {'lat','lon'}, use_global_device_ids=true, to_apply=%region_10.11.clone | all-reduce | flops 1024 | bytes 8192
  519.8 19.3 %reshape.199 = bf16[1024,12,2,36]{3,2,1,0:T(2,128)(2,1)} reshape(bf16[16,2,27648]{2,1,0:T(2,128)(2,1)} %all-to-all-done.1) | data formatting | bytes 3538944
  539.0 17.0 %copy.150 = bf16[2,12,36,16,64]{4,3,0,2,1:T(8,128)(2,1)} copy(bf16[2,12,36,16,64]{2,0,1,4,3:T(2,128)(2,1)} %bitcast.65) | data formatting | bytes 3538944 | tf_op jit(solution)/shard_map/all_to_all | solution.py:132
  556.0 7.0 copy.141
  563.1 8.6 copy.145
  571.7 292.6 %reduce-scatter.5.cloned.1.call-done = f32[8,1024]{1,0:T(8,128)} async-done(((f32[1024,1024]{1,0:T(8,128)}), f32[8,1024]{1,0:T(8,128)}) %reduce-scatter.5.cloned.1.call-update) | async-done | bytes 32784 | tf_op jit(solution)/shard_map/reduce_scatter | solution.py:119
  864.3 655.6 %reduce-scatter.3.cloned.1.call-done = f32[8,3072]{1,0:T(8,128)} async-done(((f32[1024,3072]{1,0:T(8,128)}), f32[8,3072]{1,0:T(8,128)}) %reduce-scatter.3.cloned.1.call-update) | async-done | bytes 98320 | tf_op jit(solution)/shard_map/reduce_scatter | solution.py:118
  (96 shorter events, 172.0 us)
Async XLA Ops:
  7.2 191.9 %copy-start = (bf16[1024,1024]{1,0:T(8,128)(2,1)S(1)}, bf16[1024,1024]{1,0:T(8,128)(2,1)}, u32[]{:S(2)}) copy-start(bf16[1024,1024]{1,0:T(8,128)(2,1)} %param.10) | copy-start | bytes 6291460
  15.9 14.6 copy-start.8
  15.9 14.8 slice-start.2
  23.3 33.0 %all-to-all-start = ((bf16[16,2,27648]{2,1,0:T(2,128)(2,1)}), bf16[16,2,27648]{2,1,0:T(2,128)(2,1)}, u32[]{:S(2)}, u32[]{:S(2)}) async-start(bf16[16,2,27648]{2,1,0:T(2,128)(2,1)} %reshape.196), calls=%async_computation | async-start | bytes 3538944 | tf_op jit(solution)/shard_map/all_to_all | solution.py:89
  30.4 833.8 %reduce-scatter.5.cloned.1.call-start = ((), (), s32[]{:S(2)}) async-start(), calls=%async_computation.5 | async-start | bytes 4227072 | tf_op jit(solution)/shard_map/reduce_scatter | solution.py:119
  78.1 5.9 slice-start.1
  79.3 4.6 collective-permute-start
  86.4 2.6 copy-start.1
  86.5 5.1 copy-start.4
  91.8 5.1 copy-start.6
  92.1 4.9 copy-start.10
  92.1 4.9 copy-start.9
  97.1 11.0 copy-start.12
  199.0 1320.9 %reduce-scatter.3.cloned.1.call-start = ((), (), s32[]{:S(2)}) async-start(), calls=%async_computation.4 | async-start | bytes 12681216 | tf_op jit(solution)/shard_map/reduce_scatter | solution.py:118
  338.0 8.5 copy-start.5
  338.0 8.5 copy-start.7
  367.7 0.7 copy-start.11
  367.7 0.7 copy-start.13
  368.4 10.9 copy-start.2
  368.4 10.9 copy-start.3
  385.4 12.4 slice-start
  386.8 11.0 collective-permute-start.1
  430.9 88.9 %all-to-all-start.1 = ((bf16[16,2,27648]{2,1,0:T(2,128)(2,1)}), bf16[16,2,27648]{2,1,0:T(2,128)(2,1)}, u32[]{:S(2)}, u32[]{:S(2)}) async-start(bf16[16,2,27648]{2,1,0:T(2,128)(2,1)} %reshape.198), calls=%async_computation.1 | async-start | bytes 3538944 | tf_op jit(solution)/shard_map/all_to_all | solution.py:132
Sparse Core Ops, SparseCore 0:
  199.1 665.1 reduce-scatter.4
  867.4 652.4 reduce-scatter.2
where the time goes:
time: 1540 us; the launch traced here: 1530 us
  waiting for transfers between devices  979 us (64%)
  local copies, waits for them, and re-layouts  290 us (19%)
  matrix products  141 us (9%)
  blocking collectives  69.9 us (5%)
  other arithmetic  17.8 us (1%)
    reduce_scatter x1, waiting for transfers between devices, per_device(): lax.psum_scatter(qkv_weight_grad, ('lat', 'lon'), scatter_dimension=0, ti...  656 us
    reduce_scatter x1, waiting for transfers between devices, per_device(): lax.psum_scatter(out_weight_grad, ('lat', 'lon'), scatter_dimension=0, ti...  293 us
    unnamed x37, local copies, waits for them, and re-layouts  75.1 us
    unnamed x1, blocking collectives  69.9 us
  transfers between devices with their start and end apart: 6, of which 5 were waited for; matrix products, arithmetic and copies ran while one was open for 19% of the time, Pallas kernels for 0%

commit v1 on v0

v1 whole, which is shorter than its diff:
```python
import functools

import jax
import jax.numpy as jnp
from jax import lax
from jax.experimental import pallas as pl
from jax.experimental.pallas import tpu as pltpu
from jax.sharding import PartitionSpec as P

F32 = jnp.float32
BF16 = jnp.bfloat16
D = 1024
HEAD = 64
WIN = 144
HALF = 72
WINS = 6
TOK = WIN * WINS
SHIFT = 6
LON = 576
GROUPS = 4
GW = D // GROUPS
SCALE = HEAD**-0.5
LOG2E = 1.4426950408889634
MIB = 1 << 20
AXES = ("lat", "lon")


def nn(a, b):
    return lax.dot_general(a, b, (((1,), (0,)), ((), ())), preferred_element_type=F32)


def nt(a, b):
    return lax.dot_general(a, b, (((1,), (1,)), ((), ())), preferred_element_type=F32)


def params(mib):
    return pltpu.CompilerParams(vmem_limit_bytes=mib * MIB)


def cost(flops, nbytes):
    return pl.CostEstimate(flops=int(flops), bytes_accessed=int(nbytes), transcendentals=0)


def vmem(n):
    return [pl.BlockSpec(memory_space=pltpu.VMEM)] * n


def split_kernel(z_ref, out_ref, t_ref, s_ref):
    row = lax.broadcasted_iota(jnp.int32, (LON, LON), 0)
    col = lax.broadcasted_iota(jnp.int32, (LON, LON), 1)
    source = row + SHIFT
    source = jnp.where(source >= LON, source - LON, source)
    pick = (col == source).astype(BF16)
    for r in range(12):
        both = jnp.concatenate([z_ref[0, r], z_ref[1, r]], axis=0)
        t_ref[...] = nt(pick, both)
        for v in range(48):
            at = ((r // 6) * 3 + v % 3) * HALF + (r % 6) * 12
            s_ref[v // 3, at : at + 12, :] = t_ref[12 * v : 12 * v + 12, :]
    for k in range(16):
        out_ref[k] = s_ref[k].astype(BF16)


def split_pieces(z):
    return pl.pallas_call(
        split_kernel,
        out_shape=jax.ShapeDtypeStruct((16, 6 * HALF, 128), BF16),
        in_specs=vmem(1),
        out_specs=vmem(1)[0],
        scratch_shapes=[pltpu.VMEM((LON, 128), F32), pltpu.VMEM((16, 6 * HALF, 128), F32)],
        compiler_params=params(32),
        cost_estimate=cost(2e9, 4e6),
        name="split_pieces",
    )(z)


def norm_parts(x):
    centred = x - jnp.sum(x, axis=-1, keepdims=True) * (1.0 / D)
    variance = jnp.sum(centred * centred, axis=-1, keepdims=True) * (1.0 / D)
    inv_scale = lax.rsqrt(variance + 1e-05)
    return centred * inv_scale, inv_scale


def enter_kernel(r_ref, gain_ref, pick_ref, x_ref, scaled_ref, scaled_t_ref, xs_ref):
    low = lax.broadcasted_iota(jnp.int32, (6 * HALF, 128), 1) < HEAD
    for p in range(8):
        first = r_ref[2 * p].astype(F32)
        second = r_ref[2 * p + 1].astype(F32)
        level0 = jnp.where(low, first, pltpu.roll(second, HEAD, 1))
        level1 = jnp.where(low, pltpu.roll(first, HEAD, 1), second)
        for w in range(WINS):
            at = w * WIN
            xs_ref[at : at + HALF, 128 * p : 128 * p + 128] = level0[HALF * w : HALF * w + HALF]
            xs_ref[at + HALF : at + WIN, 128 * p : 128 * p + 128] = level1[HALF * w : HALF * w + HALF]

    def rows(i, _):
        at = pl.ds(pl.multiple_of(i * 48, 48), 48)
        x = xs_ref[at, :]
        x_ref[at, :] = x.astype(BF16)
        normed, _ = norm_parts(x)
        scaled_ref[at, :] = (normed * gain_ref[...]).astype(BF16)
        return 0

    lax.fori_loop(0, TOK // 48, rows, 0)

    def turn(i, _):
        at = pl.ds(pl.multiple_of(i * 256, 256), 256)
        scaled_t_ref[at, :] = nt(pick_ref[at, :], scaled_ref[...]).astype(BF16)
        return 0

    lax.fori_loop(0, 4, turn, 0)


def enter(pieces, gain, pick):
    return pl.pallas_call(
        enter_kernel,
        out_shape=(
            jax.ShapeDtypeStruct((TOK, D), BF16),
            jax.ShapeDtypeStruct((TOK, D), BF16),
            jax.ShapeDtypeStruct((D, TOK), BF16),
        ),
        in_specs=vmem(3),
        out_specs=tuple(vmem(3)),
        scratch_shapes=[pltpu.VMEM((TOK, D), F32)],
        compiler_params=params(32),
        cost_estimate=cost(3e9, 9e6),
        name="enter",
    )(pieces, gain, pick)


def attend_kernel(
    scaled_ref, scaled_t_ref, up_ref, wq_ref, wk_ref, wv_ref, wo_ref, mask_ref,
    att_ref, grad_ref, keep_ref, send_ref, q_ref, k_ref, v_ref, o_ref,
):
    for w_ref, p_ref in ((wq_ref, q_ref), (wk_ref, k_ref), (wv_ref, v_ref)):
        p_ref[...] = nn(scaled_ref[...], w_ref[...]).astype(BF16)
    o_ref[...] = nt(up_ref[...], wo_ref[...]).astype(BF16)

    same = lax.broadcasted_iota(jnp.int32, (WIN, WIN), 0) == lax.broadcasted_iota(
        jnp.int32, (WIN, WIN), 1
    )
    lane = lax.broadcasted_iota(jnp.int32, (WIN, 128), 1)
    zero = jnp.zeros((WIN, 128), BF16)

    def window(i, _):
        at = pl.ds(pl.multiple_of(i * WIN, WIN), WIN)
        bias = jnp.where(same, 0.0, mask_ref[at, :])
        for pair in range(GW // 128):
            cols = slice(128 * pair, 128 * pair + 128)
            q, k, v, o = q_ref[at, cols], k_ref[at, cols], v_ref[at, cols], o_ref[at, cols]
            k_t = (k * BF16(SCALE)).T
            v_t = v.T
            att_t, dq_t, dk, dv = [], [], None, None
            for h in range(2):
                mine = (lane < HEAD) if h == 0 else (lane >= HEAD)
                q_h = jnp.where(mine, q, zero)
                o_h = jnp.where(mine, o, zero)
                part = slice(HEAD * h, HEAD * h + HEAD)
                scores = nt(k, q_h) * (SCALE * LOG2E) + bias
                raised = jnp.exp2(scores - jnp.max(scores, axis=0, keepdims=True))
                prob = raised * (1.0 / jnp.sum(raised, axis=0, keepdims=True))
                prob_half = prob.astype(BF16)
                att_t.append(nn(v_t[part], prob_half))
                prob_grad = nt(v, o_h)
                inner = jnp.sum(prob * prob_grad, axis=0, keepdims=True)
                score_grad = (prob * (prob_grad - inner)).astype(BF16)
                dq_t.append(nn(k_t[part], score_grad))
                dk_h = nn(score_grad, q_h * BF16(SCALE))
                dv_h = nn(prob_half, o_h)
                dk = dk_h if dk is None else dk + dk_h
                dv = dv_h if dv is None else dv + dv_h
            att_ref[at, cols] = jnp.concatenate(att_t, axis=0).astype(BF16).T
            base = 128 * pair
            grad_ref[at, base : base + 128] = jnp.concatenate(dq_t, axis=0).astype(BF16).T
            grad_ref[at, GW + base : GW + base + 128] = dk.astype(BF16)
            grad_ref[at, 2 * GW + base : 2 * GW + base + 128] = dv.astype(BF16)
        return 0

    lax.fori_loop(0, WINS, window, 0)

    def weights(i, _):
        at = pl.ds(pl.multiple_of(i * 256, 256), 256)
        keep_ref[at, :] = nn(scaled_t_ref[at, :], grad_ref[...])
        far = pl.ds(pl.multiple_of(i * 256 + 512, 256), 256)
        send_ref[at, :] = nn(scaled_t_ref[far, :], grad_ref[...])
        return 0

    lax.fori_loop(0, 2, weights, 0)


def attend(g, scaled, scaled_t, up, qkv_weight, out_weight, mask):
    full = lambda shape: pl.BlockSpec(shape, lambda i: (0, 0))
    return pl.pallas_call(
        attend_kernel,
        grid=(1,),
        out_shape=(
            jax.ShapeDtypeStruct((TOK, GW), BF16),
            jax.ShapeDtypeStruct((TOK, 3 * GW), BF16),
            jax.ShapeDtypeStruct((D // 2, 3 * GW), F32),
            jax.ShapeDtypeStruct((D // 2, 3 * GW), F32),
        ),
        in_specs=[
            full((TOK, D)),
            full((D, TOK)),
            full((TOK, D)),
            pl.BlockSpec((D, GW), lambda i: (0, g)),
            pl.BlockSpec((D, GW), lambda i: (0, GROUPS + g)),
            pl.BlockSpec((D, GW), lambda i: (0, 2 * GROUPS + g)),
            pl.BlockSpec((GW, D), lambda i: (g, 0)),
            full((TOK, 1)),
        ],
        out_specs=(
            full((TOK, GW)),
            full((TOK, 3 * GW)),
            full((D // 2, 3 * GW)),
            full((D // 2, 3 * GW)),
        ),
        scratch_shapes=[pltpu.VMEM((TOK, GW), BF16)] * 4,
        compiler_params=params(48),
        cost_estimate=cost(8e9, 15e6),
        name="attend",
    )(scaled, scaled_t, up, qkv_weight, qkv_weight, qkv_weight, out_weight, mask)


def out_grad_kernel(a0, a1, a2, a3, up_ref, pick_ref, keep_ref, send_ref, t_ref):
    for g, a in enumerate((a0, a1, a2, a3)):
        piece = nt(pick_ref[:, GW * g : GW * g + GW], a[...])
        t_ref[...] = piece if g == 0 else t_ref[...] + piece

    def rows(i, _):
        at = pl.ds(pl.multiple_of(i * 256, 256), 256)
        keep_ref[at, :] = nn(t_ref[at, :].astype(BF16), up_ref[...])
        far = pl.ds(pl.multiple_of(i * 256 + 512, 256), 256)
        send_ref[at, :] = nn(t_ref[far, :].astype(BF16), up_ref[...])
        return 0

    lax.fori_loop(0, 2, rows, 0)


def out_weight_sum(att, up, pick):
    return pl.pallas_call(
        out_grad_kernel,
        out_shape=(
            jax.ShapeDtypeStruct((D // 2, D), F32),
            jax.ShapeDtypeStruct((D // 2, D), F32),
        ),
        in_specs=vmem(6),
        out_specs=tuple(vmem(2)),
        scratch_shapes=[pltpu.VMEM((D, TOK), F32)],
        compiler_params=params(40),
        cost_estimate=cost(4e9, 10e6),
        name="out_weight_sum",
    )(*att, up, pick)


def block_kernel(a0, a1, a2, a3, x_ref, w_ref, out_ref):
    def rows(i, _):
        at = pl.ds(pl.multiple_of(i * 432, 432), 432)
        total = x_ref[at, :].astype(F32)
        for g, a in enumerate((a0, a1, a2, a3)):
            total = total + nn(a[at, :], w_ref[GW * g : GW * g + GW, :])
        out_ref[at, :] = total.astype(BF16)
        return 0

    lax.fori_loop(0, 2, rows, 0)


def block_sum(att, x, out_weight):
    return pl.pallas_call(
        block_kernel,
        out_shape=jax.ShapeDtypeStruct((TOK, D), BF16),
        in_specs=vmem(6),
        out_specs=vmem(1)[0],
        compiler_params=params(32),
        cost_estimate=cost(2e9, 8e6),
        name="block_sum",
    )(*att, x, out_weight)


def leave_kernel(g0, g1, g2, g3, w_ref, x_ref, up_ref, gain_ref, out_ref, gain_out_ref, n_ref):
    def product(i, _):
        at = pl.ds(pl.multiple_of(i * 432, 432), 432)
        total = None
        for g, d in enumerate((g0, g1, g2, g3)):
            for part in range(3):
                base = part * D + g * GW
                piece = nt(d[at, part * GW : part * GW + GW], w_ref[:, base : base + GW])
                total = piece if total is None else total + piece
        n_ref[at, :] = total
        return 0

    lax.fori_loop(0, 2, product, 0)

    def rows(i, gain_sum):
        at = pl.ds(pl.multiple_of(i * 48, 48), 48)
        normed, inv_scale = norm_parts(x_ref[at, :].astype(F32))
        n = n_ref[at, :]
        both = n * normed
        gain = gain_ref[...]
        g = n * gain
        mean_g = jnp.sum(g, axis=-1, keepdims=True) * (1.0 / D)
        mean_gn = jnp.sum(both * gain, axis=-1, keepdims=True) * (1.0 / D)
        n_ref[at, :] = up_ref[at, :].astype(F32) + inv_scale * (g - mean_g - normed * mean_gn)
        return gain_sum + jnp.sum(both.reshape(6, 8, D), axis=0)

    gain_sum = lax.fori_loop(0, TOK // 48, rows, jnp.zeros((8, D), F32))
    gain_out_ref[...] = jnp.sum(gain_sum, axis=0, keepdims=True)

    low = lax.broadcasted_iota(jnp.int32, (6 * HALF, 128), 1) < HEAD
    for p in range(8):
        cols = slice(128 * p, 128 * p + 128)
        level0 = jnp.concatenate([n_ref[WIN * w : WIN * w + HALF, cols] for w in range(WINS)], axis=0)
        level1 = jnp.concatenate([n_ref[WIN * w + HALF : WIN * w + WIN, cols] for w in range(WINS)], axis=0)
        out_ref[2 * p] = jnp.where(low, level0, pltpu.roll(level1, HEAD, 1)).astype(BF16)
        out_ref[2 * p + 1] = jnp.where(low, pltpu.roll(level0, HEAD, 1), level1).astype(BF16)


def leave(grads, qkv_weight, x, up, gain):
    return pl.pallas_call(
        leave_kernel,
        out_shape=(
            jax.ShapeDtypeStruct((16, 6 * HALF, 128), BF16),
            jax.ShapeDtypeStruct((1, D), F32),
        ),
        in_specs=vmem(8),
        out_specs=tuple(vmem(2)),
        scratch_shapes=[pltpu.VMEM((TOK, D), F32)],
        compiler_params=params(44),
        cost_estimate=cost(6e9, 18e6),
        name="leave",
    )(*grads, qkv_weight, x, up, gain)


def join_kernel(r_ref, out_ref, s_ref, t_ref):
    for k in range(16):
        s_ref[k] = r_ref[k].astype(F32)
    same = lax.broadcasted_iota(jnp.int32, (128, 128), 0) == lax.broadcasted_iota(
        jnp.int32, (128, 128), 1
    )
    same = same.astype(BF16)
    for r in range(12):
        for v in range(48):
            at = ((r // 6) * 3 + v % 3) * HALF + (r % 6) * 12
            to = 12 * v + SHIFT
            if to + 12 <= LON:
                t_ref[to : to + 12, :] = s_ref[v // 3, at : at + 12, :]
            else:
                t_ref[to:LON, :] = s_ref[v // 3, at : at + LON - to, :]
                t_ref[0 : to + 12 - LON, :] = s_ref[v // 3, at + LON - to : at + 12, :]
        turned = nt(same, t_ref[...].astype(BF16)).astype(BF16)
        out_ref[0, r] = turned[:HEAD]
        out_ref[1, r] = turned[HEAD:]


def join_pieces(pieces):
    return pl.pallas_call(
        join_kernel,
        out_shape=jax.ShapeDtypeStruct((2, 12, HEAD, LON), BF16),
        in_specs=vmem(1),
        out_specs=vmem(1)[0],
        scratch_shapes=[pltpu.VMEM((16, 6 * HALF, 128), F32), pltpu.VMEM((LON, 128), F32)],
        compiler_params=params(32),
        cost_estimate=cost(2e9, 4e6),
        name="join_pieces",
    )(pieces)


def device_index(x, y, z, core):
    return ((z * 2 + x % 2) * 4 + y) * 4 + (x // 2) * 2 + core


def moved(dz=0, dx=0, dy=0, core=0):
    pairs = []
    for x in range(4):
        for y in range(4):
            for z in range(4):
                for c in range(2):
                    to = device_index((x + dx) % 4, (y + dy) % 4, (z + dz) % 4, c ^ core)
                    pairs.append((device_index(x, y, z, c), to))
    return sorted(pairs)


def ship(a, **by):
    return lax.ppermute(a, AXES, moved(**by))


def scatter_sum(keep, send, order):
    names = ["dz", "dx", "dy"]
    wide = keep.shape[-1]
    terms = [keep.reshape(4, 4, 4, 8, wide), ship(send, core=1).reshape(4, 4, 4, 8, wide)]
    for axis in order:
        at = names.index(axis)
        names.pop(at)

        def cut(d):
            total = None
            for t in terms:
                piece = lax.index_in_dim(t, d, at, keepdims=False)
                total = piece if total is None else total + piece
            return total

        terms = [cut(0)] + [ship(cut(d), **{axis: d}) for d in (1, 2, 3)]
    return functools.reduce(lambda a, b: a + b, terms)


def row_picks():
    lat, lon = lax.axis_index("lat"), lax.axis_index("lon")
    z, xl = lat // 2, lat % 2
    y, xh, c = lon // 4, (lon // 2) % 2, lon % 2
    x = xh * 2 + xl
    i = jnp.arange(D, dtype=jnp.int32)
    tc = (c + i // 512) % 2
    tz = (z + (i // 128) % 4) % 4
    tx = (x + (i // 32) % 4) % 4
    ty = (y + (i // 8) % 4) % 4
    block = ((tz * 2 + tx % 2) * 4 + ty) * 4 + (tx // 2) * 2 + tc
    source = block * 8 + i % 8
    return (source[:, None] == jnp.arange(D, dtype=jnp.int32)[None, :]).astype(BF16)


def window_order(a):
    a = a.reshape((2, 2, 6, 3, 12) + a.shape[3:])
    return a.transpose((1, 3, 0, 2, 4) + tuple(range(5, a.ndim)))


def per_device(latents, land_mask, norm_gain, qkv_weight, out_weight, out_cotangent):
    lon_index = lax.axis_index("lon")
    pieces = split_pieces(latents.transpose(0, 1, 3, 2))
    pieces = lax.all_to_all(pieces, "lon", split_axis=0, concat_axis=0, tiled=True)
    pick = row_picks()
    mask = jnp.roll(land_mask, -SHIFT, axis=2)
    mask = lax.dynamic_slice_in_dim(mask, lon_index * 36, 36, 2)
    mask = jnp.where(window_order(mask).reshape(TOK, 1) == 1, 0.0, -1e30).astype(F32)
    up = window_order(out_cotangent).reshape(TOK, D)
    gain = norm_gain.reshape(1, D)
    x, scaled, scaled_t = enter(pieces, gain, pick)
    att, grads, sums = [], [], []
    orders = (("dz", "dy", "dx"), ("dy", "dx", "dz"), ("dx", "dz", "dy"), ("dz", "dx", "dy"), ("dy", "dz", "dx"))
    for g in range(GROUPS):
        a, d, keep, send = attend(g, scaled, scaled_t, up, qkv_weight, out_weight, mask)
        att.append(a)
        grads.append(d)
        sums.append(scatter_sum(keep, send, orders[g]))
    back, gain_part = leave(grads, qkv_weight, x, up, gain)
    back = lax.all_to_all(back, "lon", split_axis=0, concat_axis=0, tiled=True)
    keep, send = out_weight_sum(att, up, pick)
    out_weight_grad = scatter_sum(keep, send, orders[4])
    gain_all = lax.all_to_all(gain_part.reshape(128, 8), AXES, split_axis=0, concat_axis=0, tiled=True)
    gain_grad = jnp.sum(gain_all, axis=0)
    block = block_sum(att, x, out_weight)
    block = block.reshape(2, 3, 2, 6, 12, D).transpose(2, 0, 3, 1, 4, 5).reshape(2, 12, 36, D)
    latent_grad = join_pieces(back).transpose(0, 1, 3, 2)
    qkv_weight_grad = jnp.stack(sums, axis=1).reshape(8, GROUPS, 3, GW)
    qkv_weight_grad = qkv_weight_grad.transpose(0, 2, 1, 3).reshape(8, 3 * D)
    return (block, latent_grad, qkv_weight_grad, out_weight_grad, gain_grad)


def solution(mesh):
    return jax.shard_map(
        per_device,
        mesh=mesh,
        in_specs=(
            P(None, "lat", None, "lon"),
            P(None, "lat", None),
            P(),
            P(),
            P(),
            P(None, "lat", "lon", None),
        ),
        out_specs=(
            P(None, "lat", "lon", None),
            P(None, "lat", None, "lon"),
            P(("lat", "lon"), None),
            P(("lat", "lon"), None),
            P(("lat", "lon")),
        ),
        check_vma=False,
    )
```

time: 1540 us -> 333 us (0.22)
  waiting for transfers between devices: 979 us -> 53.9 us
  local copies, waits for them, and re-layouts: 290 us -> 31.5 us
  matrix products: 141 us -> 0 us
  Pallas kernels: 0 us -> 114 us
  starting transfers between devices: 14.9 us -> 107 us
  blocking collectives: 69.9 us -> 0 us
    reduce_scatter x2 -> x0, waiting for transfers between devices: 948 us -> none  [the longest x1 656 us: per_device(): lax.psum_scatter(qkv_weight_grad, ('lat', 'lon'), scatter_dimension=0, ti...]
    dot_general x11 -> x0, matrix products: 128 us -> none  [the longest x1 24.3 us: window_pass(): jnp.einsum('bhqk,bqhe->bkhe', score_grad, queries, preferred_element_type...]
    pallas_call x0 -> x10, Pallas kernels: none -> 114 us  [the longest x4 72.3 us: attend(): pl.pallas_call(attend_kernel, grid=(1,), out_shape=(jax.ShapeDtypeStruct(...]
    ppermute x2 -> x50, starting transfers between devices: 3.27 us -> 85.8 us  [ship(): return lax.ppermute(a, AXES, moved(**by))]
    unnamed x1 -> x0, blocking collectives: 69.9 us -> none
    unnamed x37 -> x72, local copies, waits for them, and re-layouts: 75.1 us -> 18.8 us
    all_to_all x5 -> x1, local copies, waits for them, and re-layouts: 38.7 us -> 0.71 us  [per_device(): lax.all_to_all(gain_part.reshape(128, 8), AXES, split_axis=0, concat_axis...]
    another operation x6 -> x0, local copies, waits for them, and re-layouts: 37.1 us -> none  [the longest x2 12.5 us: window_pass(): grad_heads = upstream.reshape(batch, win_tokens, HEADS, head_dim)]
  transfers between devices with their start and end apart: 6 -> 53, of which waited for: 5 -> 15; matrix products, arithmetic and copies ran while one was open for 19% -> 10% of each run, Pallas kernels for 0% -> 14%
where the time goes in v1:
time: 333 us; the launch traced here: 329 us
  Pallas kernels  114 us (34%)
  starting transfers between devices  107 us (32%)
  waiting for transfers between devices  53.9 us (16%)
  local copies, waits for them, and re-layouts  31.5 us (9%)
  other arithmetic  21.1 us (6%)
    ppermute x50, starting transfers between devices, ship(): return lax.ppermute(a, AXES, moved(**by))  85.8 us
    pallas_call x4, Pallas kernels, attend(): pl.pallas_call(attend_kernel, grid=(1,), out_shape=(jax.ShapeDtypeStruct(...  72.3 us
    ppermute x50, waiting for transfers between devices, ship(): return lax.ppermute(a, AXES, moved(**by))  33.4 us
    all_to_all x1, waiting for transfers between devices, per_device(): lax.all_to_all(pieces, 'lon', split_axis=0, concat_axis=0, tiled=True)  20.5 us
    unnamed x72, local copies, waits for them, and re-layouts  18.8 us
    add x17, other arithmetic, cut(): total = piece if total is None else total + piece  17.9 us
    pallas_call x1, Pallas kernels, leave(): pl.pallas_call(leave_kernel, out_shape=(jax.ShapeDtypeStruct((16, 6 * HAL...  16.4 us
    pallas_call x1, Pallas kernels, enter(): pl.pallas_call(enter_kernel, out_shape=(jax.ShapeDtypeStruct((TOK, D), BF...  8.76 us
  transfers between devices with their start and end apart: 53, of which 15 were waited for; matrix products, arithmetic and copies ran while one was open for 10% of the time, Pallas kernels for 14%

profile of v1, /device:TPU:0, one launch (start us, length us, event | category | flops | bytes accessed | tf_op | source)
XLA Modules:
  0.0 329.4 jit_solution(4742236844429664034)
XLA Ops:
  2.2 4.2 %split_pieces.1 = bf16[16,432,128]{2,1,0:T(8,128)(2,1)} custom-call(bf16[2,12,64,576]{3,2,1,0:T(8,128)(2,1)S(1)} %bitcast.362), custom_call_target="tpu_custom_call" | custom-call | flops 2000000000 | bytes 4000000 | tf_op jit(solution)/shard_map/split_pieces/pallas_call | solution.py:65
  6.4 7.8 %all-to-all-start = ((bf16[16,432,128]{2,1,0:T(8,128)(2,1)}), bf16[16,432,128]{2,1,0:T(8,128)(2,1)}, u32[]{:S(2)}, u32[]{:S(2)}) async-start(bf16[16,432,128]{2,1,0:T(8,128)(2,1)} %split_pieces.1), calls=%async_computation | async-start | bytes 3538944 | tf_op jit(solution)/shard_map/all_to_all | solution.py:429
  19.5 20.5 %all-to-all-done.r_ref = bf16[16,432,128]{2,1,0:T(8,128)(2,1)} async-done(((bf16[16,432,128]{2,1,0:T(8,128)(2,1)}), bf16[16,432,128]{2,1,0:T(8,128)(2,1)}, u32[]{:S(2)}, u32[]{:S(2)}) %all-to-all-start) | async-done | bytes 1769504 | tf_op jit(solution)/shard_map/all_to_all | solution.py:429
  40.0 8.8 %enter.1 = (bf16[864,1024]{1,0:T(8,128)(2,1)S(1)}, bf16[864,1024]{1,0:T(8,128)(2,1)S(1)}, bf16[1024,864]{1,0:T(8,128)(2,1)S(1)}) custom-call(bf16[16,432,128]{2,1,0:T(8,128)(2,1)} %all-to-all-done.r_ref, f32[1,1024]{1,0:T(1,128)S(1)} %bitcast.363, bf16[1024,1024]{1,0:T(8,128)(2,1)S(1)} %fusion.pick_ref), custom_call_target="tpu_custom_call" | custom-call | flops 3000000000 | bytes 9000000 | tf_op jit(solution)/shard_map/enter/pallas_call | solution.py:115
  51.2 18.5 %attend.7 = (bf16[864,256]{1,0:T(8,128)(2,1)S(1)}, bf16[864,768]{1,0:T(8,128)(2,1)S(1)}, f32[512,768]{1,0:T(8,128)S(1)}, f32[512,768]{1,0:T(8,128)}) custom-call(bf16[864,1024]{1,0:T(8,128)(2,1)} %copy-done.21, bf16[1024,864]{1,0:T(8,128)(2,1)} %copy-done.20, bf16[864,1024]{1,0:T(8,128)(2,1)} %reshape.458.up_ref, bf16[1024,3072]{1,0:T(8,128)(2,1)} %w_ref.3, ...), custom_call_target="tpu_custom_call" | custom-call | flops 8000000000 | bytes 15000000 | tf_op jit(solution)/shard_map/attend/pallas_call | solution.py:193
  70.9 17.8 %attend.6 = (bf16[864,256]{1,0:T(8,128)(2,1)S(1)}, bf16[864,768]{1,0:T(8,128)(2,1)S(1)}, f32[512,768]{1,0:T(8,128)S(1)}, f32[512,768]{1,0:T(8,128)}) custom-call(bf16[864,1024]{1,0:T(8,128)(2,1)} %copy-done.21, bf16[1024,864]{1,0:T(8,128)(2,1)} %copy-done.20, bf16[864,1024]{1,0:T(8,128)(2,1)} %reshape.458.up_ref, bf16[1024,3072]{1,0:T(8,128)(2,1)} %w_ref.3, ...), custom_call_target="tpu_custom_call" | custom-call | flops 8000000000 | bytes 15000000 | tf_op jit(solution)/shard_map/attend/pallas_call | solution.py:193
  90.9 18.0 %attend.5 = (bf16[864,256]{1,0:T(8,128)(2,1)S(1)}, bf16[864,768]{1,0:T(8,128)(2,1)S(1)}, f32[512,768]{1,0:T(8,128)S(1)}, f32[512,768]{1,0:T(8,128)}) custom-call(bf16[864,1024]{1,0:T(8,128)(2,1)} %copy-done.21, bf16[1024,864]{1,0:T(8,128)(2,1)} %copy-done.20, bf16[864,1024]{1,0:T(8,128)(2,1)} %reshape.458.up_ref, bf16[1024,3072]{1,0:T(8,128)(2,1)} %w_ref.3, ...), custom_call_target="tpu_custom_call" | custom-call | flops 8000000000 | bytes 15000000 | tf_op jit(solution)/shard_map/attend/pallas_call | solution.py:193
  110.6 17.9 %attend.4 = (bf16[864,256]{1,0:T(8,128)(2,1)S(1)}, bf16[864,768]{1,0:T(8,128)(2,1)S(1)}, f32[512,768]{1,0:T(8,128)S(1)}, f32[512,768]{1,0:T(8,128)}) custom-call(bf16[864,1024]{1,0:T(8,128)(2,1)} %copy-done.21, bf16[1024,864]{1,0:T(8,128)(2,1)} %copy-done.20, bf16[864,1024]{1,0:T(8,128)(2,1)} %reshape.458.up_ref, bf16[1024,3072]{1,0:T(8,128)(2,1)} %w_ref.3, ...), custom_call_target="tpu_custom_call" | custom-call | flops 8000000000 | bytes 15000000 | tf_op jit(solution)/shard_map/attend/pallas_call | solution.py:193
  130.2 16.4 %leave.1 = (bf16[16,432,128]{2,1,0:T(8,128)(2,1)}, f32[1,1024]{1,0:T(1,128)S(1)}) custom-call(bf16[864,768]{1,0:T(8,128)(2,1)S(1)} %get-tuple-element.35.g0, bf16[864,768]{1,0:T(8,128)(2,1)S(1)} %get-tuple-element.36.g1, bf16[864,768]{1,0:T(8,128)(2,1)S(1)} %get-tuple-element.37.g2, bf16[864,768]{1,0:T(8,128)(2,1)S(1)} %get-tuple-element.38.g3, ...), custom_call_target="tpu_custom_call" | custom-call | flops 6000000000 | bytes 18000000 | tf_op jit(solution)/shard_map/leave/pallas_call | solution.py:319
  148.5 7.2 %all-to-all-start.2 = ((f32[128,1,8]{2,1,0:T(1,128)}), f32[128,1,8]{2,1,0:T(1,128)S(1)}, u32[]{:S(2)}, u32[]{:S(2)}) async-start(f32[128,1,8]{2,1,0:T(1,128)} %bitcast.108), calls=%async_computation.2 | async-start | bytes 131072 | tf_op jit(solution)/shard_map/all_to_all | solution.py:448
  164.0 4.7 %copy.87 = bf16[2,2,6,3,12,1024]{5,0,4,3,2,1:T(2,128)(2,1)} copy(bf16[2,2,6,3,12,1024]{5,4,2,0,3,1:T(8,128)(2,1)} %bitcast.365) | data formatting | bytes 3538944 | tf_op jit(solution)/shard_map/transpose | solution.py:451
  168.8 6.5 %all-to-all-start.1 = ((bf16[16,432,128]{2,1,0:T(8,128)(2,1)}), bf16[16,432,128]{2,1,0:T(8,128)(2,1)}, u32[]{:S(2)}, u32[]{:S(2)}) async-start(bf16[16,432,128]{2,1,0:T(8,128)(2,1)} %get-tuple-element.39), calls=%async_computation.1 | async-start | bytes 3538944 | tf_op jit(solution)/shard_map/all_to_all | solution.py:445
  179.4 6.2 %out_weight_sum.1 = (f32[512,1024]{1,0:T(8,128)S(1)}, f32[512,1024]{1,0:T(8,128)}) custom-call(bf16[864,256]{1,0:T(8,128)(2,1)S(1)} %copy-done.15, bf16[864,256]{1,0:T(8,128)(2,1)S(1)} %get-tuple-element.31.a1, bf16[864,256]{1,0:T(8,128)(2,1)S(1)} %get-tuple-element.32.a2, bf16[864,256]{1,0:T(8,128)(2,1)S(1)} %get-tuple-element.33.a3, ...), custom_call_target="tpu_custom_call" | custom-call | flops 4000000000 | bytes 10000000 | tf_op jit(solution)/shard_map/out_weight_sum/pallas_call | solution.py:241
  186.3 2.9 slice_add_fusion.3
  189.2 3.5 %collective-permute-start.33 = (f32[4,4,8,768]{3,2,1,0:T(8,128)S(1)}, f32[4,4,8,768]{3,2,1,0:T(8,128)S(1)}, u32[]{:S(2)}, u32[]{:S(2)}) collective-permute-start(f32[4,4,8,768]{3,2,1,0:T(8,128)S(1)} %bitcast.373), channel_id=1, source_target_pairs={{0,96},{1,97},{2,98},{3,99},{4,100},{5,101},{6,102},{7,103},{8,104... | collective-permute-start | bytes 1179656 | tf_op jit(solution)/shard_map/ppermute | solution.py:384
  196.7 3.2 collective-permute-start.23
  206.9 3.2 collective-permute-done.33
  210.8 2.8 collective-permute-done.31
  219.5 4.0 %join_pieces.1 = bf16[2,12,64,576]{3,2,1,0:T(8,128)(2,1)} custom-call(bf16[16,432,128]{2,1,0:T(8,128)(2,1)} %all-to-all-done.1.r_ref), custom_call_target="tpu_custom_call" | custom-call | flops 2000000000 | bytes 4000000 | tf_op jit(solution)/shard_map/join_pieces/pallas_call | solution.py:356
  225.9 3.1 collective-permute-start.12
  230.9 2.7 collective-permute-start.13
  236.4 2.7 collective-permute-start.36
  240.4 3.1 collective-permute-start.35
  246.2 3.8 %collective-permute-start.26 = (f32[4,8,768]{2,1,0:T(8,128)S(1)}, f32[4,8,768]{2,1,0:T(8,128)S(1)}, u32[]{:S(2)}, u32[]{:S(2)}) collective-permute-start(f32[4,8,768]{2,1,0:T(8,128)S(1)} %get-tuple-element.82), channel_id=1, source_target_pairs={{0,96},{1,97},{2,98},{3,99},{4,100},{5,101},{6,102},{7,103},{8,104... | collective-permute-start | bytes 294920 | tf_op jit(solution)/shard_map/ppermute | solution.py:384
  251.3 4.4 %collective-permute-start.6 = (f32[4,8,768]{2,1,0:T(8,128)S(1)}, f32[4,8,768]{2,1,0:T(8,128)S(1)}, u32[]{:S(2)}, u32[]{:S(2)}) collective-permute-start(f32[4,8,768]{2,1,0:T(8,128)S(1)} %get-tuple-element.74), channel_id=1, source_target_pairs={{0,12},{1,13},{2,14},{3,15},{4,0},{5,1},{6,2},{7,3},{8,4},{9,5},{1... | collective-permute-start | bytes 294920 | tf_op jit(solution)/shard_map/ppermute | solution.py:384
  256.7 2.9 collective-permute-start.4
  259.7 9.6 %collective-permute-start.15 = (f32[4,8,768]{2,1,0:T(8,128)S(1)}, f32[4,8,768]{2,1,0:T(8,128)S(1)}, u32[]{:S(2)}, u32[]{:S(2)}) collective-permute-start(f32[4,8,768]{2,1,0:T(8,128)S(1)} %get-tuple-element.79), channel_id=1, source_target_pairs={{0,2},{1,3},{2,0},{3,1},{4,6},{5,7},{6,4},{7,5},{8,10},{9,11},{10,... | collective-permute-start | bytes 294920 | tf_op jit(solution)/shard_map/ppermute | solution.py:384
  290.9 3.2 collective-permute-start.19
  295.3 6.0 %collective-permute-done.41 = f32[4,4,8,1024]{3,2,1,0:T(8,128)S(1)} collective-permute-done((f32[4,4,8,1024]{3,2,1,0:T(8,128)S(1)}, f32[4,4,8,1024]{3,2,1,0:T(8,128)S(1)}, u32[]{:S(2)}, u32[]{:S(2)}) %collective-permute-start.41) | collective-permute-done | bytes 524320 | tf_op jit(solution)/shard_map/ppermute | solution.py:384
  302.4 4.7 %collective-permute-done.43 = f32[4,4,8,1024]{3,2,1,0:T(8,128)S(1)} collective-permute-done((f32[4,4,8,1024]{3,2,1,0:T(8,128)S(1)}, f32[4,4,8,1024]{3,2,1,0:T(8,128)S(1)}, u32[]{:S(2)}, u32[]{:S(2)}) %collective-permute-start.43) | collective-permute-done | bytes 524320 | tf_op jit(solution)/shard_map/ppermute | solution.py:384
  310.5 2.9 collective-permute-start.45
  325.5 2.8 collective-permute-done.48
  (196 shorter events, 101.6 us)
Async XLA Ops:
  6.4 33.6 %all-to-all-start = ((bf16[16,432,128]{2,1,0:T(8,128)(2,1)}), bf16[16,432,128]{2,1,0:T(8,128)(2,1)}, u32[]{:S(2)}, u32[]{:S(2)}) async-start(bf16[16,432,128]{2,1,0:T(8,128)(2,1)} %split_pieces.1), calls=%async_computation | async-start | bytes 3538944 | tf_op jit(solution)/shard_map/all_to_all | solution.py:429
  110.1 76.2 %collective-permute-start.30 = (f32[512,768]{1,0:T(8,128)}, f32[512,768]{1,0:T(8,128)}, u32[]{:S(2)}, u32[]{:S(2)}) collective-permute-start(f32[512,768]{1,0:T(8,128)} %get-tuple-element.47), channel_id=1, source_target_pairs={{0,1},{1,0},{2,3},{3,2},{4,5},{5,4},{6,7},{7,6},{8,9},{9,8},{10,11... | collective-permute-start | bytes 4718600 | tf_op jit(solution)/shard_map/ppermute | solution.py:384
  110.1 82.9 %collective-permute-start.20 = (f32[512,768]{1,0:T(8,128)}, f32[512,768]{1,0:T(8,128)}, u32[]{:S(2)}, u32[]{:S(2)}) collective-permute-start(f32[512,768]{1,0:T(8,128)} %get-tuple-element.45), channel_id=1, source_target_pairs={{0,1},{1,0},{2,3},{3,2},{4,5},{5,4},{6,7},{7,6},{8,9},{9,8},{10,11... | collective-permute-start | bytes 4718600 | tf_op jit(solution)/shard_map/ppermute | solution.py:384
  129.7 67.0 %collective-permute-start = (f32[512,768]{1,0:T(8,128)}, f32[512,768]{1,0:T(8,128)}, u32[]{:S(2)}, u32[]{:S(2)}) collective-permute-start(f32[512,768]{1,0:T(8,128)} %get-tuple-element.41), channel_id=1, source_target_pairs={{0,1},{1,0},{2,3},{3,2},{4,5},{5,4},{6,7},{7,6},{8,9},{9,8},{10,11... | collective-permute-start | bytes 4718600 | tf_op jit(solution)/shard_map/ppermute | solution.py:384
  129.7 72.9 %collective-permute-start.10 = (f32[512,768]{1,0:T(8,128)}, f32[512,768]{1,0:T(8,128)}, u32[]{:S(2)}, u32[]{:S(2)}) collective-permute-start(f32[512,768]{1,0:T(8,128)} %get-tuple-element.43), channel_id=1, source_target_pairs={{0,1},{1,0},{2,3},{3,2},{4,5},{5,4},{6,7},{7,6},{8,9},{9,8},{10,11... | collective-permute-start | bytes 4718600 | tf_op jit(solution)/shard_map/ppermute | solution.py:384
  148.5 20.3 %all-to-all-start.2 = ((f32[128,1,8]{2,1,0:T(1,128)}), f32[128,1,8]{2,1,0:T(1,128)S(1)}, u32[]{:S(2)}, u32[]{:S(2)}) async-start(f32[128,1,8]{2,1,0:T(1,128)} %bitcast.108), calls=%async_computation.2 | async-start | bytes 131072 | tf_op jit(solution)/shard_map/all_to_all | solution.py:448
  168.8 50.7 %all-to-all-start.1 = ((bf16[16,432,128]{2,1,0:T(8,128)(2,1)}), bf16[16,432,128]{2,1,0:T(8,128)(2,1)}, u32[]{:S(2)}, u32[]{:S(2)}) async-start(bf16[16,432,128]{2,1,0:T(8,128)(2,1)} %get-tuple-element.39), calls=%async_computation.1 | async-start | bytes 3538944 | tf_op jit(solution)/shard_map/all_to_all | solution.py:445
  189.2 20.9 %collective-permute-start.33 = (f32[4,4,8,768]{3,2,1,0:T(8,128)S(1)}, f32[4,4,8,768]{3,2,1,0:T(8,128)S(1)}, u32[]{:S(2)}, u32[]{:S(2)}) collective-permute-start(f32[4,4,8,768]{3,2,1,0:T(8,128)S(1)} %bitcast.373), channel_id=1, source_target_pairs={{0,96},{1,97},{2,98},{3,99},{4,100},{5,101},{6,102},{7,103},{8,104... | collective-permute-start | bytes 1179656 | tf_op jit(solution)/shard_map/ppermute | solution.py:384
  192.6 17.5 %collective-permute-start.32 = (f32[4,4,8,768]{3,2,1,0:T(8,128)S(1)}, f32[4,4,8,768]{3,2,1,0:T(8,128)S(1)}, u32[]{:S(2)}, u32[]{:S(2)}) collective-permute-start(f32[4,4,8,768]{3,2,1,0:T(8,128)S(1)} %bitcast.372), channel_id=1, source_target_pairs={{0,64},{1,65},{2,66},{3,67},{4,68},{5,69},{6,70},{7,71},{8,72},{9,... | collective-permute-start | bytes 1179656 | tf_op jit(solution)/shard_map/ppermute | solution.py:384
  193.0 20.6 %collective-permute-start.31 = (f32[4,4,8,768]{3,2,1,0:T(8,128)S(1)}, f32[4,4,8,768]{3,2,1,0:T(8,128)S(1)}, u32[]{:S(2)}, u32[]{:S(2)}) collective-permute-start(f32[4,4,8,768]{3,2,1,0:T(8,128)S(1)} %bitcast.371), channel_id=1, source_target_pairs={{0,32},{1,33},{2,34},{3,35},{4,36},{5,37},{6,38},{7,39},{8,40},{9,... | collective-permute-start | bytes 1179656 | tf_op jit(solution)/shard_map/ppermute | solution.py:384
  196.7 19.5 %collective-permute-start.23 = (f32[4,4,8,768]{3,2,1,0:T(8,128)S(1)}, f32[4,4,8,768]{3,2,1,0:T(8,128)S(1)}, u32[]{:S(2)}, u32[]{:S(2)}) collective-permute-start(f32[4,4,8,768]{3,2,1,0:T(8,128)S(1)} %get-tuple-element.62), channel_id=1, source_target_pairs={{0,18},{1,19},{2,16},{3,17},{4,22},{5,23},{6,20},{7,21},{8,26},{9,... | collective-permute-start | bytes 1179656 | tf_op jit(solution)/shard_map/ppermute | solution.py:384
  202.5 20.9 %collective-permute-start.22 = (f32[4,4,8,768]{3,2,1,0:T(8,128)}, f32[4,4,8,768]{3,2,1,0:T(8,128)}, u32[]{:S(2)}, u32[]{:S(2)}) collective-permute-start(f32[4,4,8,768]{3,2,1,0:T(8,128)} %get-tuple-element.63), channel_id=1, source_target_pairs={{0,2},{1,3},{2,0},{3,1},{4,6},{5,7},{6,4},{7,5},{8,10},{9,11},{10,... | collective-permute-start | bytes 1179656 | tf_op jit(solution)/shard_map/ppermute | solution.py:384
  210.1 71.7 %collective-permute-start.40 = (f32[512,1024]{1,0:T(8,128)}, f32[512,1024]{1,0:T(8,128)}, u32[]{:S(2)}, u32[]{:S(2)}) collective-permute-start(f32[512,1024]{1,0:T(8,128)} %get-tuple-element.49), channel_id=1, source_target_pairs={{0,1},{1,0},{2,3},{3,2},{4,5},{5,4},{6,7},{7,6},{8,9},{9,8},{10,11... | collective-permute-start | bytes 6291464 | tf_op jit(solution)/shard_map/ppermute | solution.py:384
  210.1 14.1 %collective-permute-start.21 = (f32[4,4,8,768]{3,2,1,0:T(8,128)}, f32[4,4,8,768]{3,2,1,0:T(8,128)}, u32[]{:S(2)}, u32[]{:S(2)}) collective-permute-start(f32[4,4,8,768]{3,2,1,0:T(8,128)} %get-tuple-element.64), channel_id=1, source_target_pairs={{0,16},{1,17},{2,18},{3,19},{4,20},{5,21},{6,22},{7,23},{8,24},{9,... | collective-permute-start | bytes 1179656 | tf_op jit(solution)/shard_map/ppermute | solution.py:384
  213.6 12.4 %collective-permute-start.3 = (f32[4,4,8,768]{3,2,1,0:T(8,128)}, f32[4,4,8,768]{3,2,1,0:T(8,128)}, u32[]{:S(2)}, u32[]{:S(2)}) collective-permute-start(f32[4,4,8,768]{3,2,1,0:T(8,128)} %bitcast.11), channel_id=1, source_target_pairs={{0,96},{1,97},{2,98},{3,99},{4,100},{5,101},{6,102},{7,103},{8,104... | collective-permute-start | bytes 1179656 | tf_op jit(solution)/shard_map/ppermute | solution.py:384
  217.0 14.0 %collective-permute-start.2 = (f32[4,4,8,768]{3,2,1,0:T(8,128)}, f32[4,4,8,768]{3,2,1,0:T(8,128)}, u32[]{:S(2)}, u32[]{:S(2)}) collective-permute-start(f32[4,4,8,768]{3,2,1,0:T(8,128)} %bitcast.10), channel_id=1, source_target_pairs={{0,64},{1,65},{2,66},{3,67},{4,68},{5,69},{6,70},{7,71},{8,72},{9,... | collective-permute-start | bytes 1179656 | tf_op jit(solution)/shard_map/ppermute | solution.py:384
  223.5 12.9 %collective-permute-start.1 = (f32[4,4,8,768]{3,2,1,0:T(8,128)S(1)}, f32[4,4,8,768]{3,2,1,0:T(8,128)S(1)}, u32[]{:S(2)}, u32[]{:S(2)}) collective-permute-start(f32[4,4,8,768]{3,2,1,0:T(8,128)S(1)} %bitcast.370), channel_id=1, source_target_pairs={{0,32},{1,33},{2,34},{3,35},{4,36},{5,37},{6,38},{7,39},{8,40},{9,... | collective-permute-start | bytes 1179656 | tf_op jit(solution)/shard_map/ppermute | solution.py:384
  224.4 15.9 %collective-permute-start.11 = (f32[4,4,8,768]{3,2,1,0:T(8,128)S(1)}, f32[4,4,8,768]{3,2,1,0:T(8,128)S(1)}, u32[]{:S(2)}, u32[]{:S(2)}) collective-permute-start(f32[4,4,8,768]{3,2,1,0:T(8,128)S(1)} %copy-done.24), channel_id=1, source_target_pairs={{0,4},{1,5},{2,6},{3,7},{4,8},{5,9},{6,10},{7,11},{8,12},{9,13},{1... | collective-permute-start | bytes 1179656 | tf_op jit(solution)/shard_map/ppermute | solution.py:384
  225.9 18.6 %collective-permute-start.12 = (f32[4,4,8,768]{3,2,1,0:T(8,128)S(1)}, f32[4,4,8,768]{3,2,1,0:T(8,128)S(1)}, u32[]{:S(2)}, u32[]{:S(2)}) collective-permute-start(f32[4,4,8,768]{3,2,1,0:T(8,128)S(1)} %copy-done.23), channel_id=1, source_target_pairs={{0,8},{1,9},{2,10},{3,11},{4,12},{5,13},{6,14},{7,15},{8,0},{9,1},... | collective-permute-start | bytes 1179656 | tf_op jit(solution)/shard_map/ppermute | solution.py:384
  230.9 15.2 %collective-permute-start.13 = (f32[4,4,8,768]{3,2,1,0:T(8,128)S(1)}, f32[4,4,8,768]{3,2,1,0:T(8,128)S(1)}, u32[]{:S(2)}, u32[]{:S(2)}) collective-permute-start(f32[4,4,8,768]{3,2,1,0:T(8,128)S(1)} %copy-done.26), channel_id=1, source_target_pairs={{0,12},{1,13},{2,14},{3,15},{4,0},{5,1},{6,2},{7,3},{8,4},{9,5},{1... | collective-permute-start | bytes 1179656 | tf_op jit(solution)/shard_map/ppermute | solution.py:384
  236.4 13.7 %collective-permute-start.36 = (f32[4,8,768]{2,1,0:T(8,128)S(1)}, f32[4,8,768]{2,1,0:T(8,128)S(1)}, u32[]{:S(2)}, u32[]{:S(2)}) collective-permute-start(f32[4,8,768]{2,1,0:T(8,128)S(1)} %get-tuple-element.86), channel_id=1, source_target_pairs={{0,18},{1,19},{2,16},{3,17},{4,22},{5,23},{6,20},{7,21},{8,26},{9,... | collective-permute-start | bytes 294920 | tf_op jit(solution)/shard_map/ppermute | solution.py:384
  240.4 9.8 %collective-permute-start.35 = (f32[4,8,768]{2,1,0:T(8,128)S(1)}, f32[4,8,768]{2,1,0:T(8,128)S(1)}, u32[]{:S(2)}, u32[]{:S(2)}) collective-permute-start(f32[4,8,768]{2,1,0:T(8,128)S(1)} %get-tuple-element.87), channel_id=1, source_target_pairs={{0,2},{1,3},{2,0},{3,1},{4,6},{5,7},{6,4},{7,5},{8,10},{9,11},{10,... | collective-permute-start | bytes 294920 | tf_op jit(solution)/shard_map/ppermute | solution.py:384
  255.7 13.5 %collective-permute-start.5 = (f32[4,8,768]{2,1,0:T(8,128)S(1)}, f32[4,8,768]{2,1,0:T(8,128)S(1)}, u32[]{:S(2)}, u32[]{:S(2)}) collective-permute-start(f32[4,8,768]{2,1,0:T(8,128)S(1)} %get-tuple-element.75), channel_id=1, source_target_pairs={{0,8},{1,9},{2,10},{3,11},{4,12},{5,13},{6,14},{7,15},{8,0},{9,1},... | collective-permute-start | bytes 294920 | tf_op jit(solution)/shard_map/ppermute | solution.py:384
  256.7 12.6 %collective-permute-start.4 = (f32[4,8,768]{2,1,0:T(8,128)S(1)}, f32[4,8,768]{2,1,0:T(8,128)S(1)}, u32[]{:S(2)}, u32[]{:S(2)}) collective-permute-start(f32[4,8,768]{2,1,0:T(8,128)S(1)} %get-tuple-element.76), channel_id=1, source_target_pairs={{0,4},{1,5},{2,6},{3,7},{4,8},{5,9},{6,10},{7,11},{8,12},{9,13},{1... | collective-permute-start | bytes 294920 | tf_op jit(solution)/shard_map/ppermute | solution.py:384
  259.6 10.8 %collective-permute-start.16 = (f32[4,8,768]{2,1,0:T(8,128)S(1)}, f32[4,8,768]{2,1,0:T(8,128)S(1)}, u32[]{:S(2)}, u32[]{:S(2)}) collective-permute-start(f32[4,8,768]{2,1,0:T(8,128)S(1)} %get-tuple-element.78), channel_id=1, source_target_pairs={{0,18},{1,19},{2,16},{3,17},{4,22},{5,23},{6,20},{7,21},{8,26},{9,... | collective-permute-start | bytes 294920 | tf_op jit(solution)/shard_map/ppermute | solution.py:384
  259.7 13.3 %collective-permute-start.15 = (f32[4,8,768]{2,1,0:T(8,128)S(1)}, f32[4,8,768]{2,1,0:T(8,128)S(1)}, u32[]{:S(2)}, u32[]{:S(2)}) collective-permute-start(f32[4,8,768]{2,1,0:T(8,128)S(1)} %get-tuple-element.79), channel_id=1, source_target_pairs={{0,2},{1,3},{2,0},{3,1},{4,6},{5,7},{6,4},{7,5},{8,10},{9,11},{10,... | collective-permute-start | bytes 294920 | tf_op jit(solution)/shard_map/ppermute | solution.py:384
  285.6 15.7 %collective-permute-start.41 = (f32[4,4,8,1024]{3,2,1,0:T(8,128)S(1)}, f32[4,4,8,1024]{3,2,1,0:T(8,128)S(1)}, u32[]{:S(2)}, u32[]{:S(2)}) collective-permute-start(f32[4,4,8,1024]{3,2,1,0:T(8,128)S(1)} %get-tuple-element.51), channel_id=1, source_target_pairs={{0,4},{1,5},{2,6},{3,7},{4,8},{5,9},{6,10},{7,11},{8,12},{9,13},{1... | collective-permute-start | bytes 1572872 | tf_op jit(solution)/shard_map/ppermute | solution.py:384
  286.7 20.3 %collective-permute-start.43 = (f32[4,4,8,1024]{3,2,1,0:T(8,128)S(1)}, f32[4,4,8,1024]{3,2,1,0:T(8,128)S(1)}, u32[]{:S(2)}, u32[]{:S(2)}) collective-permute-start(f32[4,4,8,1024]{3,2,1,0:T(8,128)S(1)} %get-tuple-element.52), channel_id=1, source_target_pairs={{0,12},{1,13},{2,14},{3,15},{4,0},{5,1},{6,2},{7,3},{8,4},{9,5},{1... | collective-permute-start | bytes 1572872 | tf_op jit(solution)/shard_map/ppermute | solution.py:384
  288.9 19.4 %collective-permute-start.42 = (f32[4,4,8,1024]{3,2,1,0:T(8,128)S(1)}, f32[4,4,8,1024]{3,2,1,0:T(8,128)S(1)}, u32[]{:S(2)}, u32[]{:S(2)}) collective-permute-start(f32[4,4,8,1024]{3,2,1,0:T(8,128)S(1)} %get-tuple-element.53), channel_id=1, source_target_pairs={{0,8},{1,9},{2,10},{3,11},{4,12},{5,13},{6,14},{7,15},{8,0},{9,1},... | collective-permute-start | bytes 1572872 | tf_op jit(solution)/shard_map/ppermute | solution.py:384
  290.9 22.5 %collective-permute-start.17 = (f32[8,768]{1,0:T(8,128)S(1)}, f32[8,768]{1,0:T(8,128)S(1)}, u32[]{:S(2)}, u32[]{:S(2)}) collective-permute-start(f32[8,768]{1,0:T(8,128)S(1)} %get-tuple-element.95), channel_id=1, source_target_pairs={{0,32},{1,33},{2,34},{3,35},{4,36},{5,37},{6,38},{7,39},{8,40},{9,... | collective-permute-start | bytes 73736 | tf_op jit(solution)/shard_map/ppermute | solution.py:384
  290.9 22.5 %collective-permute-start.19 = (f32[8,768]{1,0:T(8,128)S(1)}, f32[8,768]{1,0:T(8,128)S(1)}, u32[]{:S(2)}, u32[]{:S(2)}) collective-permute-start(f32[8,768]{1,0:T(8,128)S(1)} %get-tuple-element.96), channel_id=1, source_target_pairs={{0,96},{1,97},{2,98},{3,99},{4,100},{5,101},{6,102},{7,103},{8,104... | collective-permute-start | bytes 73736 | tf_op jit(solution)/shard_map/ppermute | solution.py:384
  301.3 12.1 %collective-permute-start.18 = (f32[8,768]{1,0:T(8,128)S(1)}, f32[8,768]{1,0:T(8,128)S(1)}, u32[]{:S(2)}, u32[]{:S(2)}) collective-permute-start(f32[8,768]{1,0:T(8,128)S(1)} %get-tuple-element.97), channel_id=1, source_target_pairs={{0,64},{1,65},{2,66},{3,67},{4,68},{5,69},{6,70},{7,71},{8,72},{9,... | collective-permute-start | bytes 73736 | tf_op jit(solution)/shard_map/ppermute | solution.py:384
  (58 other events, 467.9 us)

commit v2 on v1

v2 whole, which is shorter than its diff:
```python
import functools

import jax
import jax.numpy as jnp
from jax import lax
from jax.experimental import pallas as pl
from jax.experimental.pallas import tpu as pltpu
from jax.sharding import PartitionSpec as P

F32 = jnp.float32
BF16 = jnp.bfloat16
D = 1024
HEAD = 64
WIN = 144
HALF = 72
WINS = 6
TOK = WIN * WINS
SHIFT = 6
LON = 576
GROUPS = 4
ROWS = 6 * HALF + 16
GW = D // GROUPS
QUADS = GW // HEAD
SCALE = HEAD**-0.5
LOG2E = 1.4426950408889634
MIB = 1 << 20
AXES = ("lat", "lon")


def nn(a, b):
    return lax.dot_general(a, b, (((1,), (0,)), ((), ())), preferred_element_type=F32)


def nt(a, b):
    return lax.dot_general(a, b, (((1,), (1,)), ((), ())), preferred_element_type=F32)


def params(mib):
    return pltpu.CompilerParams(vmem_limit_bytes=mib * MIB)


def cost(flops, nbytes):
    return pl.CostEstimate(flops=int(flops / 10), bytes_accessed=int(nbytes / 10), transcendentals=0)


def waits(after):
    return [pl.BlockSpec(memory_space=pl.ANY)] * len(after)


def behind(kernel, count, operands, passed=0, results=1):
    def body(*refs):
        rest = refs[operands + count :]
        kernel(*refs[:operands], *rest[:results], *rest[results + passed :])

    return body


def vmem(n):
    return [pl.BlockSpec(memory_space=pltpu.VMEM)] * n


def split_kernel(z_ref, out_ref, t_ref, s_ref):
    row = lax.broadcasted_iota(jnp.int32, (LON, LON), 0)
    col = lax.broadcasted_iota(jnp.int32, (LON, LON), 1)
    source = row + SHIFT
    source = jnp.where(source >= LON, source - LON, source)
    pick = (col == source).astype(BF16)
    for r in range(12):
        both = jnp.concatenate([z_ref[0, r], z_ref[1, r]], axis=0)
        t_ref[...] = nt(pick, both)
        for v in range(48):
            at = ((r // 6) * 3 + v % 3) * HALF + (r % 6) * 12
            s_ref[v // 3, at : at + 12, :] = t_ref[12 * v : 12 * v + 12, :]
    for k in range(16):
        out_ref[k] = s_ref[k].astype(BF16)


def split_pieces(z):
    return pl.pallas_call(
        split_kernel,
        out_shape=jax.ShapeDtypeStruct((16, 6 * HALF, 128), BF16),
        in_specs=vmem(1),
        out_specs=vmem(1)[0],
        scratch_shapes=[pltpu.VMEM((LON, 128), F32), pltpu.VMEM((16, 6 * HALF, 128), F32)],
        compiler_params=params(32),
        cost_estimate=cost(2e9, 4e6),
        name="split_pieces",
    )(z)


def norm_parts(x):
    centred = x - jnp.sum(x, axis=-1, keepdims=True) * (1.0 / D)
    variance = jnp.sum(centred * centred, axis=-1, keepdims=True) * (1.0 / D)
    inv_scale = lax.rsqrt(variance + 1e-05)
    return centred * inv_scale, inv_scale


def enter_kernel(r_ref, gain_ref, pick_ref, x_ref, scaled_ref, scaled_t_ref, xs_ref):
    low = lax.broadcasted_iota(jnp.int32, (6 * HALF, 128), 1) < HEAD
    for p in range(8):
        first = r_ref[2 * p].astype(F32)
        second = r_ref[2 * p + 1].astype(F32)
        level0 = jnp.where(low, first, pltpu.roll(second, HEAD, 1))
        level1 = jnp.where(low, pltpu.roll(first, HEAD, 1), second)
        for w in range(WINS):
            at = w * WIN
            xs_ref[at : at + HALF, 128 * p : 128 * p + 128] = level0[HALF * w : HALF * w + HALF]
            xs_ref[at + HALF : at + WIN, 128 * p : 128 * p + 128] = level1[HALF * w : HALF * w + HALF]

    def rows(i, _):
        at = pl.ds(pl.multiple_of(i * 48, 48), 48)
        x = xs_ref[at, :]
        x_ref[at, :] = x.astype(BF16)
        normed, _ = norm_parts(x)
        scaled_ref[at, :] = (normed * gain_ref[...]).astype(BF16)
        return 0

    lax.fori_loop(0, TOK // 48, rows, 0)

    def turn(i, _):
        at = pl.ds(pl.multiple_of(i * 256, 256), 256)
        scaled_t_ref[at, :] = nt(pick_ref[at, :], scaled_ref[...]).astype(BF16)
        return 0

    lax.fori_loop(0, 4, turn, 0)


def enter(pieces, gain, pick):
    return pl.pallas_call(
        enter_kernel,
        out_shape=(
            jax.ShapeDtypeStruct((TOK, D), BF16),
            jax.ShapeDtypeStruct((TOK, D), BF16),
            jax.ShapeDtypeStruct((D, TOK), BF16),
        ),
        in_specs=vmem(3),
        out_specs=tuple(vmem(3)),
        scratch_shapes=[pltpu.VMEM((TOK, D), F32)],
        compiler_params=params(32),
        cost_estimate=cost(3e9, 9e6),
        name="enter",
    )(pieces, gain, pick)


def attend_kernel(
    scaled_ref, scaled_t_ref, up_ref, wq_ref, wk_ref, wv_ref, wo_ref, mask_ref,
    pick_ref, z_ref, att_ref, grad_ref, keep_ref, send_ref, q_ref, k_ref, v_ref, o_ref, other_ref,
):
    for w_ref, p_ref in ((wq_ref, q_ref), (wk_ref, k_ref), (wv_ref, v_ref)):
        p_ref[...] = nn(scaled_ref[...], w_ref[...]).astype(BF16)
    o_ref[...] = nt(up_ref[...], wo_ref[...]).astype(BF16)

    wide = (WIN, QUADS * WIN)
    key = lax.broadcasted_iota(jnp.int32, wide, 0)
    query = lax.broadcasted_iota(jnp.int32, wide, 1)
    same = query == key
    for h in range(1, QUADS):
        same = same | (query == key + h * WIN)
    other_ref[...] = jnp.where(same, 0.0, 1.0)
    lane = lax.broadcasted_iota(jnp.int32, (WIN, GW), 1)
    mine = [(lane >= HEAD * h) & (lane < HEAD * h + HEAD) for h in range(QUADS)]
    zero = jnp.zeros((WIN, GW), BF16)

    def by_head(a):
        return jnp.concatenate([jnp.where(m, a, zero) for m in mine], axis=0)

    def own_head(a):
        total = a[:WIN]
        for h in range(1, QUADS):
            total = jnp.where(mine[h], a[h * WIN : h * WIN + WIN], total)
        return total

    def window(i, _):
        at = pl.ds(pl.multiple_of(i * WIN, WIN), WIN)
        k, v = k_ref[at, :], v_ref[at, :]
        q, o = by_head(q_ref[at, :]), by_head(o_ref[at, :])
        scores = nt(k, q) * (SCALE * LOG2E) + other_ref[...] * mask_ref[at, :]
        raised = jnp.exp2(scores - jnp.max(scores, axis=0, keepdims=True))
        prob = raised * (1.0 / jnp.sum(raised, axis=0, keepdims=True))
        prob_half = prob.astype(BF16)
        prob_grad = nt(v, o)
        inner = jnp.sum(prob * prob_grad, axis=0, keepdims=True)
        score_grad = (prob * (prob_grad - inner)).astype(BF16)
        att_ref[at, :] = own_head(nn(prob_half.T, v)).astype(BF16)
        grad_ref[at, 0:GW] = (own_head(nn(score_grad.T, k)) * SCALE).astype(BF16)
        grad_ref[at, GW : 2 * GW] = (nn(score_grad, q) * SCALE).astype(BF16)
        grad_ref[at, 2 * GW : 3 * GW] = nn(prob_half, o).astype(BF16)
        return 0

    lax.fori_loop(0, WINS, window, 0)

    def weights(i, _):
        at = pl.ds(pl.multiple_of(i * 256, 256), 256)
        keep_ref[at, 0 : 3 * GW] = nn(scaled_t_ref[at, :], grad_ref[...])
        far = pl.ds(pl.multiple_of(i * 256 + 512, 256), 256)
        send_ref[at, 0 : 3 * GW] = nn(scaled_t_ref[far, :], grad_ref[...])
        return 0

    lax.fori_loop(0, 2, weights, 0)

    turned = nt(pick_ref[...], att_ref[...]).astype(BF16)
    for e in range(4):
        cols = pl.ds(pl.multiple_of((z_ref[0] ^ e) * GW, GW), GW)
        part = nn(turned, up_ref[:, cols])
        for y in range(4):
            at = 128 * y + 32 * e
            keep_ref[at : at + 32, 3 * GW :] = part[32 * y : 32 * y + 32]
            send_ref[at : at + 32, 3 * GW :] = part[128 + 32 * y : 160 + 32 * y]


def attend(g, scaled, scaled_t, up, qkv_weight, out_weight, mask, pick, z, after=()):
    full = lambda shape: pl.BlockSpec(shape, lambda i: (0, 0))
    return pl.pallas_call(
        behind(attend_kernel, len(after), 10),
        grid=(1,),
        out_shape=(
            jax.ShapeDtypeStruct((TOK, GW), BF16),
            jax.ShapeDtypeStruct((TOK, 3 * GW), BF16),
            jax.ShapeDtypeStruct((D // 2, 4 * GW), F32),
            jax.ShapeDtypeStruct((D // 2, 4 * GW), F32),
        ),
        in_specs=[
            full((TOK, D)),
            full((D, TOK)),
            full((TOK, D)),
            pl.BlockSpec((D, GW), lambda i: (0, g)),
            pl.BlockSpec((D, GW), lambda i: (0, GROUPS + g)),
            pl.BlockSpec((D, GW), lambda i: (0, 2 * GROUPS + g)),
            pl.BlockSpec((GW, D), lambda i: (g, 0)),
            full((TOK, 1)),
            full((GW, GW)),
            pl.BlockSpec(memory_space=pltpu.SMEM),
        ]
        + waits(after),
        out_specs=(
            full((TOK, GW)),
            full((TOK, 3 * GW)),
            full((D // 2, 4 * GW)),
            full((D // 2, 4 * GW)),
        ),
        scratch_shapes=[pltpu.VMEM((TOK, GW), BF16)] * 4 + [pltpu.VMEM((WIN, QUADS * WIN), F32)],
        compiler_params=params(48),
        cost_estimate=cost(8e9, 15e6),
        name="attend",
    )(scaled, scaled_t, up, qkv_weight, qkv_weight, qkv_weight, out_weight, mask, pick, z, *after)


def block_kernel(a0, a1, a2, a3, x_ref, w_ref, out_ref):
    def rows(i, _):
        at = pl.ds(pl.multiple_of(i * 432, 432), 432)
        total = x_ref[at, :].astype(F32)
        for g, a in enumerate((a0, a1, a2, a3)):
            total = total + nn(a[at, :], w_ref[GW * g : GW * g + GW, :])
        out_ref[at, :] = total.astype(BF16)
        return 0

    lax.fori_loop(0, 2, rows, 0)


def block_sum(att, x, out_weight, passed, after):
    after = tuple(passed) + tuple(after)
    return pl.pallas_call(
        behind(block_kernel, len(after), 6, len(passed)),
        out_shape=(jax.ShapeDtypeStruct((TOK, D), BF16),)
        + tuple(jax.ShapeDtypeStruct(p.shape, p.dtype) for p in passed),
        in_specs=vmem(6) + waits(after),
        out_specs=tuple(vmem(1) + waits(passed)),
        input_output_aliases={6 + i: 1 + i for i in range(len(passed))},
        compiler_params=params(32),
        cost_estimate=cost(2e9, 8e6),
        name="block_sum",
    )(*att, x, out_weight, *after)


def product_kernel(g0, g1, g2, g3, w_ref, n_ref):
    def product(i, _):
        at = pl.ds(pl.multiple_of(i * 432, 432), 432)
        total = None
        for g, d in enumerate((g0, g1, g2, g3)):
            for part in range(3):
                base = part * D + g * GW
                piece = nt(d[at, part * GW : part * GW + GW], w_ref[:, base : base + GW])
                total = piece if total is None else total + piece
        n_ref[at, :] = total
        return 0

    lax.fori_loop(0, 2, product, 0)


def product(grads, qkv_weight, after=()):
    return pl.pallas_call(
        behind(product_kernel, len(after), 5),
        out_shape=jax.ShapeDtypeStruct((TOK, D), F32),
        in_specs=vmem(5) + waits(after),
        out_specs=vmem(1)[0],
        compiler_params=params(40),
        cost_estimate=cost(6e9, 15e6),
        name="product",
    )(*grads, qkv_weight, *after)


def leave_kernel(s_ref, x_ref, up_ref, gain_ref, mix_ref, out_ref, n_ref):
    def rows(i, gain_sum):
        at = pl.ds(pl.multiple_of(i * 48, 48), 48)
        normed, inv_scale = norm_parts(x_ref[at, :].astype(F32))
        n = s_ref[at, :]
        both = n * normed
        gain = gain_ref[...]
        g = n * gain
        mean_g = jnp.sum(g, axis=-1, keepdims=True) * (1.0 / D)
        mean_gn = jnp.sum(both * gain, axis=-1, keepdims=True) * (1.0 / D)
        n_ref[at, :] = up_ref[at, :].astype(F32) + inv_scale * (g - mean_g - normed * mean_gn)
        return gain_sum + jnp.sum(both.reshape(6, 8, D), axis=0)

    gain_sum = lax.fori_loop(0, TOK // 48, rows, jnp.zeros((8, D), F32))
    whole = jnp.sum(gain_sum, axis=0, keepdims=True)
    high = whole.astype(BF16).astype(F32)
    mid = (whole - high).astype(BF16).astype(F32)
    row16 = lax.broadcasted_iota(jnp.int32, (16, D), 0)
    split = jnp.where(row16 == 0, high, jnp.where(row16 == 1, mid, whole - high - mid))
    split = jnp.where(row16 < 3, split, 0.0).astype(BF16)
    split = nn(split, mix_ref[...]).astype(BF16)

    low = lax.broadcasted_iota(jnp.int32, (6 * HALF, 128), 1) < HEAD
    for p in range(8):
        cols = slice(128 * p, 128 * p + 128)
        level0 = jnp.concatenate([n_ref[WIN * w : WIN * w + HALF, cols] for w in range(WINS)], axis=0)
        level1 = jnp.concatenate([n_ref[WIN * w + HALF : WIN * w + WIN, cols] for w in range(WINS)], axis=0)
        out_ref[2 * p, 0 : 6 * HALF] = jnp.where(low, level0, pltpu.roll(level1, HEAD, 1)).astype(BF16)
        out_ref[2 * p + 1, 0 : 6 * HALF] = jnp.where(low, pltpu.roll(level0, HEAD, 1), level1).astype(BF16)
        out_ref[2 * p, 6 * HALF :] = split[:, cols]
        out_ref[2 * p + 1, 6 * HALF :] = split[:, cols]


def leave(norm_grad, x, up, gain, mix, after=()):
    return pl.pallas_call(
        behind(leave_kernel, len(after), 5),
        out_shape=jax.ShapeDtypeStruct((16, ROWS, 128), BF16),
        in_specs=vmem(5) + waits(after),
        out_specs=vmem(1)[0],
        scratch_shapes=[pltpu.VMEM((TOK, D), F32)],
        compiler_params=params(32),
        cost_estimate=cost(4e9, 10e6),
        name="leave",
    )(norm_grad, x, up, gain, mix, *after)


def join_kernel(r_ref, out_ref, gain_ref, s_ref, t_ref):
    gain = None
    for k in range(16):
        s_ref[k] = r_ref[k, 0 : 6 * HALF].astype(F32)
        term = r_ref[k, 6 * HALF :].astype(F32)
        gain = term if gain is None else gain + term
    gain_ref[...] = jnp.sum(gain, axis=0, keepdims=True)
    same = lax.broadcasted_iota(jnp.int32, (128, 128), 0) == lax.broadcasted_iota(
        jnp.int32, (128, 128), 1
    )
    same = same.astype(BF16)
    for r in range(12):
        for v in range(48):
            at = ((r // 6) * 3 + v % 3) * HALF + (r % 6) * 12
            to = 12 * v + SHIFT
            if to + 12 <= LON:
                t_ref[to : to + 12, :] = s_ref[v // 3, at : at + 12, :]
            else:
                t_ref[to:LON, :] = s_ref[v // 3, at : at + LON - to, :]
                t_ref[0 : to + 12 - LON, :] = s_ref[v // 3, at + LON - to : at + 12, :]
        turned = nt(same, t_ref[...].astype(BF16)).astype(BF16)
        out_ref[0, r] = turned[:HEAD]
        out_ref[1, r] = turned[HEAD:]


def join_pieces(pieces, passed, after):
    after = tuple(passed) + tuple(after)
    return pl.pallas_call(
        behind(join_kernel, len(after), 1, len(passed), 2),
        out_shape=(
            jax.ShapeDtypeStruct((2, 12, HEAD, LON), BF16),
            jax.ShapeDtypeStruct((1, 128), F32),
        )
        + tuple(jax.ShapeDtypeStruct(p.shape, p.dtype) for p in passed),
        in_specs=vmem(1) + waits(after),
        out_specs=tuple(vmem(2) + waits(passed)),
        input_output_aliases={1 + i: 2 + i for i in range(len(passed))},
        scratch_shapes=[pltpu.VMEM((16, 6 * HALF, 128), F32), pltpu.VMEM((LON, 128), F32)],
        compiler_params=params(32),
        cost_estimate=cost(2e9, 4e6),
        name="join_pieces",
    )(pieces, *after)


def device_index(x, y, z, core):
    return ((z * 2 + x % 2) * 4 + y) * 4 + (x // 2) * 2 + core


def swapped(z=0, x=0, y=0, core=0):
    pairs = []
    for px in range(4):
        for py in range(4):
            for pz in range(4):
                for c in range(2):
                    to = device_index(px ^ x, py ^ y, pz ^ z, c ^ core)
                    pairs.append((device_index(px, py, pz, c), to))
    return sorted(pairs)


class Sum:
    def __init__(self, keep, got):
        self.tail = (8, keep.shape[-1])
        self.spots = {n: (0, 1, 2, 3) for n in "yzx"}
        self.whole = {n: {e: e for e in range(4)} for n in "yzx"}
        self.terms = [(keep.reshape((4, 4, 4) + self.tail), self.whole, 0)]
        self.terms.append((got.reshape((4, 4, 4) + self.tail), self.whole, 0))

    def columns(self, low, high):
        part = Sum.__new__(Sum)
        part.tail, part.whole, part.spots = (8, high - low), self.whole, dict(self.spots)
        part.terms = [(a, places, low) for a, places, _ in self.terms]
        return part

    def cut(self, name, chosen):
        total = None
        spots = dict(self.spots)
        spots[name] = chosen
        for array, places, low in self.terms:
            index = tuple(
                slice(places[n][spots[n][0]], places[n][spots[n][-1]] + 1) for n in "yzx"
            )
            piece = array[index + (slice(None), slice(low, low + self.tail[1]))]
            total = piece if total is None else total + piece
        return total

    def offer(self, name, by):
        if len(self.spots[name]) == 4:
            give, rest = ((1, 2), (0, 3)) if by == 1 else ((2, 3), (0, 1))
        else:
            give, rest = (by,), (0,)
        piece = self.cut(name, give)
        self.spots[name] = rest
        places = {n: {e: i for i, e in enumerate(self.spots[n])} for n in "yzx"}
        places[name] = {e ^ by: i for i, e in enumerate(give)}
        return piece, places

    def ring_y(self, y):
        (keep, _, _), (got, _, _) = self.terms
        total = ordered_sum(keep, got, y)
        rest = total.reshape(4 * 128, self.tail[1])
        rest = lax.psum_scatter(rest, "lon", scatter_dimension=0, axis_index_groups=Y_RINGS, tiled=True)
        self.reduced = rest
        self.spots["y"] = (0,)
        places = dict(self.whole)
        places["y"] = {0: 0}
        self.terms = [(rest.reshape((1, 4, 4) + self.tail), places, 0)]
        return total

    def cells(self):
        found = []
        for array, places, low in self.terms:
            at = places["y"][0] * array.shape[1] + places["z"][0]
            found.append((array.reshape(-1, 32, array.shape[-1]), at, low // self.tail[1]))
        return found


Y_RINGS = [[c, c + 4, c + 8, c + 12] for c in range(4)]


def exchange(sums, name, by):
    offers = [s.offer(name, by) for s in sums]
    flat = [piece.reshape((-1,) + piece.shape[3:]) for piece, _ in offers]
    out = flat[0] if len(flat) == 1 else jnp.concatenate(flat, axis=-1)
    got = lax.ppermute(out, AXES, swapped(**{name: by}))
    at = 0
    for s, (piece, places) in zip(sums, offers):
        wide = piece.shape[-1]
        s.terms.append((got.reshape(piece.shape[:3] + (8, -1)), places, at))
        at += wide
    return out, got


def add_kernel(y_ref, a_ref, b_ref, out_ref):
    out_ref[...] = a_ref[...] + b_ref[...]


def ordered_sum(a, b, y):
    a, b = (t.reshape(4, 128, t.shape[-1]) for t in (a, b))
    block = (1,) + a.shape[1:]
    return pl.pallas_call(
        add_kernel,
        grid_spec=pltpu.PrefetchScalarGridSpec(
            num_scalar_prefetch=1,
            grid=(4,),
            in_specs=[pl.BlockSpec(block, lambda i, y: (i ^ y[0], 0, 0))] * 2,
            out_specs=pl.BlockSpec(block, lambda i, y: (i, 0, 0)),
        ),
        out_shape=jax.ShapeDtypeStruct(a.shape, F32),
        compiler_params=params(16),
        cost_estimate=cost(0, 5e6),
        name="ordered_sum",
    )(y, a, b)


def last_cut_kernel(counts, *refs):
    ins, gain_ref, outs = refs[: sum(counts)], refs[sum(counts)], refs[sum(counts) + 1 :]
    at, col = 0, 0
    for n in counts:
        total = ins[at][0]
        for r in ins[at + 1 : at + n]:
            total = total + r[0]
        wide = total.shape[-1]
        for e in range(4):
            outs[e][:, col : col + wide] = total[8 * e : 8 * e + 8]
        at, col = at + n, col + wide
    row = lax.broadcasted_iota(jnp.int32, (8, 128), 0)
    outs[1][:, col:] = jnp.where(row == 0, gain_ref[...], 0.0)


def last_cut(parts, gain):
    cells = [t.cells() for t in parts]
    counts = tuple(len(c) for c in cells)
    widths = [t.tail[1] for t, c in zip(parts, cells) for _ in c]
    cells = sum(cells, [])
    whole = lambda shape: pl.BlockSpec(shape, lambda i: (0, 0))
    wide = [4 * D, 4 * D + 128, 4 * D, 4 * D]
    return pl.pallas_call(
        functools.partial(last_cut_kernel, counts),
        grid=(1,),
        in_specs=[
            pl.BlockSpec((1, 32, wide), functools.partial(lambda at, col, i: (at, 0, col), at, col))
            for (_, at, col), wide in zip(cells, widths)
        ]
        + [whole((1, 128))],
        out_specs=tuple(whole((8, w)) for w in wide),
        out_shape=tuple(jax.ShapeDtypeStruct((8, w), F32) for w in wide),
        compiler_params=params(24),
        cost_estimate=cost(0, 5e6),
        name="last_cut",
    )(*[a for a, _, _ in cells], gain)


def quarter_kernel(own, got1, got2, got3, gain_ref, z_ref, out_ref, s0, s1, s2, s3, q_ref):
    total = own[...] + got1[:, : 4 * D] + got2[...] + got3[...]
    for g in range(GROUPS):
        for part in range(3):
            at = part * D + g * GW
            out_ref[:, at : at + GW] = total[:, g * D + part * GW : g * D + part * GW + GW]
        q_ref[g] = total[:, g * D + 3 * GW : g * D + D]
    gain = jnp.broadcast_to(gain_ref[...] + got1[0:1, 4 * D :], (8, 128))
    for d, send in enumerate((s0, s1, s2, s3)):
        send[:, :GW] = q_ref[z_ref[0] ^ d]
        send[:, GW:] = gain


def quarters_of(own, got, gain, z):
    return pl.pallas_call(
        quarter_kernel,
        out_shape=(jax.ShapeDtypeStruct((8, 3 * D), F32),)
        + (jax.ShapeDtypeStruct((8, GW + 128), F32),) * 4,
        in_specs=vmem(5) + [pl.BlockSpec(memory_space=pltpu.SMEM)],
        out_specs=tuple(vmem(5)),
        scratch_shapes=[pltpu.VMEM((4, 8, GW), F32)],
        compiler_params=params(16),
        cost_estimate=cost(0, 1e6),
        name="quarters_of",
    )(own, *got, gain, z)


def gather_kernel(m0, m1, m2, m3, z_ref, out_ref, gain_ref, q_ref):
    gain = None
    for d, m in enumerate((m0, m1, m2, m3)):
        q_ref[d] = m[:, :GW]
        term = m[0:1, GW:]
        gain = term if gain is None else gain + term
    for e in range(4):
        out_ref[:, e * GW : e * GW + GW] = q_ref[z_ref[0] ^ e]
    gain_ref[...] = gain


def gather_quarters(pieces, z):
    return pl.pallas_call(
        gather_kernel,
        out_shape=(jax.ShapeDtypeStruct((8, D), F32), jax.ShapeDtypeStruct((1, 128), F32)),
        in_specs=vmem(4) + [pl.BlockSpec(memory_space=pltpu.SMEM)],
        out_specs=tuple(vmem(2)),
        scratch_shapes=[pltpu.VMEM((4, 8, GW), F32)],
        compiler_params=params(16),
        cost_estimate=cost(0, 1e6),
        name="gather_quarters",
    )(*pieces, z)


def row_picks():
    lat, lon = lax.axis_index("lat"), lax.axis_index("lon")
    z, xl = lat // 2, lat % 2
    y, xh, c = lon // 4, (lon // 2) % 2, lon % 2
    x = xh * 2 + xl
    i = jnp.arange(D, dtype=jnp.int32)
    tc = c ^ (i // 512)
    ty = y ^ ((i // 128) % 4)
    tz = z ^ ((i // 32) % 4)
    tx = x ^ ((i // 8) % 4)
    block = ((tz * 2 + tx % 2) * 4 + ty) * 4 + (tx // 2) * 2 + tc
    source = block * 8 + i % 8
    i = jnp.arange(GW, dtype=jnp.int32)
    tc = c ^ (i // 128)
    ty = y ^ ((i // 32) % 4)
    tx = x ^ ((i // 8) % 4)
    block = ((tx % 2) * 4 + ty) * 4 + (tx // 2) * 2 + tc
    group = block * 8 + i % 8
    return tuple(
        (t[:, None] == jnp.arange(t.shape[0], dtype=jnp.int32)[None, :]).astype(BF16)
        for t in (source, group)
    )


def gain_mix():
    i = jnp.arange(D, dtype=jnp.int32)
    source = ((i // 8) % 8) * 128 + (i // 64) * 8 + i % 8
    return (jnp.arange(D, dtype=jnp.int32)[:, None] == source[None, :]).astype(BF16)


def window_order(a):
    a = a.reshape((2, 2, 6, 3, 12) + a.shape[3:])
    return a.transpose((1, 3, 0, 2, 4) + tuple(range(5, a.ndim)))


def per_device(latents, land_mask, norm_gain, qkv_weight, out_weight, out_cotangent):
    lon_index = lax.axis_index("lon")
    pieces = split_pieces(latents.transpose(0, 1, 3, 2))
    pieces = lax.all_to_all(pieces, "lon", split_axis=0, concat_axis=0, tiled=True)
    pick, pick_group = row_picks()
    z_index = (lax.axis_index("lat") // 2).reshape(1)
    mask = jnp.roll(land_mask, -SHIFT, axis=2)
    mask = lax.dynamic_slice_in_dim(mask, lon_index * 36, 36, 2)
    mask = jnp.where(window_order(mask).reshape(TOK, 1) == 1, 0.0, -1e30).astype(F32)
    up = window_order(out_cotangent).reshape(TOK, D)
    gain = norm_gain.reshape(1, D)
    x, scaled, scaled_t = enter(pieces, gain, pick)
    y_index = (lon_index // 4).reshape(1)
    att, grads = [], []

    def heads(g, after):
        a, d, keep, send = attend(
            g, scaled, scaled_t, up, qkv_weight, out_weight, mask, pick_group, z_index, after
        )
        att.append(a)
        grads.append(d)
        return Sum(keep, lax.ppermute(send, AXES, swapped(core=1)))

    def newest(t):
        return t.terms[-1][0]

    s0 = heads(0, ())
    s1 = heads(1, ())
    total = s0.ring_y(y_index)
    s2 = heads(2, (total,))
    total = s1.ring_y(y_index)
    s3 = heads(3, (total,))
    out2, _ = exchange([s2], "z", 1)
    norm_grad = product(grads, qkv_weight, (out2,))
    s3, s4 = s3.columns(0, 2 * GW), s3.columns(2 * GW, 4 * GW)
    out3, _ = exchange([s3], "z", 1)
    out4, _ = exchange([s4], "z", 3)
    leaving = leave(norm_grad, x, up, gain, gain_mix(), (out3, out4))
    back = lax.all_to_all(leaving, "lon", split_axis=0, concat_axis=0, tiled=True)
    def hand(sums, arrays):
        for t, p in zip(sums, arrays):
            t.terms[-1] = (p,) + t.terms[-1][1:]

    waiting = (s2, s3, s4)
    block, *passed = block_sum(att, x, out_weight, [newest(t) for t in waiting], (leaving,))
    hand(waiting, passed)
    exchange([s2], "z", 3)
    exchange([s3], "z", 3)
    exchange([s4], "z", 1)
    exchange([s2, s3, s4], "y", 1)
    exchange([s0, s1], "z", 1)
    joined, gain_sum, one, two = join_pieces(back, (newest(s2), newest(s0)), (block,))
    hand((s2, s3, s4, s0, s1), (one, one, one, two, two))
    exchange([s2, s3, s4], "y", 3)
    exchange([s0, s1], "z", 3)
    own, *send = last_cut((s0, s1, s2, s3, s4), gain_sum)
    got = [lax.ppermute(a, AXES, swapped(x=d)) for d, a in zip((1, 2, 3), send)]
    qkv_weight_grad, own, *send = quarters_of(own, got, gain_sum, z_index)
    got = [lax.ppermute(a, AXES, swapped(z=d)) for d, a in zip((1, 2, 3), send)]
    out_weight_grad, gain_sum = gather_quarters([own] + got, z_index)
    at = (lon_index % 2) * 64 + lax.axis_index("lat") * 8
    gain_grad = lax.dynamic_slice_in_dim(gain_sum.reshape(128), at, 8, 0)
    block = block.reshape(2, 3, 2, 6, 12, D).transpose(2, 0, 3, 1, 4, 5).reshape(2, 12, 36, D)
    latent_grad = joined.transpose(0, 1, 3, 2)
    return (block, latent_grad, qkv_weight_grad, out_weight_grad, gain_grad)


def solution(mesh):
    return jax.shard_map(
        per_device,
        mesh=mesh,
        in_specs=(
            P(None, "lat", None, "lon"),
            P(None, "lat", None),
            P(),
            P(),
            P(),
            P(None, "lat", "lon", None),
        ),
        out_specs=(
            P(None, "lat", "lon", None),
            P(None, "lat", None, "lon"),
            P(("lat", "lon"), None),
            P(("lat", "lon"), None),
            P(("lat", "lon")),
        ),
        check_vma=False,
    )
```

time: 333 us -> 279 us (0.84)
  starting transfers between devices: 107 us -> 38.4 us
  Pallas kernels: 114 us -> 91.8 us
  waiting for transfers between devices: 53.9 us -> 71.2 us
  between operations: 1.62 us -> 14.7 us
  local copies, waits for them, and re-layouts: 31.5 us -> 42.5 us
    ppermute x50 -> x20, starting transfers between devices: 85.8 us -> 26.4 us  [the longest x10 16.1 us: exchange(): got = lax.ppermute(out, AXES, swapped(**{name: by}))]
    pallas_call x8 -> x13, Pallas kernels: 101 us -> 80.3 us  [the longest x4 56 us: attend(): pl.pallas_call(behind(attend_kernel, len(after), 10), grid=(1,), out_shap...]
    ppermute x50 -> x20, waiting for transfers between devices: 33.4 us -> 52 us  [the longest x10 36.3 us: exchange(): got = lax.ppermute(out, AXES, swapped(**{name: by}))]
    all_to_all x1, waiting for transfers between devices: 20.5 us -> 11 us  [per_device(): lax.all_to_all(pieces, 'lon', split_axis=0, concat_axis=0, tiled=True)]
    all_to_all x2 -> x1, starting transfers between devices: 13.8 us -> 4.55 us  [per_device(): lax.all_to_all(leaving, 'lon', split_axis=0, concat_axis=0, tiled=True)]
    all_to_all x2 -> x1, waiting for transfers between devices: 0.01 us -> 8.13 us  [per_device(): lax.all_to_all(leaving, 'lon', split_axis=0, concat_axis=0, tiled=True)]
    add x17 -> x6, other arithmetic: 17.9 us -> 10.6 us  [cut(): total = piece if total is None else total + piece]
    select_n x3, local copies, waits for them, and re-layouts: 0.28 us -> 4.58 us  [per_device(): jnp.where(window_order(mask).reshape(TOK, 1) == 1, 0.0, -1e+30).astype(F32)]
  transfers between devices with their start and end apart: 53 -> 24, of which waited for: 15 -> 11; matrix products, arithmetic and copies ran while one was open for 10% -> 13% of each run, Pallas kernels for 14% -> 21%
where the time goes in v2:
time: 279 us; the launch traced here: 278 us
  Pallas kernels  91.8 us (33%)
  waiting for transfers between devices  71.2 us (26%)
  local copies, waits for them, and re-layouts  42.5 us (15%)
  starting transfers between devices  38.4 us (14%)
  other arithmetic  19.2 us (7%)
  between operations  14.7 us (5%)
    pallas_call x4, Pallas kernels, attend(): pl.pallas_call(behind(attend_kernel, len(after), 10), grid=(1,), out_shap...  56 us
    ppermute x10, waiting for transfers between devices, exchange(): got = lax.ppermute(out, AXES, swapped(**{name: by}))  36.3 us
    unnamed x98, local copies, waits for them, and re-layouts  21.9 us
    ppermute x10, starting transfers between devices, exchange(): got = lax.ppermute(out, AXES, swapped(**{name: by}))  16.1 us
    all_to_all x1, waiting for transfers between devices, per_device(): lax.all_to_all(pieces, 'lon', split_axis=0, concat_axis=0, tiled=True)  11 us
    add x6, other arithmetic, cut(): total = piece if total is None else total + piece  10.6 us
    pallas_call x1, Pallas kernels, product(): pl.pallas_call(behind(product_kernel, len(after), 5), out_shape=jax.Shape...  8.83 us
    ppermute x4, waiting for transfers between devices, heads(): return Sum(keep, lax.ppermute(send, AXES, swapped(core=1)))  8.58 us
  transfers between devices with their start and end apart: 24, of which 11 were waited for; matrix products, arithmetic and copies ran while one was open for 13% of the time, Pallas kernels for 21%

profile of v2, /device:TPU:0, one launch (start us, length us, event | category | flops | bytes accessed | tf_op | source)
XLA Modules:
  0.0 277.8 jit_solution(15985277943137132411)
XLA Ops:
  8.7 4.2 %split_pieces.1 = bf16[16,432,128]{2,1,0:T(8,128)(2,1)} custom-call(bf16[2,12,64,576]{3,2,1,0:T(8,128)(2,1)S(1)} %bitcast.142), custom_call_target="tpu_custom_call" | custom-call | flops 200000000 | bytes 400000 | tf_op jit(solution)/shard_map/split_pieces/pallas_call | solution.py:79
  12.9 7.2 %all-to-all-start = ((bf16[16,432,128]{2,1,0:T(8,128)(2,1)}), bf16[16,432,128]{2,1,0:T(8,128)(2,1)S(1)}, u32[]{:S(2)}, u32[]{:S(2)}) async-start(bf16[16,432,128]{2,1,0:T(8,128)(2,1)} %split_pieces.1), calls=%async_computation | async-start | bytes 3538944 | tf_op jit(solution)/shard_map/all_to_all | solution.py:629
  29.9 2.5 reshape.434.refs_2_
  35.0 11.0 %all-to-all-done.r_ref = bf16[16,432,128]{2,1,0:T(8,128)(2,1)S(1)} async-done(((bf16[16,432,128]{2,1,0:T(8,128)(2,1)}), bf16[16,432,128]{2,1,0:T(8,128)(2,1)S(1)}, u32[]{:S(2)}, u32[]{:S(2)}) %all-to-all-start) | async-done | bytes 1769504 | tf_op jit(solution)/shard_map/all_to_all | solution.py:629
  50.3 7.3 %enter.1 = (bf16[864,1024]{1,0:T(8,128)(2,1)S(1)}, bf16[864,1024]{1,0:T(8,128)(2,1)S(1)}, bf16[1024,864]{1,0:T(8,128)(2,1)S(1)}) custom-call(bf16[16,432,128]{2,1,0:T(8,128)(2,1)S(1)} %copy-done.14, f32[1,1024]{1,0:T(1,128)S(1)} %bitcast.152, bf16[1024,1024]{1,0:T(8,128)(2,1)S(1)} %copy-done.11), custom_call_target="tpu_custom_call" | custom-call | flops 300000000 | bytes 900000 | tf_op jit(solution)/shard_map/enter/pallas_call | solution.py:129
  58.8 14.5 %attend.5 = (bf16[864,256]{1,0:T(8,128)(2,1)S(1)}, bf16[864,768]{1,0:T(8,128)(2,1)S(1)}, f32[512,1024]{1,0:T(8,128)}, f32[512,1024]{1,0:T(8,128)}) custom-call(bf16[864,1024]{1,0:T(8,128)(2,1)S(1)} %get-tuple-element.43.refs_0_, bf16[1024,864]{1,0:T(8,128)(2,1)} %copy-done.1, bf16[864,1024]{1,0:T(8,128)(2,1)S(1)} %reshape.434.refs_2_, ...), custom_call_target="tpu_custom_call" | custom-call | flops 800000000 | bytes 1500000 | tf_op jit(solution)/shard_map/attend/pallas_call | solution.py:213
  73.4 4.4 %collective-permute-done.1 = f32[512,1024]{1,0:T(8,128)S(1)} collective-permute-done((f32[512,1024]{1,0:T(8,128)}, f32[512,1024]{1,0:T(8,128)S(1)}, u32[]{:S(2)}, u32[]{:S(2)}) %collective-permute-start.1) | collective-permute-done | bytes 2097184 | tf_op jit(solution)/shard_map/ppermute | solution.py:647
  83.2 13.8 %attend.4 = (bf16[864,256]{1,0:T(8,128)(2,1)S(1)}, bf16[864,768]{1,0:T(8,128)(2,1)S(1)}, f32[512,1024]{1,0:T(8,128)}, f32[512,1024]{1,0:T(8,128)}) custom-call(bf16[864,1024]{1,0:T(8,128)(2,1)S(1)} %get-tuple-element.43.refs_0_, bf16[1024,864]{1,0:T(8,128)(2,1)} %copy-done.1, bf16[864,1024]{1,0:T(8,128)(2,1)S(1)} %reshape.434.refs_2_, ...), custom_call_target="tpu_custom_call" | custom-call | flops 800000000 | bytes 1500000 | tf_op jit(solution)/shard_map/attend/pallas_call | solution.py:213
  99.0 4.2 %collective-permute-done = f32[512,1024]{1,0:T(8,128)S(1)} collective-permute-done((f32[512,1024]{1,0:T(8,128)}, f32[512,1024]{1,0:T(8,128)S(1)}, u32[]{:S(2)}, u32[]{:S(2)}) %collective-permute-start) | collective-permute-done | bytes 2097184 | tf_op jit(solution)/shard_map/ppermute | solution.py:647
  106.5 13.8 %attend.6 = (bf16[864,256]{1,0:T(8,128)(2,1)S(1)}, bf16[864,768]{1,0:T(8,128)(2,1)S(1)}, f32[512,1024]{1,0:T(8,128)}, f32[512,1024]{1,0:T(8,128)}) custom-call(bf16[864,1024]{1,0:T(8,128)(2,1)S(1)} %get-tuple-element.43.refs_0_, bf16[1024,864]{1,0:T(8,128)(2,1)} %copy-done.1, bf16[864,1024]{1,0:T(8,128)(2,1)S(1)} %reshape.434.refs_2_, ...), custom_call_target="tpu_custom_call" | custom-call | flops 800000000 | bytes 1500000 | tf_op jit(solution)/shard_map/attend/pallas_call | solution.py:213
  122.3 13.9 %attend.7 = (bf16[864,256]{1,0:T(8,128)(2,1)S(1)}, bf16[864,768]{1,0:T(8,128)(2,1)S(1)}, f32[512,1024]{1,0:T(8,128)}, f32[512,1024]{1,0:T(8,128)}) custom-call(bf16[864,1024]{1,0:T(8,128)(2,1)S(1)} %get-tuple-element.43.refs_0_, bf16[1024,864]{1,0:T(8,128)(2,1)} %copy-done.1, bf16[864,1024]{1,0:T(8,128)(2,1)S(1)} %reshape.434.refs_2_, ...), custom_call_target="tpu_custom_call" | custom-call | flops 800000000 | bytes 1500000 | tf_op jit(solution)/shard_map/attend/pallas_call | solution.py:213
  140.3 2.3 collective-permute-start.3
  146.2 2.5 collective-permute-start.6
  149.6 8.8 %product.1.refs_0_ = f32[864,1024]{1,0:T(8,128)S(1)} custom-call(bf16[864,768]{1,0:T(8,128)(2,1)S(1)} %copy-done.34, bf16[864,768]{1,0:T(8,128)(2,1)S(1)} %copy-done.32, bf16[864,768]{1,0:T(8,128)(2,1)S(1)} %copy-done.36, bf16[864,768]{1,0:T(8,128)(2,1)S(1)} %copy-done.38, bf16[1024,3072]{1,0:T(8,128)(2,1)} %refs_4_.9, f32[32,8,1024]{2,1,0:T(8,128)S(1)} %bitcast.130), custom_call_target="tpu_custom_call" | custom-call | flops 600000000 | bytes 1500000 | tf_op jit(solution)/shard_map/product/pallas_call | solution.py:291
  158.5 6.2 %leave.1.refs_9_ = bf16[16,448,128]{2,1,0:T(8,128)(2,1)S(1)} custom-call(f32[864,1024]{1,0:T(8,128)S(1)} %product.1.refs_0_, bf16[864,1024]{1,0:T(8,128)(2,1)S(1)} %copy-done.18, bf16[864,1024]{1,0:T(8,128)(2,1)S(1)} %reshape.434.refs_2_, f32[1,1024]{1,0:T(1,128)S(1)} %bitcast.153, bf16[1024,1024]{1,0:T(8,128)(2,1)S(1)} %fusion.1.refs_4_, ...), custom_call_target="tpu_custom_call" | custom-call | flops 400000000 | bytes 1000000 | tf_op jit(solution)/shard_map/leave/pallas_call | solution.py:336
  164.7 12.6 %collective-permute-done.5 = f32[32,8,512]{2,1,0:T(8,128)S(1)} collective-permute-done((f32[32,8,512]{2,1,0:T(8,128)S(1)}, f32[32,8,512]{2,1,0:T(8,128)S(1)}, u32[]{:S(2)}, u32[]{:S(2)}) %collective-permute-start.5) | collective-permute-done | bytes 524320 | tf_op jit(solution)/shard_map/ppermute | solution.py:471
  177.3 2.2 block_sum.1
  179.6 2.9 %fusion.2 = f32[4,1,4,8,1024]{4,3,2,1,0:T(8,128)} fusion(f32[4,4,4,8,1024]{4,3,2,1,0:T(8,128)} %bitcast.12, f32[4,4,4,8,1024]{4,3,2,1,0:T(8,128)} %bitcast.118, f32[4,2,4,8,1024]{4,3,2,1,0:T(8,128)S(1)} %get-tuple-element.63), kind=kLoop, calls=%fused_computation.7 | loop fusion | flops 262144 | bytes 2097152 | tf_op jit(solution)/shard_map/add | solution.py:430
  182.5 3.9 %collective-permute-start.7 = (f32[16,8,1024]{2,1,0:T(8,128)}, f32[16,8,1024]{2,1,0:T(8,128)}, u32[]{:S(2)}, u32[]{:S(2)}) collective-permute-start(f32[16,8,1024]{2,1,0:T(8,128)} %bitcast.23), channel_id=1, source_target_pairs={{0,96},{1,97},{2,98},{3,99},{4,100},{5,101},{6,102},{7,103},{8,104... | collective-permute-start | bytes 1572872 | tf_op jit(solution)/shard_map/ppermute | solution.py:471
  188.5 4.6 %all-to-all-start.1 = ((bf16[16,448,128]{2,1,0:T(8,128)(2,1)}), bf16[16,448,128]{2,1,0:T(8,128)(2,1)}, u32[]{:S(2)}, u32[]{:S(2)}) async-start(bf16[16,448,128]{2,1,0:T(8,128)(2,1)} %copy-done.6), calls=%async_computation.1 | async-start | bytes 3670016 | tf_op jit(solution)/shard_map/all_to_all | solution.py:664
  193.1 10.5 %collective-permute-done.8 = f32[16,8,512]{2,1,0:T(8,128)S(1)} collective-permute-done((f32[16,8,512]{2,1,0:T(8,128)}, f32[16,8,512]{2,1,0:T(8,128)S(1)}, u32[]{:S(2)}, u32[]{:S(2)}) %collective-permute-start.8) | collective-permute-done | bytes 262176 | tf_op jit(solution)/shard_map/ppermute | solution.py:471
  211.4 8.1 %all-to-all-done.1.refs_0_ = bf16[16,448,128]{2,1,0:T(8,128)(2,1)} async-done(((bf16[16,448,128]{2,1,0:T(8,128)(2,1)}), bf16[16,448,128]{2,1,0:T(8,128)(2,1)}, u32[]{:S(2)}, u32[]{:S(2)}) %all-to-all-start.1) | async-done | bytes 1835040 | tf_op jit(solution)/shard_map/all_to_all | solution.py:664
  219.6 7.5 %collective-permute-done.10 = f32[8,8,2048]{2,1,0:T(8,128)S(1)} collective-permute-done((f32[8,8,2048]{2,1,0:T(8,128)}, f32[8,8,2048]{2,1,0:T(8,128)S(1)}, u32[]{:S(2)}, u32[]{:S(2)}) %collective-permute-start.10) | collective-permute-done | bytes 524320 | tf_op jit(solution)/shard_map/ppermute | solution.py:471
  228.5 4.0 %join_pieces.1 = (bf16[2,12,64,576]{3,2,1,0:T(8,128)(2,1)}, f32[1,128]{1,0:T(1,128)S(1)}, f32[2,1,4,8,2048]{4,3,2,1,0:T(8,128)S(1)}, f32[1,2,4,8,2048]{4,3,2,1,0:T(8,128)S(1)}) custom-call(bf16[16,448,128]{2,1,0:T(8,128)(2,1)} %all-to-all-done.1.refs_0_, f32[2,1,4,8,2048]{4,3,2,1,0:T(8,128)S(1)} %bitcast.111, ...), custom_call_target="tpu_custom_call", output_to_operand_aliasing={{2}: (1, {}), {3}: (2, {})} | custom-call | flops 200000000 | bytes 400000 | tf_op jit(solution)/shard_map/join_pieces/pallas_call | solution.py:375
  234.7 2.1 collective-permute-start.13
  236.8 3.2 %collective-permute-start.12 = (f32[4,8,2048]{2,1,0:T(8,128)S(1)}, f32[4,8,2048]{2,1,0:T(8,128)S(1)}, u32[]{:S(2)}, u32[]{:S(2)}) collective-permute-start(f32[4,8,2048]{2,1,0:T(8,128)S(1)} %pad_maximum_fusion.2), channel_id=1, source_target_pairs={{0,96},{1,97},{2,98},{3,99},{4,100},{5,101},{6,102},{7,103},{8,104... | collective-permute-start | bytes 786440 | tf_op jit(solution)/shard_map/ppermute | solution.py:471
  240.0 3.8 %collective-permute-done.13 = f32[4,8,2048]{2,1,0:T(8,128)S(1)} collective-permute-done((f32[4,8,2048]{2,1,0:T(8,128)S(1)}, f32[4,8,2048]{2,1,0:T(8,128)S(1)}, u32[]{:S(2)}, u32[]{:S(2)}) %collective-permute-start.13) | collective-permute-done | bytes 262176 | tf_op jit(solution)/shard_map/ppermute | solution.py:471
  247.8 4.0 %collective-permute-start.15 = (f32[8,4096]{1,0:T(8,128)S(1)}, f32[8,4096]{1,0:T(8,128)S(1)}, u32[]{:S(2)}, u32[]{:S(2)}) collective-permute-start(f32[8,4096]{1,0:T(8,128)S(1)} %get-tuple-element.72), channel_id=1, source_target_pairs={{0,2},{1,3},{2,0},{3,1},{4,6},{5,7},{6,4},{7,5},{8,10},{9,11},{10,... | collective-permute-start | bytes 393224 | tf_op jit(solution)/shard_map/ppermute | solution.py:682
  251.8 5.5 %collective-permute-done.15.got2 = f32[8,4096]{1,0:T(8,128)S(1)} collective-permute-done((f32[8,4096]{1,0:T(8,128)S(1)}, f32[8,4096]{1,0:T(8,128)S(1)}, u32[]{:S(2)}, u32[]{:S(2)}) %collective-permute-start.15) | collective-permute-done | bytes 131104 | tf_op jit(solution)/shard_map/ppermute | solution.py:682
  261.1 2.6 collective-permute-start.18
  264.3 2.4 reshape.447
  266.7 3.1 %copy.37 = bf16[2,2,6,3,12,1024]{5,0,4,3,2,1:T(2,128)(2,1)} copy(bf16[2,2,6,3,12,1024]{5,4,2,0,3,1:T(8,128)(2,1)S(1)} %bitcast.154) | data formatting | bytes 3538944 | tf_op jit(solution)/shard_map/transpose | solution.py:688
  (167 shorter events, 63.7 us)
Async XLA Ops:
  12.9 15.0 %copy-start.48 = (bf16[2,12,36,1024]{3,0,2,1:T(2,128)(2,1)S(1)}, bf16[2,12,36,1024]{3,0,2,1:T(2,128)(2,1)}, u32[]{:S(2)}) copy-start(bf16[2,12,36,1024]{3,0,2,1:T(2,128)(2,1)} %param.11) | copy-start | bytes 5308420
  12.9 33.0 %all-to-all-start = ((bf16[16,432,128]{2,1,0:T(8,128)(2,1)}), bf16[16,432,128]{2,1,0:T(8,128)(2,1)S(1)}, u32[]{:S(2)}, u32[]{:S(2)}) async-start(bf16[16,432,128]{2,1,0:T(8,128)(2,1)} %split_pieces.1), calls=%async_computation | async-start | bytes 3538944 | tf_op jit(solution)/shard_map/all_to_all | solution.py:629
  20.2 188.5 %reduce-scatter.5.cloned.1.call-start = ((), (), s32[]{:S(2)}) async-start(), calls=%async_computation.5 | async-start | bytes 2621440 | tf_op jit(solution)/shard_map/reduce_scatter | solution.py:448
  73.3 4.5 %collective-permute-start.1 = (f32[512,1024]{1,0:T(8,128)}, f32[512,1024]{1,0:T(8,128)S(1)}, u32[]{:S(2)}, u32[]{:S(2)}) collective-permute-start(f32[512,1024]{1,0:T(8,128)} %get-tuple-element.51), channel_id=1, source_target_pairs={{0,1},{1,0},{2,3},{3,2},{4,5},{5,4},{6,7},{7,6},{8,9},{9,8},{10,11... | collective-permute-start | bytes 6291464 | tf_op jit(solution)/shard_map/ppermute | solution.py:647
  81.0 128.6 %reduce-scatter.3.cloned.1.call-start = ((), (), s32[]{:S(2)}) async-start(), calls=%async_computation.4 | async-start | bytes 2621440 | tf_op jit(solution)/shard_map/reduce_scatter | solution.py:448
  98.9 4.4 %collective-permute-start = (f32[512,1024]{1,0:T(8,128)}, f32[512,1024]{1,0:T(8,128)S(1)}, u32[]{:S(2)}, u32[]{:S(2)}) collective-permute-start(f32[512,1024]{1,0:T(8,128)} %get-tuple-element.48), channel_id=1, source_target_pairs={{0,1},{1,0},{2,3},{3,2},{4,5},{5,4},{6,7},{7,6},{8,9},{9,8},{10,11... | collective-permute-start | bytes 6291464 | tf_op jit(solution)/shard_map/ppermute | solution.py:647
  122.1 16.3 %collective-permute-start.2 = (f32[512,1024]{1,0:T(8,128)}, f32[512,1024]{1,0:T(8,128)}, u32[]{:S(2)}, u32[]{:S(2)}) collective-permute-start(f32[512,1024]{1,0:T(8,128)} %get-tuple-element.55), channel_id=1, source_target_pairs={{0,1},{1,0},{2,3},{3,2},{4,5},{5,4},{6,7},{7,6},{8,9},{9,8},{10,11... | collective-permute-start | bytes 6291464 | tf_op jit(solution)/shard_map/ppermute | solution.py:647
  138.0 4.6 %collective-permute-start.4 = (f32[512,1024]{1,0:T(8,128)}, f32[512,1024]{1,0:T(8,128)}, u32[]{:S(2)}, u32[]{:S(2)}) collective-permute-start(f32[512,1024]{1,0:T(8,128)} %get-tuple-element.57), channel_id=1, source_target_pairs={{0,1},{1,0},{2,3},{3,2},{4,5},{5,4},{6,7},{7,6},{8,9},{9,8},{10,11... | collective-permute-start | bytes 6291464 | tf_op jit(solution)/shard_map/ppermute | solution.py:647
  140.3 37.0 %collective-permute-start.3 = (f32[32,8,1024]{2,1,0:T(8,128)S(1)}, f32[32,8,1024]{2,1,0:T(8,128)S(1)}, u32[]{:S(2)}, u32[]{:S(2)}) collective-permute-start(f32[32,8,1024]{2,1,0:T(8,128)S(1)} %bitcast.129), channel_id=1, source_target_pairs={{0,32},{1,33},{2,34},{3,35},{4,36},{5,37},{6,38},{7,39},{8,40},{9,... | collective-permute-start | bytes 3145736 | tf_op jit(solution)/shard_map/ppermute | solution.py:471
  144.2 33.1 %collective-permute-start.5 = (f32[32,8,512]{2,1,0:T(8,128)S(1)}, f32[32,8,512]{2,1,0:T(8,128)S(1)}, u32[]{:S(2)}, u32[]{:S(2)}) collective-permute-start(f32[32,8,512]{2,1,0:T(8,128)S(1)} %bitcast.140), channel_id=1, source_target_pairs={{0,32},{1,33},{2,34},{3,35},{4,36},{5,37},{6,38},{7,39},{8,40},{9,... | collective-permute-start | bytes 1572872 | tf_op jit(solution)/shard_map/ppermute | solution.py:471
  146.2 31.1 %collective-permute-start.6 = (f32[32,8,512]{2,1,0:T(8,128)S(1)}, f32[32,8,512]{2,1,0:T(8,128)S(1)}, u32[]{:S(2)}, u32[]{:S(2)}) collective-permute-start(f32[32,8,512]{2,1,0:T(8,128)S(1)} %bitcast.138), channel_id=1, source_target_pairs={{0,96},{1,97},{2,98},{3,99},{4,100},{5,101},{6,102},{7,103},{8,104... | collective-permute-start | bytes 1572872 | tf_op jit(solution)/shard_map/ppermute | solution.py:471
  158.5 18.8 %copy-start = (bf16[1024,1024]{1,0:T(8,128)(2,1)S(1)}, bf16[1024,1024]{1,0:T(8,128)(2,1)}, u32[]{:S(2)}) copy-start(bf16[1024,1024]{1,0:T(8,128)(2,1)} %refs_5_.9) | copy-start | bytes 6291460
  158.5 18.8 %copy-start.40 = (bf16[864,256]{1,0:T(8,128)(2,1)S(1)}, bf16[864,256]{1,0:T(8,128)(2,1)}, u32[]{:S(2)}) copy-start(bf16[864,256]{1,0:T(8,128)(2,1)} %copy-done.39) | copy-start | bytes 1327108
  158.5 18.8 %copy-start.42 = (bf16[864,256]{1,0:T(8,128)(2,1)S(1)}, bf16[864,256]{1,0:T(8,128)(2,1)}, u32[]{:S(2)}) copy-start(bf16[864,256]{1,0:T(8,128)(2,1)} %copy-done.41) | copy-start | bytes 1327108
  158.5 18.8 %copy-start.44 = (bf16[864,256]{1,0:T(8,128)(2,1)S(1)}, bf16[864,256]{1,0:T(8,128)(2,1)}, u32[]{:S(2)}) copy-start(bf16[864,256]{1,0:T(8,128)(2,1)} %copy-done.43) | copy-start | bytes 1327108
  158.5 18.8 %copy-start.46 = (bf16[864,256]{1,0:T(8,128)(2,1)S(1)}, bf16[864,256]{1,0:T(8,128)(2,1)}, u32[]{:S(2)}) copy-start(bf16[864,256]{1,0:T(8,128)(2,1)} %copy-done.45) | copy-start | bytes 1327108
  179.6 27.1 %copy-start.9 = (f32[4,2,4,8,1024]{4,3,2,1,0:T(8,128)}, f32[4,2,4,8,1024]{4,3,2,1,0:T(8,128)S(1)}, u32[]{:S(2)}) copy-start(f32[4,2,4,8,1024]{4,3,2,1,0:T(8,128)S(1)} %get-tuple-element.63) | copy-start | bytes 3145732
  182.5 23.2 %collective-permute-start.7 = (f32[16,8,1024]{2,1,0:T(8,128)}, f32[16,8,1024]{2,1,0:T(8,128)}, u32[]{:S(2)}, u32[]{:S(2)}) collective-permute-start(f32[16,8,1024]{2,1,0:T(8,128)} %bitcast.23), channel_id=1, source_target_pairs={{0,96},{1,97},{2,98},{3,99},{4,100},{5,101},{6,102},{7,103},{8,104... | collective-permute-start | bytes 1572872 | tf_op jit(solution)/shard_map/ppermute | solution.py:471
  188.3 15.2 %collective-permute-start.8 = (f32[16,8,512]{2,1,0:T(8,128)}, f32[16,8,512]{2,1,0:T(8,128)S(1)}, u32[]{:S(2)}, u32[]{:S(2)}) collective-permute-start(f32[16,8,512]{2,1,0:T(8,128)} %bitcast.27), channel_id=1, source_target_pairs={{0,96},{1,97},{2,98},{3,99},{4,100},{5,101},{6,102},{7,103},{8,104... | collective-permute-start | bytes 786440 | tf_op jit(solution)/shard_map/ppermute | solution.py:471
  188.4 16.1 %copy-start.5 = (f32[512,1024]{1,0:T(8,128)S(1)}, f32[512,1024]{1,0:T(8,128)}, u32[]{:S(2)}) copy-start(f32[512,1024]{1,0:T(8,128)} %get-tuple-element.56) | copy-start | bytes 6291460
  188.4 15.1 %collective-permute-start.9 = (f32[16,8,512]{2,1,0:T(8,128)}, f32[16,8,512]{2,1,0:T(8,128)}, u32[]{:S(2)}, u32[]{:S(2)}) collective-permute-start(f32[16,8,512]{2,1,0:T(8,128)} %bitcast.31), channel_id=1, source_target_pairs={{0,32},{1,33},{2,34},{3,35},{4,36},{5,37},{6,38},{7,39},{8,40},{9,... | collective-permute-start | bytes 786440 | tf_op jit(solution)/shard_map/ppermute | solution.py:471
  188.5 31.1 %all-to-all-start.1 = ((bf16[16,448,128]{2,1,0:T(8,128)(2,1)}), bf16[16,448,128]{2,1,0:T(8,128)(2,1)}, u32[]{:S(2)}, u32[]{:S(2)}) async-start(bf16[16,448,128]{2,1,0:T(8,128)(2,1)} %copy-done.6), calls=%async_computation.1 | async-start | bytes 3670016 | tf_op jit(solution)/shard_map/all_to_all | solution.py:664
  208.6 18.4 %collective-permute-start.10 = (f32[8,8,2048]{2,1,0:T(8,128)}, f32[8,8,2048]{2,1,0:T(8,128)S(1)}, u32[]{:S(2)}, u32[]{:S(2)}) collective-permute-start(f32[8,8,2048]{2,1,0:T(8,128)} %pad_maximum_fusion), channel_id=1, source_target_pairs={{0,4},{1,5},{2,6},{3,7},{4,0},{5,1},{6,2},{7,3},{8,12},{9,13},{10,... | collective-permute-start | bytes 1572872 | tf_op jit(solution)/shard_map/ppermute | solution.py:471
  211.4 15.6 %collective-permute-start.11 = (f32[8,8,2048]{2,1,0:T(8,128)}, f32[8,8,2048]{2,1,0:T(8,128)S(1)}, u32[]{:S(2)}, u32[]{:S(2)}) collective-permute-start(f32[8,8,2048]{2,1,0:T(8,128)} %pad_maximum_fusion.1), channel_id=1, source_target_pairs={{0,32},{1,33},{2,34},{3,35},{4,36},{5,37},{6,38},{7,39},{8,40},{9,... | collective-permute-start | bytes 1572872 | tf_op jit(solution)/shard_map/ppermute | solution.py:471
  234.7 9.1 %collective-permute-start.13 = (f32[4,8,2048]{2,1,0:T(8,128)S(1)}, f32[4,8,2048]{2,1,0:T(8,128)S(1)}, u32[]{:S(2)}, u32[]{:S(2)}) collective-permute-start(f32[4,8,2048]{2,1,0:T(8,128)S(1)} %pad_maximum_fusion.3), channel_id=1, source_target_pairs={{0,12},{1,13},{2,14},{3,15},{4,8},{5,9},{6,10},{7,11},{8,4},{9,5},... | collective-permute-start | bytes 786440 | tf_op jit(solution)/shard_map/ppermute | solution.py:471
  236.8 9.0 %collective-permute-start.12 = (f32[4,8,2048]{2,1,0:T(8,128)S(1)}, f32[4,8,2048]{2,1,0:T(8,128)S(1)}, u32[]{:S(2)}, u32[]{:S(2)}) collective-permute-start(f32[4,8,2048]{2,1,0:T(8,128)S(1)} %pad_maximum_fusion.2), channel_id=1, source_target_pairs={{0,96},{1,97},{2,98},{3,99},{4,100},{5,101},{6,102},{7,103},{8,104... | collective-permute-start | bytes 786440 | tf_op jit(solution)/shard_map/ppermute | solution.py:471
  247.0 11.9 %collective-permute-start.14 = (f32[8,4224]{1,0:T(8,128)S(1)}, f32[8,4224]{1,0:T(8,128)S(1)}, u32[]{:S(2)}, u32[]{:S(2)}) collective-permute-start(f32[8,4224]{1,0:T(8,128)S(1)} %get-tuple-element.71), channel_id=1, source_target_pairs={{0,16},{1,17},{2,18},{3,19},{4,20},{5,21},{6,22},{7,23},{8,24},{9,... | collective-permute-start | bytes 405512 | tf_op jit(solution)/shard_map/ppermute | solution.py:682
  247.8 9.5 %collective-permute-start.15 = (f32[8,4096]{1,0:T(8,128)S(1)}, f32[8,4096]{1,0:T(8,128)S(1)}, u32[]{:S(2)}, u32[]{:S(2)}) collective-permute-start(f32[8,4096]{1,0:T(8,128)S(1)} %get-tuple-element.72), channel_id=1, source_target_pairs={{0,2},{1,3},{2,0},{3,1},{4,6},{5,7},{6,4},{7,5},{8,10},{9,11},{10,... | collective-permute-start | bytes 393224 | tf_op jit(solution)/shard_map/ppermute | solution.py:682
  251.8 7.1 %collective-permute-start.16 = (f32[8,4096]{1,0:T(8,128)S(1)}, f32[8,4096]{1,0:T(8,128)S(1)}, u32[]{:S(2)}, u32[]{:S(2)}) collective-permute-start(f32[8,4096]{1,0:T(8,128)S(1)} %get-tuple-element.73), channel_id=1, source_target_pairs={{0,18},{1,19},{2,16},{3,17},{4,22},{5,23},{6,20},{7,21},{8,26},{9,... | collective-permute-start | bytes 393224 | tf_op jit(solution)/shard_map/ppermute | solution.py:682
  259.6 10.2 %collective-permute-start.17 = (f32[8,384]{1,0:T(8,128)S(1)}, f32[8,384]{1,0:T(8,128)S(1)}, u32[]{:S(2)}, u32[]{:S(2)}) collective-permute-start(f32[8,384]{1,0:T(8,128)S(1)} %get-tuple-element.76), channel_id=1, source_target_pairs={{0,32},{1,33},{2,34},{3,35},{4,36},{5,37},{6,38},{7,39},{8,40},{9,... | collective-permute-start | bytes 36872 | tf_op jit(solution)/shard_map/ppermute | solution.py:684
  261.1 8.7 %collective-permute-start.18 = (f32[8,384]{1,0:T(8,128)S(1)}, f32[8,384]{1,0:T(8,128)S(1)}, u32[]{:S(2)}, u32[]{:S(2)}) collective-permute-start(f32[8,384]{1,0:T(8,128)S(1)} %get-tuple-element.77), channel_id=1, source_target_pairs={{0,64},{1,65},{2,66},{3,67},{4,68},{5,69},{6,70},{7,71},{8,72},{9,... | collective-permute-start | bytes 36872 | tf_op jit(solution)/shard_map/ppermute | solution.py:684
  263.7 6.0 %collective-permute-start.19 = (f32[8,384]{1,0:T(8,128)S(1)}, f32[8,384]{1,0:T(8,128)S(1)}, u32[]{:S(2)}, u32[]{:S(2)}) collective-permute-start(f32[8,384]{1,0:T(8,128)S(1)} %get-tuple-element.78), channel_id=1, source_target_pairs={{0,96},{1,97},{2,98},{3,99},{4,100},{5,101},{6,102},{7,103},{8,104... | collective-permute-start | bytes 36872 | tf_op jit(solution)/shard_map/ppermute | solution.py:684
  (42 other events, 207.7 us)
Sparse Core Ops, SparseCore 0:
  81.2 28.2 reduce-scatter.4
  138.5 28.2 reduce-scatter.2

commit v3 on v2

--- a/solution.py
+++ b/solution.py
@@ -441,9 +441,9 @@
         places[name] = {e ^ by: i for i, e in enumerate(give)}
         return piece, places
 
-    def ring_y(self, y):
+    def ring_y(self, y, after=()):
         (keep, _, _), (got, _, _) = self.terms
-        total = ordered_sum(keep, got, y)
+        total = ordered_sum(keep, got, y, after)
         rest = total.reshape(4 * 128, self.tail[1])
         rest = lax.psum_scatter(rest, "lon", scatter_dimension=0, axis_index_groups=Y_RINGS, tiled=True)
         self.reduced = rest
@@ -477,11 +477,12 @@
     return out, got
 
 
-def add_kernel(y_ref, a_ref, b_ref, out_ref):
+def add_kernel(y_ref, a_ref, b_ref, *refs):
+    out_ref = refs[-1]
     out_ref[...] = a_ref[...] + b_ref[...]
 
 
-def ordered_sum(a, b, y):
+def ordered_sum(a, b, y, after):
     a, b = (t.reshape(4, 128, t.shape[-1]) for t in (a, b))
     block = (1,) + a.shape[1:]
     return pl.pallas_call(
@@ -489,14 +490,14 @@
         grid_spec=pltpu.PrefetchScalarGridSpec(
             num_scalar_prefetch=1,
             grid=(4,),
-            in_specs=[pl.BlockSpec(block, lambda i, y: (i ^ y[0], 0, 0))] * 2,
+            in_specs=[pl.BlockSpec(block, lambda i, y: (i ^ y[0], 0, 0))] * 2 + waits(after),
             out_specs=pl.BlockSpec(block, lambda i, y: (i, 0, 0)),
         ),
         out_shape=jax.ShapeDtypeStruct(a.shape, F32),
         compiler_params=params(16),
         cost_estimate=cost(0, 5e6),
         name="ordered_sum",
-    )(y, a, b)
+    )(y, a, b, *after)
 
 
 def last_cut_kernel(counts, *refs):
@@ -653,31 +654,30 @@
     s1 = heads(1, ())
     total = s0.ring_y(y_index)
     s2 = heads(2, (total,))
-    total = s1.ring_y(y_index)
-    s3 = heads(3, (total,))
-    out2, _ = exchange([s2], "z", 1)
-    norm_grad = product(grads, qkv_weight, (out2,))
+    total = s1.ring_y(y_index, (att[2],))
+    s3 = heads(3, (total, s0.reduced))
+    total = s2.ring_y(y_index, (att[3],))
+    norm_grad = product(grads, qkv_weight, (total,))
     s3, s4 = s3.columns(0, 2 * GW), s3.columns(2 * GW, 4 * GW)
     out3, _ = exchange([s3], "z", 1)
     out4, _ = exchange([s4], "z", 3)
-    leaving = leave(norm_grad, x, up, gain, gain_mix(), (out3, out4))
+    leaving = leave(norm_grad, x, up, gain, gain_mix(), (out3, out4, s1.reduced))
     back = lax.all_to_all(leaving, "lon", split_axis=0, concat_axis=0, tiled=True)
     def hand(sums, arrays):
         for t, p in zip(sums, arrays):
             t.terms[-1] = (p,) + t.terms[-1][1:]
 
-    waiting = (s2, s3, s4)
+    waiting = (s3, s4)
     block, *passed = block_sum(att, x, out_weight, [newest(t) for t in waiting], (leaving,))
     hand(waiting, passed)
-    exchange([s2], "z", 3)
     exchange([s3], "z", 3)
     exchange([s4], "z", 1)
-    exchange([s2, s3, s4], "y", 1)
-    exchange([s0, s1], "z", 1)
-    joined, gain_sum, one, two = join_pieces(back, (newest(s2), newest(s0)), (block,))
-    hand((s2, s3, s4, s0, s1), (one, one, one, two, two))
-    exchange([s2, s3, s4], "y", 3)
-    exchange([s0, s1], "z", 3)
+    exchange([s3, s4], "y", 1)
+    exchange([s0, s1, s2], "z", 1)
+    joined, gain_sum, one, two = join_pieces(back, (newest(s3), newest(s0)), (block,))
+    hand((s3, s4, s0, s1, s2), (one, one, two, two, two))
+    exchange([s3, s4], "y", 3)
+    exchange([s0, s1, s2], "z", 3)
     own, *send = last_cut((s0, s1, s2, s3, s4), gain_sum)
     got = [lax.ppermute(a, AXES, swapped(x=d)) for d, a in zip((1, 2, 3), send)]
     qkv_weight_grad, own, *send = quarters_of(own, got, gain_sum, z_index)

time: 279 us -> 268 us (0.961)
  waiting for transfers between devices: 71.2 us -> 45.6 us
  local copies, waits for them, and re-layouts: 42.5 us -> 58.8 us
  other arithmetic: 19.2 us -> 13.2 us
  Pallas kernels: 91.8 us -> 96.8 us
    unnamed x98 -> x120, local copies, waits for them, and re-layouts: 21.9 us -> 38.6 us
    ppermute x10 -> x8, waiting for transfers between devices: 36.3 us -> 20.4 us  [exchange(): got = lax.ppermute(out, AXES, swapped(**{name: by}))]
    all_to_all x1, waiting for transfers between devices: 8.13 us -> 0.01 us  [per_device(): lax.all_to_all(leaving, 'lon', split_axis=0, concat_axis=0, tiled=True)]
    add x6 -> x3, other arithmetic: 10.6 us -> 4.83 us  [cut(): total = piece if total is None else total + piece]
    pallas_call x2 -> x3, Pallas kernels: 0.67 us -> 4.89 us  [ordered_sum(): pl.pallas_call(add_kernel, grid_spec=pltpu.PrefetchScalarGridSpec(num_sca...]
    ppermute x10 -> x8, starting transfers between devices: 16.1 us -> 14.6 us  [exchange(): got = lax.ppermute(out, AXES, swapped(**{name: by}))]
  transfers between devices with their start and end apart: 24 -> 23, of which waited for: 11 -> 10; matrix products, arithmetic and copies ran while one was open for 13% -> 12% of each run, Pallas kernels for 21% -> 24%
where the time goes in v3:
time: 268 us; the launch traced here: 266 us
  Pallas kernels  96.8 us (36%)
  local copies, waits for them, and re-layouts  58.8 us (22%)
  waiting for transfers between devices  45.6 us (17%)
  starting transfers between devices  37.6 us (14%)
  between operations  14.2 us (5%)
  other arithmetic  13.2 us (5%)
    pallas_call x4, Pallas kernels, attend(): pl.pallas_call(behind(attend_kernel, len(after), 10), grid=(1,), out_shap...  56.9 us
    unnamed x120, local copies, waits for them, and re-layouts  38.6 us
    ppermute x8, waiting for transfers between devices, exchange(): got = lax.ppermute(out, AXES, swapped(**{name: by}))  20.4 us
    ppermute x8, starting transfers between devices, exchange(): got = lax.ppermute(out, AXES, swapped(**{name: by}))  14.6 us
    all_to_all x1, waiting for transfers between devices, per_device(): lax.all_to_all(pieces, 'lon', split_axis=0, concat_axis=0, tiled=True)  10.8 us
    pallas_call x1, Pallas kernels, product(): pl.pallas_call(behind(product_kernel, len(after), 5), out_shape=jax.Shape...  8.8 us
    ppermute x4, waiting for transfers between devices, heads(): return Sum(keep, lax.ppermute(send, AXES, swapped(core=1)))  8.35 us
    pallas_call x1, Pallas kernels, enter(): pl.pallas_call(enter_kernel, out_shape=(jax.ShapeDtypeStruct((TOK, D), BF...  7.29 us
  transfers between devices with their start and end apart: 23, of which 10 were waited for; matrix products, arithmetic and copies ran while one was open for 12% of the time, Pallas kernels for 24%

profile of v3, /device:TPU:0, one launch (start us, length us, event | category | flops | bytes accessed | tf_op | source)
XLA Modules:
  0.0 266.3 jit_solution(16867152131068210300)
XLA Ops:
  8.7 4.2 %split_pieces.1 = bf16[16,432,128]{2,1,0:T(8,128)(2,1)} custom-call(bf16[2,12,64,576]{3,2,1,0:T(8,128)(2,1)S(1)} %bitcast.123), custom_call_target="tpu_custom_call" | custom-call | flops 200000000 | bytes 400000 | tf_op jit(solution)/shard_map/split_pieces/pallas_call | solution.py:79
  12.9 7.2 %all-to-all-start = ((bf16[16,432,128]{2,1,0:T(8,128)(2,1)}), bf16[16,432,128]{2,1,0:T(8,128)(2,1)S(1)}, u32[]{:S(2)}, u32[]{:S(2)}) async-start(bf16[16,432,128]{2,1,0:T(8,128)(2,1)} %split_pieces.1), calls=%async_computation | async-start | bytes 3538944 | tf_op jit(solution)/shard_map/all_to_all | solution.py:630
  29.9 2.5 reshape.419.refs_2_
  35.1 10.8 %all-to-all-done.r_ref = bf16[16,432,128]{2,1,0:T(8,128)(2,1)S(1)} async-done(((bf16[16,432,128]{2,1,0:T(8,128)(2,1)}), bf16[16,432,128]{2,1,0:T(8,128)(2,1)S(1)}, u32[]{:S(2)}, u32[]{:S(2)}) %all-to-all-start) | async-done | bytes 1769504 | tf_op jit(solution)/shard_map/all_to_all | solution.py:630
  50.3 7.3 %enter.1 = (bf16[864,1024]{1,0:T(8,128)(2,1)S(1)}, bf16[864,1024]{1,0:T(8,128)(2,1)S(1)}, bf16[1024,864]{1,0:T(8,128)(2,1)S(1)}) custom-call(bf16[16,432,128]{2,1,0:T(8,128)(2,1)S(1)} %copy-done.20, f32[1,1024]{1,0:T(1,128)S(1)} %bitcast.129, bf16[1024,1024]{1,0:T(8,128)(2,1)S(1)} %copy-done.17), custom_call_target="tpu_custom_call" | custom-call | flops 300000000 | bytes 900000 | tf_op jit(solution)/shard_map/enter/pallas_call | solution.py:129
  58.8 14.5 %attend.4 = (bf16[864,256]{1,0:T(8,128)(2,1)S(1)}, bf16[864,768]{1,0:T(8,128)(2,1)S(1)}, f32[512,1024]{1,0:T(8,128)}, f32[512,1024]{1,0:T(8,128)}) custom-call(bf16[864,1024]{1,0:T(8,128)(2,1)S(1)} %get-tuple-element.42.refs_0_, bf16[1024,864]{1,0:T(8,128)(2,1)} %copy-done.3, bf16[864,1024]{1,0:T(8,128)(2,1)S(1)} %reshape.419.refs_2_, ...), custom_call_target="tpu_custom_call" | custom-call | flops 800000000 | bytes 1500000 | tf_op jit(solution)/shard_map/attend/pallas_call | solution.py:213
  73.4 4.4 %collective-permute-done = f32[512,1024]{1,0:T(8,128)S(1)} collective-permute-done((f32[512,1024]{1,0:T(8,128)}, f32[512,1024]{1,0:T(8,128)S(1)}, u32[]{:S(2)}, u32[]{:S(2)}) %collective-permute-start) | collective-permute-done | bytes 2097184 | tf_op jit(solution)/shard_map/ppermute | solution.py:648
  83.2 13.9 %attend.5 = (bf16[864,256]{1,0:T(8,128)(2,1)S(1)}, bf16[864,768]{1,0:T(8,128)(2,1)S(1)}, f32[512,1024]{1,0:T(8,128)}, f32[512,1024]{1,0:T(8,128)}) custom-call(bf16[864,1024]{1,0:T(8,128)(2,1)S(1)} %get-tuple-element.42.refs_0_, bf16[1024,864]{1,0:T(8,128)(2,1)} %copy-done.3, bf16[864,1024]{1,0:T(8,128)(2,1)S(1)} %reshape.419.refs_2_, ...), custom_call_target="tpu_custom_call" | custom-call | flops 800000000 | bytes 1500000 | tf_op jit(solution)/shard_map/attend/pallas_call | solution.py:213
  99.1 14.1 %attend.6 = (bf16[864,256]{1,0:T(8,128)(2,1)S(1)}, bf16[864,768]{1,0:T(8,128)(2,1)S(1)}, f32[512,1024]{1,0:T(8,128)}, f32[512,1024]{1,0:T(8,128)}) custom-call(bf16[864,1024]{1,0:T(8,128)(2,1)S(1)} %get-tuple-element.42.refs_0_, bf16[1024,864]{1,0:T(8,128)(2,1)} %copy-done.3, bf16[864,1024]{1,0:T(8,128)(2,1)S(1)} %reshape.419.refs_2_, ...), custom_call_target="tpu_custom_call" | custom-call | flops 800000000 | bytes 1500000 | tf_op jit(solution)/shard_map/attend/pallas_call | solution.py:213
  117.9 14.5 %attend.7 = (bf16[864,256]{1,0:T(8,128)(2,1)S(1)}, bf16[864,768]{1,0:T(8,128)(2,1)S(1)}, f32[512,1024]{1,0:T(8,128)}, f32[512,1024]{1,0:T(8,128)}) custom-call(bf16[864,1024]{1,0:T(8,128)(2,1)S(1)} %get-tuple-element.42.refs_0_, bf16[1024,864]{1,0:T(8,128)(2,1)} %copy-done.3, bf16[864,1024]{1,0:T(8,128)(2,1)} %copy-done, bf16[1024,3072]{1,0:T(8,128)(2,1)} %refs_4_.9, ...), custom_call_target="tpu_custom_call" | custom-call | flops 800000000 | bytes 1500000 | tf_op jit(solution)/shard_map/attend/pallas_call | solution.py:213
  132.4 4.3 %ordered_sum.5.refs_5_ = f32[4,128,1024]{2,1,0:T(8,128)} custom-call(s32[1]{0:T(128)} %bitcast.6.y_ref, f32[4,128,1024]{2,1,0:T(8,128)S(1)} %bitcast.120, f32[4,128,1024]{2,1,0:T(8,128)} %bitcast.19.b_ref, bf16[864,256]{1,0:T(8,128)(2,1)S(1)} %get-tuple-element.51.refs_0_.refs_3_), custom_call_target="tpu_custom_call" | custom-call | bytes 500000 | tf_op jit(solution)/shard_map/ordered_sum/pallas_call | solution.py:488
  137.3 4.0 %collective-permute-done.2 = f32[512,1024]{1,0:T(8,128)S(1)} collective-permute-done((f32[512,1024]{1,0:T(8,128)}, f32[512,1024]{1,0:T(8,128)S(1)}, u32[]{:S(2)}, u32[]{:S(2)}) %collective-permute-start.2) | collective-permute-done | bytes 2097184 | tf_op jit(solution)/shard_map/ppermute | solution.py:648
  144.9 2.5 collective-permute-start.4
  147.4 2.2 fusion.1.refs_4_
  150.9 8.8 %product.1.refs_0_ = f32[864,1024]{1,0:T(8,128)S(1)} custom-call(bf16[864,768]{1,0:T(8,128)(2,1)S(1)} %copy-done.46, bf16[864,768]{1,0:T(8,128)(2,1)S(1)} %copy-done.48, bf16[864,768]{1,0:T(8,128)(2,1)S(1)} %copy-done.50, bf16[864,768]{1,0:T(8,128)(2,1)S(1)} %copy-done.52, bf16[1024,3072]{1,0:T(8,128)(2,1)} %refs_4_.9, f32[4,128,1024]{2,1,0:T(8,128)} %ordered_sum.5.refs_5_), custom_call_target="tpu_custom_call" | custom-call | flops 600000000 | bytes 1500000 | tf_op jit(solution)/shard_map/product/pallas_call | solution.py:291
  161.5 2.1 copy-done.13
  166.2 6.2 %leave.1.refs_8_ = bf16[16,448,128]{2,1,0:T(8,128)(2,1)S(1)} custom-call(f32[864,1024]{1,0:T(8,128)S(1)} %copy-done.13, bf16[864,1024]{1,0:T(8,128)(2,1)S(1)} %copy-done.24, bf16[864,1024]{1,0:T(8,128)(2,1)S(1)} %copy-done.1, f32[1,1024]{1,0:T(1,128)S(1)} %bitcast.130, bf16[1024,1024]{1,0:T(8,128)(2,1)S(1)} %copy-done.18, f32[32,8,512]{2,1,0:T(8,128)} %bitcast.14.refs_5_, ...), custom_call_target="tpu_custom_call" | custom-call | flops 400000000 | bytes 1000000 | tf_op jit(solution)/shard_map/leave/pallas_call | solution.py:336
  173.7 4.7 %all-to-all-start.1 = ((bf16[16,448,128]{2,1,0:T(8,128)(2,1)}), bf16[16,448,128]{2,1,0:T(8,128)(2,1)}, u32[]{:S(2)}, u32[]{:S(2)}) async-start(bf16[16,448,128]{2,1,0:T(8,128)(2,1)} %copy-done.10), calls=%async_computation.3 | async-start | bytes 3670016 | tf_op jit(solution)/shard_map/all_to_all | solution.py:665
  186.2 2.2 block_sum.1
  189.6 2.5 fusion.3
  196.6 5.3 %collective-permute-done.6 = f32[16,8,512]{2,1,0:T(8,128)} collective-permute-done((f32[16,8,512]{2,1,0:T(8,128)}, f32[16,8,512]{2,1,0:T(8,128)}, u32[]{:S(2)}, u32[]{:S(2)}) %collective-permute-start.6) | collective-permute-done | bytes 262176 | tf_op jit(solution)/shard_map/ppermute | solution.py:471
  206.8 5.9 %collective-permute-done.8 = f32[8,8,1024]{2,1,0:T(8,128)S(1)} collective-permute-done((f32[8,8,1024]{2,1,0:T(8,128)S(1)}, f32[8,8,1024]{2,1,0:T(8,128)S(1)}, u32[]{:S(2)}, u32[]{:S(2)}) %collective-permute-start.8) | collective-permute-done | bytes 262176 | tf_op jit(solution)/shard_map/ppermute | solution.py:471
  213.5 4.4 %collective-permute-done.9 = f32[8,8,3072]{2,1,0:T(8,128)S(1)} collective-permute-done((f32[8,8,3072]{2,1,0:T(8,128)}, f32[8,8,3072]{2,1,0:T(8,128)S(1)}, u32[]{:S(2)}, u32[]{:S(2)}) %collective-permute-start.9) | collective-permute-done | bytes 786464 | tf_op jit(solution)/shard_map/ppermute | solution.py:471
  220.3 4.0 %join_pieces.1 = (bf16[2,12,64,576]{3,2,1,0:T(8,128)(2,1)}, f32[1,128]{1,0:T(1,128)S(1)}, f32[2,1,4,8,1024]{4,3,2,1,0:T(8,128)S(1)}, f32[1,2,4,8,3072]{4,3,2,1,0:T(8,128)S(1)}) custom-call(bf16[16,448,128]{2,1,0:T(8,128)(2,1)} %all-to-all-done.1.refs_0_, f32[2,1,4,8,1024]{4,3,2,1,0:T(8,128)S(1)} %bitcast.115, ...), custom_call_target="tpu_custom_call", output_to_operand_aliasing={{2}: (1, {}), {3}: (2, {})} | custom-call | flops 200000000 | bytes 400000 | tf_op jit(solution)/shard_map/join_pieces/pallas_call | solution.py:375
  224.5 2.7 collective-permute-start.10
  228.1 3.0 %collective-permute-start.11 = (f32[4,8,1024]{2,1,0:T(8,128)S(1)}, f32[4,8,1024]{2,1,0:T(8,128)S(1)}, u32[]{:S(2)}, u32[]{:S(2)}) collective-permute-start(f32[4,8,1024]{2,1,0:T(8,128)S(1)} %pad_maximum_fusion.3), channel_id=1, source_target_pairs={{0,12},{1,13},{2,14},{3,15},{4,8},{5,9},{6,10},{7,11},{8,4},{9,5},... | collective-permute-start | bytes 393224 | tf_op jit(solution)/shard_map/ppermute | solution.py:471
  231.1 3.2 %collective-permute-done.11 = f32[4,8,1024]{2,1,0:T(8,128)S(1)} collective-permute-done((f32[4,8,1024]{2,1,0:T(8,128)S(1)}, f32[4,8,1024]{2,1,0:T(8,128)S(1)}, u32[]{:S(2)}, u32[]{:S(2)}) %collective-permute-start.11) | collective-permute-done | bytes 131104 | tf_op jit(solution)/shard_map/ppermute | solution.py:471
  237.8 3.7 %collective-permute-start.13 = (f32[8,4096]{1,0:T(8,128)S(1)}, f32[8,4096]{1,0:T(8,128)S(1)}, u32[]{:S(2)}, u32[]{:S(2)}) collective-permute-start(f32[8,4096]{1,0:T(8,128)S(1)} %get-tuple-element.70), channel_id=1, source_target_pairs={{0,2},{1,3},{2,0},{3,1},{4,6},{5,7},{6,4},{7,5},{8,10},{9,11},{10,... | collective-permute-start | bytes 393224 | tf_op jit(solution)/shard_map/ppermute | solution.py:682
  241.7 4.2 %collective-permute-done.13.got2 = f32[8,4096]{1,0:T(8,128)S(1)} collective-permute-done((f32[8,4096]{1,0:T(8,128)S(1)}, f32[8,4096]{1,0:T(8,128)S(1)}, u32[]{:S(2)}, u32[]{:S(2)}) %collective-permute-start.13) | collective-permute-done | bytes 131104 | tf_op jit(solution)/shard_map/ppermute | solution.py:682
  248.3 4.0 %collective-permute-start.16 = (f32[8,384]{1,0:T(8,128)S(1)}, f32[8,384]{1,0:T(8,128)S(1)}, u32[]{:S(2)}, u32[]{:S(2)}) collective-permute-start(f32[8,384]{1,0:T(8,128)S(1)} %get-tuple-element.75), channel_id=1, source_target_pairs={{0,64},{1,65},{2,66},{3,67},{4,68},{5,69},{6,70},{7,71},{8,72},{9,... | collective-permute-start | bytes 36872 | tf_op jit(solution)/shard_map/ppermute | solution.py:684
  253.0 2.4 reshape.430
  255.5 3.1 %copy.34 = bf16[2,2,6,3,12,1024]{5,0,4,3,2,1:T(2,128)(2,1)} copy(bf16[2,2,6,3,12,1024]{5,4,2,0,3,1:T(8,128)(2,1)S(1)} %bitcast.131) | data formatting | bytes 3538944 | tf_op jit(solution)/shard_map/transpose | solution.py:688
  (185 shorter events, 73.5 us)
Async XLA Ops:
  12.9 15.0 %copy-start.58 = (bf16[2,12,36,1024]{3,0,2,1:T(2,128)(2,1)S(1)}, bf16[2,12,36,1024]{3,0,2,1:T(2,128)(2,1)}, u32[]{:S(2)}) copy-start(bf16[2,12,36,1024]{3,0,2,1:T(2,128)(2,1)} %param.11) | copy-start | bytes 5308420
  12.9 33.0 %all-to-all-start = ((bf16[16,432,128]{2,1,0:T(8,128)(2,1)}), bf16[16,432,128]{2,1,0:T(8,128)(2,1)S(1)}, u32[]{:S(2)}, u32[]{:S(2)}) async-start(bf16[16,432,128]{2,1,0:T(8,128)(2,1)} %split_pieces.1), calls=%async_computation | async-start | bytes 3538944 | tf_op jit(solution)/shard_map/all_to_all | solution.py:630
  20.2 96.3 %reduce-scatter.4.cloned.1.call-start = ((), (), s32[]{:S(2)}) async-start(), calls=%async_computation.5 | async-start | bytes 2621440 | tf_op jit(solution)/shard_map/reduce_scatter | solution.py:448
  32.4 66.7 %copy-start = (bf16[864,1024]{1,0:T(8,128)(2,1)}, bf16[864,1024]{1,0:T(8,128)(2,1)S(1)}, u32[]{:S(2)}) copy-start(bf16[864,1024]{1,0:T(8,128)(2,1)S(1)} %reshape.419.refs_2_) | copy-start | bytes 5308420
  32.4 14.8 %copy-start.57 = (f32[1024]{0:T(1024)S(1)}, f32[1024]{0:T(1024)}, u32[]{:S(2)}) copy-start(f32[1024]{0:T(1024)} %param.8) | copy-start | bytes 12292
  47.2 11.7 %copy-start.14 = (f32[864,1]{1,0:T(8,128)S(1)}, f32[864,1]{1,0:T(8,128)}, u32[]{:S(2)}) copy-start(f32[864,1]{1,0:T(8,128)} %select_n.250.refs_7_) | copy-start | bytes 10372
  58.8 14.5 %copy-start.23 = (bf16[864,1024]{1,0:T(8,128)(2,1)}, bf16[864,1024]{1,0:T(8,128)(2,1)S(1)}, u32[]{:S(2)}) copy-start(bf16[864,1024]{1,0:T(8,128)(2,1)S(1)} %get-tuple-element.52.refs_1_.refs_4_) | copy-start | bytes 5308420
  73.3 4.5 %collective-permute-start = (f32[512,1024]{1,0:T(8,128)}, f32[512,1024]{1,0:T(8,128)S(1)}, u32[]{:S(2)}, u32[]{:S(2)}) collective-permute-start(f32[512,1024]{1,0:T(8,128)} %get-tuple-element.47), channel_id=1, source_target_pairs={{0,1},{1,0},{2,3},{3,2},{4,5},{5,4},{6,7},{7,6},{8,9},{9,8},{10,11... | collective-permute-start | bytes 6291464 | tf_op jit(solution)/shard_map/ppermute | solution.py:648
  81.0 80.5 %reduce-scatter.6.cloned.1.call-start = ((), (), s32[]{:S(2)}) async-start(), calls=%async_computation.6 | async-start | bytes 2621440 | tf_op jit(solution)/shard_map/reduce_scatter | solution.py:448
  99.0 14.2 %copy-start.38 = (f32[512,1024]{1,0:T(8,128)S(1)}, f32[512,1024]{1,0:T(8,128)}, u32[]{:S(2)}) copy-start(f32[512,1024]{1,0:T(8,128)} %get-tuple-element.49) | copy-start | bytes 6291460
  99.0 14.2 %collective-permute-start.1 = (f32[512,1024]{1,0:T(8,128)}, f32[512,1024]{1,0:T(8,128)S(1)}, u32[]{:S(2)}, u32[]{:S(2)}) collective-permute-start(f32[512,1024]{1,0:T(8,128)} %get-tuple-element.50), channel_id=1, source_target_pairs={{0,1},{1,0},{2,3},{3,2},{4,5},{5,4},{6,7},{7,6},{8,9},{9,8},{10,11... | collective-permute-start | bytes 6291464 | tf_op jit(solution)/shard_map/ppermute | solution.py:648
  115.9 77.2 %reduce-scatter.8.cloned.1.call-start = ((), (), s32[]{:S(2)}) async-start(), calls=%async_computation.7 | async-start | bytes 2621440 | tf_op jit(solution)/shard_map/reduce_scatter | solution.py:448
  115.9 16.5 %collective-permute-start.5 = (f32[512,1024]{1,0:T(8,128)}, f32[512,1024]{1,0:T(8,128)}, u32[]{:S(2)}, u32[]{:S(2)}) collective-permute-start(f32[512,1024]{1,0:T(8,128)} %get-tuple-element.60), channel_id=1, source_target_pairs={{0,1},{1,0},{2,3},{3,2},{4,5},{5,4},{6,7},{7,6},{8,9},{9,8},{10,11... | collective-permute-start | bytes 6291464 | tf_op jit(solution)/shard_map/ppermute | solution.py:648
  117.9 14.5 %copy-start.37 = (f32[512,1024]{1,0:T(8,128)S(1)}, f32[512,1024]{1,0:T(8,128)}, u32[]{:S(2)}) copy-start(f32[512,1024]{1,0:T(8,128)} %get-tuple-element.59) | copy-start | bytes 6291460
  136.7 4.6 %collective-permute-start.2 = (f32[512,1024]{1,0:T(8,128)}, f32[512,1024]{1,0:T(8,128)S(1)}, u32[]{:S(2)}, u32[]{:S(2)}) collective-permute-start(f32[512,1024]{1,0:T(8,128)} %get-tuple-element.54), channel_id=1, source_target_pairs={{0,1},{1,0},{2,3},{3,2},{4,5},{5,4},{6,7},{7,6},{8,9},{9,8},{10,11... | collective-permute-start | bytes 6291464 | tf_op jit(solution)/shard_map/ppermute | solution.py:648
  143.0 36.2 %collective-permute-start.3 = (f32[32,8,512]{2,1,0:T(8,128)}, f32[32,8,512]{2,1,0:T(8,128)}, u32[]{:S(2)}, u32[]{:S(2)}) collective-permute-start(f32[32,8,512]{2,1,0:T(8,128)} %bitcast.14.refs_5_), channel_id=1, source_target_pairs={{0,32},{1,33},{2,34},{3,35},{4,36},{5,37},{6,38},{7,39},{8,40},{9,... | collective-permute-start | bytes 1572872 | tf_op jit(solution)/shard_map/ppermute | solution.py:471
  144.9 34.2 %collective-permute-start.4 = (f32[32,8,512]{2,1,0:T(8,128)}, f32[32,8,512]{2,1,0:T(8,128)}, u32[]{:S(2)}, u32[]{:S(2)}) collective-permute-start(f32[32,8,512]{2,1,0:T(8,128)} %bitcast.16.refs_6_), channel_id=1, source_target_pairs={{0,96},{1,97},{2,98},{3,99},{4,100},{5,101},{6,102},{7,103},{8,104... | collective-permute-start | bytes 1572872 | tf_op jit(solution)/shard_map/ppermute | solution.py:471
  150.9 10.6 %copy-start.24 = (bf16[864,1024]{1,0:T(8,128)(2,1)S(1)}, bf16[864,1024]{1,0:T(8,128)(2,1)}, u32[]{:S(2)}) copy-start(bf16[864,1024]{1,0:T(8,128)(2,1)} %copy-done.23) | copy-start | bytes 5308420
  173.7 39.8 %all-to-all-start.1 = ((bf16[16,448,128]{2,1,0:T(8,128)(2,1)}), bf16[16,448,128]{2,1,0:T(8,128)(2,1)}, u32[]{:S(2)}, u32[]{:S(2)}) async-start(bf16[16,448,128]{2,1,0:T(8,128)(2,1)} %copy-done.10), calls=%async_computation.3 | async-start | bytes 3670016 | tf_op jit(solution)/shard_map/all_to_all | solution.py:665
  189.6 14.3 %copy-start.7 = (f32[512,1024]{1,0:T(8,128)S(1)}, f32[512,1024]{1,0:T(8,128)}, u32[]{:S(2)}) copy-start(f32[512,1024]{1,0:T(8,128)} %get-tuple-element.53) | copy-start | bytes 6291460
  192.0 10.0 %collective-permute-start.6 = (f32[16,8,512]{2,1,0:T(8,128)}, f32[16,8,512]{2,1,0:T(8,128)}, u32[]{:S(2)}, u32[]{:S(2)}) collective-permute-start(f32[16,8,512]{2,1,0:T(8,128)} %bitcast.23), channel_id=1, source_target_pairs={{0,96},{1,97},{2,98},{3,99},{4,100},{5,101},{6,102},{7,103},{8,104... | collective-permute-start | bytes 786440 | tf_op jit(solution)/shard_map/ppermute | solution.py:471
  192.7 10.2 %collective-permute-start.7 = (f32[16,8,512]{2,1,0:T(8,128)}, f32[16,8,512]{2,1,0:T(8,128)}, u32[]{:S(2)}, u32[]{:S(2)}) collective-permute-start(f32[16,8,512]{2,1,0:T(8,128)} %bitcast.27), channel_id=1, source_target_pairs={{0,32},{1,33},{2,34},{3,35},{4,36},{5,37},{6,38},{7,39},{8,40},{9,... | collective-permute-start | bytes 786440 | tf_op jit(solution)/shard_map/ppermute | solution.py:471
  195.0 22.9 %collective-permute-start.9 = (f32[8,8,3072]{2,1,0:T(8,128)}, f32[8,8,3072]{2,1,0:T(8,128)S(1)}, u32[]{:S(2)}, u32[]{:S(2)}) collective-permute-start(f32[8,8,3072]{2,1,0:T(8,128)} %pad_maximum_fusion), channel_id=1, source_target_pairs={{0,32},{1,33},{2,34},{3,35},{4,36},{5,37},{6,38},{7,39},{8,40},{9,... | collective-permute-start | bytes 2359304 | tf_op jit(solution)/shard_map/ppermute | solution.py:471
  205.1 7.7 %collective-permute-start.8 = (f32[8,8,1024]{2,1,0:T(8,128)S(1)}, f32[8,8,1024]{2,1,0:T(8,128)S(1)}, u32[]{:S(2)}, u32[]{:S(2)}) collective-permute-start(f32[8,8,1024]{2,1,0:T(8,128)S(1)} %pad_maximum_fusion.2), channel_id=1, source_target_pairs={{0,4},{1,5},{2,6},{3,7},{4,0},{5,1},{6,2},{7,3},{8,12},{9,13},{10,... | collective-permute-start | bytes 786440 | tf_op jit(solution)/shard_map/ppermute | solution.py:471
  224.5 11.4 %collective-permute-start.10 = (f32[4,8,3072]{2,1,0:T(8,128)S(1)}, f32[4,8,3072]{2,1,0:T(8,128)S(1)}, u32[]{:S(2)}, u32[]{:S(2)}) collective-permute-start(f32[4,8,3072]{2,1,0:T(8,128)S(1)} %pad_maximum_fusion.1), channel_id=1, source_target_pairs={{0,96},{1,97},{2,98},{3,99},{4,100},{5,101},{6,102},{7,103},{8,104... | collective-permute-start | bytes 1179656 | tf_op jit(solution)/shard_map/ppermute | solution.py:471
  228.1 6.3 %collective-permute-start.11 = (f32[4,8,1024]{2,1,0:T(8,128)S(1)}, f32[4,8,1024]{2,1,0:T(8,128)S(1)}, u32[]{:S(2)}, u32[]{:S(2)}) collective-permute-start(f32[4,8,1024]{2,1,0:T(8,128)S(1)} %pad_maximum_fusion.3), channel_id=1, source_target_pairs={{0,12},{1,13},{2,14},{3,15},{4,8},{5,9},{6,10},{7,11},{8,4},{9,5},... | collective-permute-start | bytes 393224 | tf_op jit(solution)/shard_map/ppermute | solution.py:471
  236.9 10.8 %collective-permute-start.12 = (f32[8,4224]{1,0:T(8,128)S(1)}, f32[8,4224]{1,0:T(8,128)S(1)}, u32[]{:S(2)}, u32[]{:S(2)}) collective-permute-start(f32[8,4224]{1,0:T(8,128)S(1)} %get-tuple-element.69), channel_id=1, source_target_pairs={{0,16},{1,17},{2,18},{3,19},{4,20},{5,21},{6,22},{7,23},{8,24},{9,... | collective-permute-start | bytes 405512 | tf_op jit(solution)/shard_map/ppermute | solution.py:682
  237.8 8.1 %collective-permute-start.13 = (f32[8,4096]{1,0:T(8,128)S(1)}, f32[8,4096]{1,0:T(8,128)S(1)}, u32[]{:S(2)}, u32[]{:S(2)}) collective-permute-start(f32[8,4096]{1,0:T(8,128)S(1)} %get-tuple-element.70), channel_id=1, source_target_pairs={{0,2},{1,3},{2,0},{3,1},{4,6},{5,7},{6,4},{7,5},{8,10},{9,11},{10,... | collective-permute-start | bytes 393224 | tf_op jit(solution)/shard_map/ppermute | solution.py:682
  241.5 6.2 %collective-permute-start.14 = (f32[8,4096]{1,0:T(8,128)S(1)}, f32[8,4096]{1,0:T(8,128)S(1)}, u32[]{:S(2)}, u32[]{:S(2)}) collective-permute-start(f32[8,4096]{1,0:T(8,128)S(1)} %get-tuple-element.71), channel_id=1, source_target_pairs={{0,18},{1,19},{2,16},{3,17},{4,22},{5,23},{6,20},{7,21},{8,26},{9,... | collective-permute-start | bytes 393224 | tf_op jit(solution)/shard_map/ppermute | solution.py:682
  248.3 10.2 %collective-permute-start.15 = (f32[8,384]{1,0:T(8,128)S(1)}, f32[8,384]{1,0:T(8,128)S(1)}, u32[]{:S(2)}, u32[]{:S(2)}) collective-permute-start(f32[8,384]{1,0:T(8,128)S(1)} %get-tuple-element.74), channel_id=1, source_target_pairs={{0,32},{1,33},{2,34},{3,35},{4,36},{5,37},{6,38},{7,39},{8,40},{9,... | collective-permute-start | bytes 36872 | tf_op jit(solution)/shard_map/ppermute | solution.py:684
  248.3 10.2 %collective-permute-start.16 = (f32[8,384]{1,0:T(8,128)S(1)}, f32[8,384]{1,0:T(8,128)S(1)}, u32[]{:S(2)}, u32[]{:S(2)}) collective-permute-start(f32[8,384]{1,0:T(8,128)S(1)} %get-tuple-element.75), channel_id=1, source_target_pairs={{0,64},{1,65},{2,66},{3,67},{4,68},{5,69},{6,70},{7,71},{8,72},{9,... | collective-permute-start | bytes 36872 | tf_op jit(solution)/shard_map/ppermute | solution.py:684
  252.3 6.2 %collective-permute-start.17 = (f32[8,384]{1,0:T(8,128)S(1)}, f32[8,384]{1,0:T(8,128)S(1)}, u32[]{:S(2)}, u32[]{:S(2)}) collective-permute-start(f32[8,384]{1,0:T(8,128)S(1)} %get-tuple-element.76), channel_id=1, source_target_pairs={{0,96},{1,97},{2,98},{3,99},{4,100},{5,101},{6,102},{7,103},{8,104... | collective-permute-start | bytes 36872 | tf_op jit(solution)/shard_map/ppermute | solution.py:684
  (52 other events, 155.7 us)
Sparse Core Ops, SparseCore 0:
  81.2 28.2 reduce-scatter.3
  116.0 28.3 reduce-scatter.5
  146.8 29.3 reduce-scatter.7

commit v4 on v3

--- a/solution.py
+++ b/solution.py
@@ -245,6 +245,24 @@
     )(scaled, scaled_t, up, qkv_weight, qkv_weight, qkv_weight, out_weight, mask, pick, z, *after)
 
 
+def gate_kernel(out_ref):
+    out_ref[...] = jnp.zeros((8, 128), F32)
+
+
+def gate(passed, after):
+    return pl.pallas_call(
+        behind(gate_kernel, len(passed) + len(after), 0, len(passed)),
+        out_shape=(jax.ShapeDtypeStruct((8, 128), F32),)
+        + tuple(jax.ShapeDtypeStruct(p.shape, p.dtype) for p in passed),
+        in_specs=waits(passed) + waits(after),
+        out_specs=tuple(vmem(1) + waits(passed)),
+        input_output_aliases={i: 1 + i for i in range(len(passed))},
+        compiler_params=params(4),
+        cost_estimate=cost(0, 1e4),
+        name="gate",
+    )(*passed, *after)[1:]
+
+
 def block_kernel(a0, a1, a2, a3, x_ref, w_ref, out_ref):
     def rows(i, _):
         at = pl.ds(pl.multiple_of(i * 432, 432), 432)
@@ -257,15 +275,12 @@
     lax.fori_loop(0, 2, rows, 0)
 
 
-def block_sum(att, x, out_weight, passed, after):
-    after = tuple(passed) + tuple(after)
-    return pl.pallas_call(
-        behind(block_kernel, len(after), 6, len(passed)),
-        out_shape=(jax.ShapeDtypeStruct((TOK, D), BF16),)
-        + tuple(jax.ShapeDtypeStruct(p.shape, p.dtype) for p in passed),
+def block_sum(att, x, out_weight, after):
+    return pl.pallas_call(
+        behind(block_kernel, len(after), 6),
+        out_shape=jax.ShapeDtypeStruct((TOK, D), BF16),
         in_specs=vmem(6) + waits(after),
-        out_specs=tuple(vmem(1) + waits(passed)),
-        input_output_aliases={6 + i: 1 + i for i in range(len(passed))},
+        out_specs=vmem(1)[0],
         compiler_params=params(32),
         cost_estimate=cost(2e9, 8e6),
         name="block_sum",
@@ -299,7 +314,13 @@
     )(*grads, qkv_weight, *after)
 
 
-def leave_kernel(s_ref, x_ref, up_ref, gain_ref, mix_ref, out_ref, n_ref):
+def leave_kernel(s_ref, x_ref, up_ref, gain_ref, mix_ref, out_ref, n_ref, sum_ref):
+    step = pl.program_id(0)
+
+    @pl.when(step == 0)
+    def _():
+        sum_ref[...] = jnp.zeros((8, D), F32)
+
     def rows(i, gain_sum):
         at = pl.ds(pl.multiple_of(i * 48, 48), 48)
         normed, inv_scale = norm_parts(x_ref[at, :].astype(F32))
@@ -312,33 +333,41 @@
         n_ref[at, :] = up_ref[at, :].astype(F32) + inv_scale * (g - mean_g - normed * mean_gn)
         return gain_sum + jnp.sum(both.reshape(6, 8, D), axis=0)
 
-    gain_sum = lax.fori_loop(0, TOK // 48, rows, jnp.zeros((8, D), F32))
-    whole = jnp.sum(gain_sum, axis=0, keepdims=True)
-    high = whole.astype(BF16).astype(F32)
-    mid = (whole - high).astype(BF16).astype(F32)
-    row16 = lax.broadcasted_iota(jnp.int32, (16, D), 0)
-    split = jnp.where(row16 == 0, high, jnp.where(row16 == 1, mid, whole - high - mid))
-    split = jnp.where(row16 < 3, split, 0.0).astype(BF16)
-    split = nn(split, mix_ref[...]).astype(BF16)
-
-    low = lax.broadcasted_iota(jnp.int32, (6 * HALF, 128), 1) < HEAD
+    gain_sum = lax.fori_loop(0, 6, rows, sum_ref[...])
+    sum_ref[...] = gain_sum
+
+    low = lax.broadcasted_iota(jnp.int32, (WIN, 128), 1) < HEAD
+    to = pl.ds(pl.multiple_of(step * WIN, WIN), WIN)
     for p in range(8):
         cols = slice(128 * p, 128 * p + 128)
-        level0 = jnp.concatenate([n_ref[WIN * w : WIN * w + HALF, cols] for w in range(WINS)], axis=0)
-        level1 = jnp.concatenate([n_ref[WIN * w + HALF : WIN * w + WIN, cols] for w in range(WINS)], axis=0)
-        out_ref[2 * p, 0 : 6 * HALF] = jnp.where(low, level0, pltpu.roll(level1, HEAD, 1)).astype(BF16)
-        out_ref[2 * p + 1, 0 : 6 * HALF] = jnp.where(low, pltpu.roll(level0, HEAD, 1), level1).astype(BF16)
-        out_ref[2 * p, 6 * HALF :] = split[:, cols]
-        out_ref[2 * p + 1, 6 * HALF :] = split[:, cols]
+        level0 = jnp.concatenate([n_ref[0:HALF, cols], n_ref[WIN : WIN + HALF, cols]], axis=0)
+        level1 = jnp.concatenate([n_ref[HALF:WIN, cols], n_ref[WIN + HALF : 2 * WIN, cols]], axis=0)
+        out_ref[2 * p, to] = jnp.where(low, level0, pltpu.roll(level1, HEAD, 1)).astype(BF16)
+        out_ref[2 * p + 1, to] = jnp.where(low, pltpu.roll(level0, HEAD, 1), level1).astype(BF16)
+
+    @pl.when(step == 2)
+    def _():
+        whole = jnp.sum(gain_sum, axis=0, keepdims=True)
+        high = whole.astype(BF16).astype(F32)
+        mid = (whole - high).astype(BF16).astype(F32)
+        row16 = lax.broadcasted_iota(jnp.int32, (16, D), 0)
+        split = jnp.where(row16 == 0, high, jnp.where(row16 == 1, mid, whole - high - mid))
+        split = jnp.where(row16 < 3, split, 0.0).astype(BF16)
+        split = nn(split, mix_ref[...]).astype(BF16)
+        for k in range(16):
+            out_ref[k, 6 * HALF :] = split[:, 128 * (k // 2) : 128 * (k // 2) + 128]
 
 
 def leave(norm_grad, x, up, gain, mix, after=()):
+    full = lambda shape: pl.BlockSpec(shape, lambda i: (0,) * len(shape))
+    part = pl.BlockSpec((2 * WIN, D), lambda i: (i, 0))
     return pl.pallas_call(
         behind(leave_kernel, len(after), 5),
+        grid=(3,),
         out_shape=jax.ShapeDtypeStruct((16, ROWS, 128), BF16),
-        in_specs=vmem(5) + waits(after),
-        out_specs=vmem(1)[0],
-        scratch_shapes=[pltpu.VMEM((TOK, D), F32)],
+        in_specs=[part, part, part, full((1, D)), full((D, D))] + waits(after),
+        out_specs=full((16, ROWS, 128)),
+        scratch_shapes=[pltpu.VMEM((2 * WIN, D), F32), pltpu.VMEM((8, D), F32)],
         compiler_params=params(32),
         cost_estimate=cost(4e9, 10e6),
         name="leave",
@@ -657,25 +686,26 @@
     total = s1.ring_y(y_index, (att[2],))
     s3 = heads(3, (total, s0.reduced))
     total = s2.ring_y(y_index, (att[3],))
-    norm_grad = product(grads, qkv_weight, (total,))
+    norm_grad = product(grads, qkv_weight)
     s3, s4 = s3.columns(0, 2 * GW), s3.columns(2 * GW, 4 * GW)
     out3, _ = exchange([s3], "z", 1)
     out4, _ = exchange([s4], "z", 3)
-    leaving = leave(norm_grad, x, up, gain, gain_mix(), (out3, out4, s1.reduced))
+    leaving = leave(norm_grad, x, up, gain, gain_mix(), (out3, out4, s1.reduced, total))
     back = lax.all_to_all(leaving, "lon", split_axis=0, concat_axis=0, tiled=True)
     def hand(sums, arrays):
         for t, p in zip(sums, arrays):
             t.terms[-1] = (p,) + t.terms[-1][1:]
 
     waiting = (s3, s4)
-    block, *passed = block_sum(att, x, out_weight, [newest(t) for t in waiting], (leaving,))
+    passed = gate([newest(t) for t in waiting], (leaving,))
+    block = block_sum(att, x, out_weight, (leaving,))
     hand(waiting, passed)
     exchange([s3], "z", 3)
     exchange([s4], "z", 1)
     exchange([s3, s4], "y", 1)
     exchange([s0, s1, s2], "z", 1)
-    joined, gain_sum, one, two = join_pieces(back, (newest(s3), newest(s0)), (block,))
-    hand((s3, s4, s0, s1, s2), (one, one, two, two, two))
+    joined, gain_sum, one = join_pieces(back, (newest(s3),), (block,))
+    hand((s3, s4), (one, one))
     exchange([s3, s4], "y", 3)
     exchange([s0, s1, s2], "z", 3)
     own, *send = last_cut((s0, s1, s2, s3, s4), gain_sum)

time: 268 us -> 259 us (0.966)
  waiting for transfers between devices: 45.6 us -> 40.1 us
  starting transfers between devices: 37.6 us -> 34.7 us
    ppermute x8, waiting for transfers between devices: 20.4 us -> 14.6 us  [exchange(): got = lax.ppermute(out, AXES, swapped(**{name: by}))]
    ppermute x8, starting transfers between devices: 14.6 us -> 11.8 us  [exchange(): got = lax.ppermute(out, AXES, swapped(**{name: by}))]
    pallas_call x2 -> x3, Pallas kernels: 8.34 us -> 9.37 us  [the longest x1 6.6 us: leave(): pl.pallas_call(behind(leave_kernel, len(after), 5), grid=(3,), out_shape=...]
  transfers between devices with their start and end apart: 23 -> 23, of which waited for: 10 -> 9; matrix products, arithmetic and copies ran while one was open for 12% -> 12% of each run, Pallas kernels for 24% -> 27%
where the time goes in v4:
time: 259 us; the launch traced here: 257 us
  Pallas kernels  97.1 us (37%)
  local copies, waits for them, and re-layouts  58.4 us (23%)
  waiting for transfers between devices  40.1 us (15%)
  starting transfers between devices  34.7 us (13%)
  between operations  14.2 us (5%)
  other arithmetic  12.9 us (5%)
    pallas_call x4, Pallas kernels, attend(): pl.pallas_call(behind(attend_kernel, len(after), 10), grid=(1,), out_shap...  56.1 us
    unnamed x120, local copies, waits for them, and re-layouts  38.7 us
    ppermute x8, waiting for transfers between devices, exchange(): got = lax.ppermute(out, AXES, swapped(**{name: by}))  14.6 us
    ppermute x8, starting transfers between devices, exchange(): got = lax.ppermute(out, AXES, swapped(**{name: by}))  11.8 us
    all_to_all x1, waiting for transfers between devices, per_device(): lax.all_to_all(pieces, 'lon', split_axis=0, concat_axis=0, tiled=True)  10.8 us
    pallas_call x1, Pallas kernels, product(): pl.pallas_call(behind(product_kernel, len(after), 5), out_shape=jax.Shape...  8.8 us
    ppermute x4, waiting for transfers between devices, heads(): return Sum(keep, lax.ppermute(send, AXES, swapped(core=1)))  8.36 us
    pallas_call x1, Pallas kernels, enter(): pl.pallas_call(enter_kernel, out_shape=(jax.ShapeDtypeStruct((TOK, D), BF...  7.29 us
  transfers between devices with their start and end apart: 23, of which 9 were waited for; matrix products, arithmetic and copies ran while one was open for 12% of the time, Pallas kernels for 27%

profile of v4, /device:TPU:0, one launch (start us, length us, event | category | flops | bytes accessed | tf_op | source)
XLA Modules:
  0.0 257.3 jit_solution(10129612335657728967)
XLA Ops:
  8.7 4.2 %split_pieces.1 = bf16[16,432,128]{2,1,0:T(8,128)(2,1)} custom-call(bf16[2,12,64,576]{3,2,1,0:T(8,128)(2,1)S(1)} %bitcast.123), custom_call_target="tpu_custom_call" | custom-call | flops 200000000 | bytes 400000 | tf_op jit(solution)/shard_map/split_pieces/pallas_call | solution.py:79
  12.9 7.2 %all-to-all-start = ((bf16[16,432,128]{2,1,0:T(8,128)(2,1)}), bf16[16,432,128]{2,1,0:T(8,128)(2,1)S(1)}, u32[]{:S(2)}, u32[]{:S(2)}) async-start(bf16[16,432,128]{2,1,0:T(8,128)(2,1)} %split_pieces.1), calls=%async_computation | async-start | bytes 3538944 | tf_op jit(solution)/shard_map/all_to_all | solution.py:659
  27.9 2.0 copy.37
  29.9 2.5 reshape.416.refs_2_
  35.2 10.8 %all-to-all-done.r_ref = bf16[16,432,128]{2,1,0:T(8,128)(2,1)S(1)} async-done(((bf16[16,432,128]{2,1,0:T(8,128)(2,1)}), bf16[16,432,128]{2,1,0:T(8,128)(2,1)S(1)}, u32[]{:S(2)}, u32[]{:S(2)}) %all-to-all-start) | async-done | bytes 1769504 | tf_op jit(solution)/shard_map/all_to_all | solution.py:659
  50.3 7.3 %enter.1 = (bf16[864,1024]{1,0:T(8,128)(2,1)S(1)}, bf16[864,1024]{1,0:T(8,128)(2,1)S(1)}, bf16[1024,864]{1,0:T(8,128)(2,1)S(1)}) custom-call(bf16[16,432,128]{2,1,0:T(8,128)(2,1)S(1)} %copy-done.23, f32[1,1024]{1,0:T(1,128)S(1)} %bitcast.129, bf16[1024,1024]{1,0:T(8,128)(2,1)S(1)} %copy-done.20), custom_call_target="tpu_custom_call" | custom-call | flops 300000000 | bytes 900000 | tf_op jit(solution)/shard_map/enter/pallas_call | solution.py:129
  60.0 13.8 %attend.4 = (bf16[864,256]{1,0:T(8,128)(2,1)S(1)}, bf16[864,768]{1,0:T(8,128)(2,1)S(1)}, f32[512,1024]{1,0:T(8,128)}, f32[512,1024]{1,0:T(8,128)}) custom-call(bf16[864,1024]{1,0:T(8,128)(2,1)S(1)} %get-tuple-element.40.refs_0_, bf16[1024,864]{1,0:T(8,128)(2,1)} %copy-done.3, bf16[864,1024]{1,0:T(8,128)(2,1)S(1)} %reshape.416.refs_2_, ...), custom_call_target="tpu_custom_call" | custom-call | flops 800000000 | bytes 1500000 | tf_op jit(solution)/shard_map/attend/pallas_call | solution.py:213
  73.9 4.4 %collective-permute-done = f32[512,1024]{1,0:T(8,128)S(1)} collective-permute-done((f32[512,1024]{1,0:T(8,128)}, f32[512,1024]{1,0:T(8,128)S(1)}, u32[]{:S(2)}, u32[]{:S(2)}) %collective-permute-start) | collective-permute-done | bytes 2097184 | tf_op jit(solution)/shard_map/ppermute | solution.py:677
  83.7 13.8 %attend.5 = (bf16[864,256]{1,0:T(8,128)(2,1)S(1)}, bf16[864,768]{1,0:T(8,128)(2,1)S(1)}, f32[512,1024]{1,0:T(8,128)}, f32[512,1024]{1,0:T(8,128)}) custom-call(bf16[864,1024]{1,0:T(8,128)(2,1)S(1)} %get-tuple-element.40.refs_0_, bf16[1024,864]{1,0:T(8,128)(2,1)} %copy-done.3, bf16[864,1024]{1,0:T(8,128)(2,1)S(1)} %reshape.416.refs_2_, ...), custom_call_target="tpu_custom_call" | custom-call | flops 800000000 | bytes 1500000 | tf_op jit(solution)/shard_map/attend/pallas_call | solution.py:213
  99.5 13.9 %attend.6 = (bf16[864,256]{1,0:T(8,128)(2,1)S(1)}, bf16[864,768]{1,0:T(8,128)(2,1)S(1)}, f32[512,1024]{1,0:T(8,128)}, f32[512,1024]{1,0:T(8,128)}) custom-call(bf16[864,1024]{1,0:T(8,128)(2,1)S(1)} %get-tuple-element.40.refs_0_, bf16[1024,864]{1,0:T(8,128)(2,1)} %copy-done.3, bf16[864,1024]{1,0:T(8,128)(2,1)S(1)} %reshape.416.refs_2_, ...), custom_call_target="tpu_custom_call" | custom-call | flops 800000000 | bytes 1500000 | tf_op jit(solution)/shard_map/attend/pallas_call | solution.py:213
  118.2 14.5 %attend.7 = (bf16[864,256]{1,0:T(8,128)(2,1)S(1)}, bf16[864,768]{1,0:T(8,128)(2,1)S(1)}, f32[512,1024]{1,0:T(8,128)}, f32[512,1024]{1,0:T(8,128)}) custom-call(bf16[864,1024]{1,0:T(8,128)(2,1)S(1)} %get-tuple-element.40.refs_0_, bf16[1024,864]{1,0:T(8,128)(2,1)} %copy-done.3, bf16[864,1024]{1,0:T(8,128)(2,1)} %copy-done, bf16[1024,3072]{1,0:T(8,128)(2,1)} %refs_4_.9, ...), custom_call_target="tpu_custom_call" | custom-call | flops 800000000 | bytes 1500000 | tf_op jit(solution)/shard_map/attend/pallas_call | solution.py:213
  132.7 4.3 %ordered_sum.5.refs_8_ = f32[4,128,1024]{2,1,0:T(8,128)} custom-call(s32[1]{0:T(128)} %bitcast.6.y_ref, f32[4,128,1024]{2,1,0:T(8,128)S(1)} %bitcast.120, f32[4,128,1024]{2,1,0:T(8,128)} %bitcast.18.b_ref, bf16[864,256]{1,0:T(8,128)(2,1)S(1)} %get-tuple-element.49.refs_0_.refs_3_), custom_call_target="tpu_custom_call" | custom-call | bytes 500000 | tf_op jit(solution)/shard_map/ordered_sum/pallas_call | solution.py:517
  137.6 4.0 %collective-permute-done.2 = f32[512,1024]{1,0:T(8,128)S(1)} collective-permute-done((f32[512,1024]{1,0:T(8,128)}, f32[512,1024]{1,0:T(8,128)S(1)}, u32[]{:S(2)}, u32[]{:S(2)}) %collective-permute-start.2) | collective-permute-done | bytes 2097184 | tf_op jit(solution)/shard_map/ppermute | solution.py:677
  145.2 2.5 collective-permute-start.5
  147.7 2.2 fusion.1.refs_4_
  151.3 8.8 %product.1.refs_0_ = f32[864,1024]{1,0:T(8,128)S(1)} custom-call(bf16[864,768]{1,0:T(8,128)(2,1)S(1)} %copy-done.47, bf16[864,768]{1,0:T(8,128)(2,1)S(1)} %copy-done.49, bf16[864,768]{1,0:T(8,128)(2,1)S(1)} %copy-done.51, bf16[864,768]{1,0:T(8,128)(2,1)S(1)} %copy-done.53, bf16[1024,3072]{1,0:T(8,128)(2,1)} %refs_4_.9), custom_call_target="tpu_custom_call" | custom-call | flops 600000000 | bytes 1500000 | tf_op jit(solution)/shard_map/product/pallas_call | solution.py:306
  161.9 2.1 copy-done.16
  166.6 6.6 %leave.1.refs_6_.refs_2_ = bf16[16,448,128]{2,1,0:T(8,128)(2,1)S(1)} custom-call(f32[864,1024]{1,0:T(8,128)S(1)} %copy-done.16, bf16[864,1024]{1,0:T(8,128)(2,1)S(1)} %copy-done.25, bf16[864,1024]{1,0:T(8,128)(2,1)S(1)} %copy-done.1, f32[1,1024]{1,0:T(1,128)S(1)} %bitcast.130, bf16[1024,1024]{1,0:T(8,128)(2,1)S(1)} %copy-done.21, ...), custom_call_target="tpu_custom_call" | custom-call | flops 400000000 | bytes 1000000 | tf_op jit(solution)/shard_map/leave/pallas_call | solution.py:364
  174.4 4.7 %all-to-all-start.1 = ((bf16[16,448,128]{2,1,0:T(8,128)(2,1)}), bf16[16,448,128]{2,1,0:T(8,128)(2,1)}, u32[]{:S(2)}, u32[]{:S(2)}) async-start(bf16[16,448,128]{2,1,0:T(8,128)(2,1)} %copy-done.4), calls=%async_computation.3 | async-start | bytes 3670016 | tf_op jit(solution)/shard_map/all_to_all | solution.py:694
  181.3 2.1 fusion.3
  188.1 5.3 %collective-permute-done.6 = f32[16,8,512]{2,1,0:T(8,128)} collective-permute-done((f32[16,8,512]{2,1,0:T(8,128)}, f32[16,8,512]{2,1,0:T(8,128)}, u32[]{:S(2)}, u32[]{:S(2)}) %collective-permute-start.6) | collective-permute-done | bytes 262176 | tf_op jit(solution)/shard_map/ppermute | solution.py:500
  202.8 2.2 block_sum.1.refs_2_
  210.6 4.0 %join_pieces.1 = (bf16[2,12,64,576]{3,2,1,0:T(8,128)(2,1)}, f32[1,128]{1,0:T(1,128)S(1)}, f32[2,1,4,8,1024]{4,3,2,1,0:T(8,128)S(1)}) custom-call(bf16[16,448,128]{2,1,0:T(8,128)(2,1)} %all-to-all-done.1.refs_0_, f32[2,1,4,8,1024]{4,3,2,1,0:T(8,128)S(1)} %bitcast.115, bf16[864,1024]{1,0:T(8,128)(2,1)S(1)} %copy-done.14), custom_call_target="tpu_custom_call", output_to_operand_aliasing={{2}: (1, {})} | custom-call | flops 200000000 | bytes 400000 | tf_op jit(solution)/shard_map/join_pieces/pallas_call | solution.py:404
  216.5 2.2 collective-permute-start.11
  218.6 4.1 %collective-permute-done.11 = f32[4,8,1024]{2,1,0:T(8,128)S(1)} collective-permute-done((f32[4,8,1024]{2,1,0:T(8,128)S(1)}, f32[4,8,1024]{2,1,0:T(8,128)S(1)}, u32[]{:S(2)}, u32[]{:S(2)}) %collective-permute-start.11) | collective-permute-done | bytes 131104 | tf_op jit(solution)/shard_map/ppermute | solution.py:500
  222.7 4.0 %collective-permute-done.10 = f32[4,8,3072]{2,1,0:T(8,128)S(1)} collective-permute-done((f32[4,8,3072]{2,1,0:T(8,128)S(1)}, f32[4,8,3072]{2,1,0:T(8,128)S(1)}, u32[]{:S(2)}, u32[]{:S(2)}) %collective-permute-start.10) | collective-permute-done | bytes 393248 | tf_op jit(solution)/shard_map/ppermute | solution.py:500
  228.6 3.6 %collective-permute-start.13 = (f32[8,4096]{1,0:T(8,128)S(1)}, f32[8,4096]{1,0:T(8,128)S(1)}, u32[]{:S(2)}, u32[]{:S(2)}) collective-permute-start(f32[8,4096]{1,0:T(8,128)S(1)} %get-tuple-element.66), channel_id=1, source_target_pairs={{0,2},{1,3},{2,0},{3,1},{4,6},{5,7},{6,4},{7,5},{8,10},{9,11},{10,... | collective-permute-start | bytes 393224 | tf_op jit(solution)/shard_map/ppermute | solution.py:712
  232.5 4.8 %collective-permute-done.13.got2 = f32[8,4096]{1,0:T(8,128)S(1)} collective-permute-done((f32[8,4096]{1,0:T(8,128)S(1)}, f32[8,4096]{1,0:T(8,128)S(1)}, u32[]{:S(2)}, u32[]{:S(2)}) %collective-permute-start.13) | collective-permute-done | bytes 131104 | tf_op jit(solution)/shard_map/ppermute | solution.py:712
  239.4 2.1 collective-permute-start.16
  241.6 2.6 collective-permute-start.17
  244.1 2.4 reshape.425
  246.5 3.1 %copy.33 = bf16[2,2,6,3,12,1024]{5,0,4,3,2,1:T(2,128)(2,1)} copy(bf16[2,2,6,3,12,1024]{5,4,2,0,3,1:T(8,128)(2,1)S(1)} %bitcast.131) | data formatting | bytes 3538944 | tf_op jit(solution)/shard_map/transpose | solution.py:718
  (186 shorter events, 71.1 us)
Async XLA Ops:
  12.9 15.0 %copy-start.59 = (bf16[2,12,36,1024]{3,0,2,1:T(2,128)(2,1)S(1)}, bf16[2,12,36,1024]{3,0,2,1:T(2,128)(2,1)}, u32[]{:S(2)}) copy-start(bf16[2,12,36,1024]{3,0,2,1:T(2,128)(2,1)} %param.11) | copy-start | bytes 5308420
  12.9 33.0 %all-to-all-start = ((bf16[16,432,128]{2,1,0:T(8,128)(2,1)}), bf16[16,432,128]{2,1,0:T(8,128)(2,1)S(1)}, u32[]{:S(2)}, u32[]{:S(2)}) async-start(bf16[16,432,128]{2,1,0:T(8,128)(2,1)} %split_pieces.1), calls=%async_computation | async-start | bytes 3538944 | tf_op jit(solution)/shard_map/all_to_all | solution.py:659
  20.2 96.6 %reduce-scatter.4.cloned.1.call-start = ((), (), s32[]{:S(2)}) async-start(), calls=%async_computation.5 | async-start | bytes 2621440 | tf_op jit(solution)/shard_map/reduce_scatter | solution.py:477
  32.4 67.1 %copy-start = (bf16[864,1024]{1,0:T(8,128)(2,1)}, bf16[864,1024]{1,0:T(8,128)(2,1)S(1)}, u32[]{:S(2)}) copy-start(bf16[864,1024]{1,0:T(8,128)(2,1)S(1)} %reshape.416.refs_2_) | copy-start | bytes 5308420
  32.4 14.8 %copy-start.58 = (f32[1024]{0:T(1024)S(1)}, f32[1024]{0:T(1024)}, u32[]{:S(2)}) copy-start(f32[1024]{0:T(1024)} %param.8) | copy-start | bytes 12292
  47.2 12.9 %copy-start.17 = (f32[864,1]{1,0:T(8,128)S(1)}, f32[864,1]{1,0:T(8,128)}, u32[]{:S(2)}) copy-start(f32[864,1]{1,0:T(8,128)} %select_n.250.refs_7_) | copy-start | bytes 10372
  73.9 4.4 %collective-permute-start = (f32[512,1024]{1,0:T(8,128)}, f32[512,1024]{1,0:T(8,128)S(1)}, u32[]{:S(2)}, u32[]{:S(2)}) collective-permute-start(f32[512,1024]{1,0:T(8,128)} %get-tuple-element.45), channel_id=1, source_target_pairs={{0,1},{1,0},{2,3},{3,2},{4,5},{5,4},{6,7},{7,6},{8,9},{9,8},{10,11... | collective-permute-start | bytes 6291464 | tf_op jit(solution)/shard_map/ppermute | solution.py:677
  81.5 80.3 %reduce-scatter.6.cloned.1.call-start = ((), (), s32[]{:S(2)}) async-start(), calls=%async_computation.6 | async-start | bytes 2621440 | tf_op jit(solution)/shard_map/reduce_scatter | solution.py:477
  99.4 14.1 %copy-start.39 = (f32[512,1024]{1,0:T(8,128)S(1)}, f32[512,1024]{1,0:T(8,128)}, u32[]{:S(2)}) copy-start(f32[512,1024]{1,0:T(8,128)} %get-tuple-element.47) | copy-start | bytes 6291460
  99.4 14.1 %collective-permute-start.1 = (f32[512,1024]{1,0:T(8,128)}, f32[512,1024]{1,0:T(8,128)S(1)}, u32[]{:S(2)}, u32[]{:S(2)}) collective-permute-start(f32[512,1024]{1,0:T(8,128)} %get-tuple-element.48), channel_id=1, source_target_pairs={{0,1},{1,0},{2,3},{3,2},{4,5},{5,4},{6,7},{7,6},{8,9},{9,8},{10,11... | collective-permute-start | bytes 6291464 | tf_op jit(solution)/shard_map/ppermute | solution.py:677
  116.2 68.3 %reduce-scatter.8.cloned.1.call-start = ((), (), s32[]{:S(2)}) async-start(), calls=%async_computation.7 | async-start | bytes 2621440 | tf_op jit(solution)/shard_map/reduce_scatter | solution.py:477
  116.2 16.5 %collective-permute-start.3 = (f32[512,1024]{1,0:T(8,128)}, f32[512,1024]{1,0:T(8,128)}, u32[]{:S(2)}, u32[]{:S(2)}) collective-permute-start(f32[512,1024]{1,0:T(8,128)} %get-tuple-element.58), channel_id=1, source_target_pairs={{0,1},{1,0},{2,3},{3,2},{4,5},{5,4},{6,7},{7,6},{8,9},{9,8},{10,11... | collective-permute-start | bytes 6291464 | tf_op jit(solution)/shard_map/ppermute | solution.py:677
  118.2 14.5 %copy-start.38 = (f32[512,1024]{1,0:T(8,128)S(1)}, f32[512,1024]{1,0:T(8,128)}, u32[]{:S(2)}) copy-start(f32[512,1024]{1,0:T(8,128)} %get-tuple-element.57) | copy-start | bytes 6291460
  137.1 4.6 %collective-permute-start.2 = (f32[512,1024]{1,0:T(8,128)}, f32[512,1024]{1,0:T(8,128)S(1)}, u32[]{:S(2)}, u32[]{:S(2)}) collective-permute-start(f32[512,1024]{1,0:T(8,128)} %get-tuple-element.56), channel_id=1, source_target_pairs={{0,1},{1,0},{2,3},{3,2},{4,5},{5,4},{6,7},{7,6},{8,9},{9,8},{10,11... | collective-permute-start | bytes 6291464 | tf_op jit(solution)/shard_map/ppermute | solution.py:677
  143.3 35.9 %collective-permute-start.4 = (f32[32,8,512]{2,1,0:T(8,128)}, f32[32,8,512]{2,1,0:T(8,128)}, u32[]{:S(2)}, u32[]{:S(2)}) collective-permute-start(f32[32,8,512]{2,1,0:T(8,128)} %bitcast.14.refs_5_), channel_id=1, source_target_pairs={{0,32},{1,33},{2,34},{3,35},{4,36},{5,37},{6,38},{7,39},{8,40},{9,... | collective-permute-start | bytes 1572872 | tf_op jit(solution)/shard_map/ppermute | solution.py:500
  145.2 34.0 %collective-permute-start.5 = (f32[32,8,512]{2,1,0:T(8,128)}, f32[32,8,512]{2,1,0:T(8,128)}, u32[]{:S(2)}, u32[]{:S(2)}) collective-permute-start(f32[32,8,512]{2,1,0:T(8,128)} %bitcast.15.refs_6_), channel_id=1, source_target_pairs={{0,96},{1,97},{2,98},{3,99},{4,100},{5,101},{6,102},{7,103},{8,104... | collective-permute-start | bytes 1572872 | tf_op jit(solution)/shard_map/ppermute | solution.py:500
  174.4 33.7 %all-to-all-start.1 = ((bf16[16,448,128]{2,1,0:T(8,128)(2,1)}), bf16[16,448,128]{2,1,0:T(8,128)(2,1)}, u32[]{:S(2)}, u32[]{:S(2)}) async-start(bf16[16,448,128]{2,1,0:T(8,128)(2,1)} %copy-done.4), calls=%async_computation.3 | async-start | bytes 3670016 | tf_op jit(solution)/shard_map/all_to_all | solution.py:694
  183.5 10.0 %collective-permute-start.6 = (f32[16,8,512]{2,1,0:T(8,128)}, f32[16,8,512]{2,1,0:T(8,128)}, u32[]{:S(2)}, u32[]{:S(2)}) collective-permute-start(f32[16,8,512]{2,1,0:T(8,128)} %bitcast.23), channel_id=1, source_target_pairs={{0,96},{1,97},{2,98},{3,99},{4,100},{5,101},{6,102},{7,103},{8,104... | collective-permute-start | bytes 786440 | tf_op jit(solution)/shard_map/ppermute | solution.py:500
  184.1 10.3 %collective-permute-start.7 = (f32[16,8,512]{2,1,0:T(8,128)}, f32[16,8,512]{2,1,0:T(8,128)}, u32[]{:S(2)}, u32[]{:S(2)}) collective-permute-start(f32[16,8,512]{2,1,0:T(8,128)} %bitcast.27), channel_id=1, source_target_pairs={{0,32},{1,33},{2,34},{3,35},{4,36},{5,37},{6,38},{7,39},{8,40},{9,... | collective-permute-start | bytes 786440 | tf_op jit(solution)/shard_map/ppermute | solution.py:500
  184.5 13.8 %copy-start.42 = (bf16[864,256]{1,0:T(8,128)(2,1)S(1)}, bf16[864,256]{1,0:T(8,128)(2,1)}, u32[]{:S(2)}) copy-start(bf16[864,256]{1,0:T(8,128)(2,1)} %copy-done.41) | copy-start | bytes 1327108
  185.5 12.7 %copy-start.2 = (bf16[1024,1024]{1,0:T(8,128)(2,1)S(1)}, bf16[1024,1024]{1,0:T(8,128)(2,1)}, u32[]{:S(2)}) copy-start(bf16[1024,1024]{1,0:T(8,128)(2,1)} %refs_5_.9) | copy-start | bytes 6291460
  185.5 12.7 %copy-start.6 = (bf16[16,448,128]{2,1,0:T(8,128)(2,1)S(1)}, bf16[16,448,128]{2,1,0:T(8,128)(2,1)}, u32[]{:S(2)}) copy-start(bf16[16,448,128]{2,1,0:T(8,128)(2,1)} %copy-done.4) | copy-start | bytes 5505028
  186.5 28.1 %collective-permute-start.9 = (f32[8,8,3072]{2,1,0:T(8,128)}, f32[8,8,3072]{2,1,0:T(8,128)S(1)}, u32[]{:S(2)}, u32[]{:S(2)}) collective-permute-start(f32[8,8,3072]{2,1,0:T(8,128)} %pad_maximum_fusion), channel_id=1, source_target_pairs={{0,32},{1,33},{2,34},{3,35},{4,36},{5,37},{6,38},{7,39},{8,40},{9,... | collective-permute-start | bytes 2359304 | tf_op jit(solution)/shard_map/ppermute | solution.py:500
  196.5 11.0 %collective-permute-start.8 = (f32[8,8,1024]{2,1,0:T(8,128)S(1)}, f32[8,8,1024]{2,1,0:T(8,128)S(1)}, u32[]{:S(2)}, u32[]{:S(2)}) collective-permute-start(f32[8,8,1024]{2,1,0:T(8,128)S(1)} %pad_maximum_fusion.2), channel_id=1, source_target_pairs={{0,4},{1,5},{2,6},{3,7},{4,0},{5,1},{6,2},{7,3},{8,12},{9,13},{10,... | collective-permute-start | bytes 786440 | tf_op jit(solution)/shard_map/ppermute | solution.py:500
  214.7 11.9 %collective-permute-start.10 = (f32[4,8,3072]{2,1,0:T(8,128)S(1)}, f32[4,8,3072]{2,1,0:T(8,128)S(1)}, u32[]{:S(2)}, u32[]{:S(2)}) collective-permute-start(f32[4,8,3072]{2,1,0:T(8,128)S(1)} %pad_maximum_fusion.1), channel_id=1, source_target_pairs={{0,96},{1,97},{2,98},{3,99},{4,100},{5,101},{6,102},{7,103},{8,104... | collective-permute-start | bytes 1179656 | tf_op jit(solution)/shard_map/ppermute | solution.py:500
  216.5 6.3 %collective-permute-start.11 = (f32[4,8,1024]{2,1,0:T(8,128)S(1)}, f32[4,8,1024]{2,1,0:T(8,128)S(1)}, u32[]{:S(2)}, u32[]{:S(2)}) collective-permute-start(f32[4,8,1024]{2,1,0:T(8,128)S(1)} %pad_maximum_fusion.3), channel_id=1, source_target_pairs={{0,12},{1,13},{2,14},{3,15},{4,8},{5,9},{6,10},{7,11},{8,4},{9,5},... | collective-permute-start | bytes 393224 | tf_op jit(solution)/shard_map/ppermute | solution.py:500
  227.7 11.0 %collective-permute-start.12 = (f32[8,4224]{1,0:T(8,128)S(1)}, f32[8,4224]{1,0:T(8,128)S(1)}, u32[]{:S(2)}, u32[]{:S(2)}) collective-permute-start(f32[8,4224]{1,0:T(8,128)S(1)} %get-tuple-element.65), channel_id=1, source_target_pairs={{0,16},{1,17},{2,18},{3,19},{4,20},{5,21},{6,22},{7,23},{8,24},{9,... | collective-permute-start | bytes 405512 | tf_op jit(solution)/shard_map/ppermute | solution.py:712
  228.6 8.7 %collective-permute-start.13 = (f32[8,4096]{1,0:T(8,128)S(1)}, f32[8,4096]{1,0:T(8,128)S(1)}, u32[]{:S(2)}, u32[]{:S(2)}) collective-permute-start(f32[8,4096]{1,0:T(8,128)S(1)} %get-tuple-element.66), channel_id=1, source_target_pairs={{0,2},{1,3},{2,0},{3,1},{4,6},{5,7},{6,4},{7,5},{8,10},{9,11},{10,... | collective-permute-start | bytes 393224 | tf_op jit(solution)/shard_map/ppermute | solution.py:712
  232.2 6.6 %collective-permute-start.14 = (f32[8,4096]{1,0:T(8,128)S(1)}, f32[8,4096]{1,0:T(8,128)S(1)}, u32[]{:S(2)}, u32[]{:S(2)}) collective-permute-start(f32[8,4096]{1,0:T(8,128)S(1)} %get-tuple-element.67), channel_id=1, source_target_pairs={{0,18},{1,19},{2,16},{3,17},{4,22},{5,23},{6,20},{7,21},{8,26},{9,... | collective-permute-start | bytes 393224 | tf_op jit(solution)/shard_map/ppermute | solution.py:712
  239.4 10.2 %collective-permute-start.15 = (f32[8,384]{1,0:T(8,128)S(1)}, f32[8,384]{1,0:T(8,128)S(1)}, u32[]{:S(2)}, u32[]{:S(2)}) collective-permute-start(f32[8,384]{1,0:T(8,128)S(1)} %get-tuple-element.70), channel_id=1, source_target_pairs={{0,32},{1,33},{2,34},{3,35},{4,36},{5,37},{6,38},{7,39},{8,40},{9,... | collective-permute-start | bytes 36872 | tf_op jit(solution)/shard_map/ppermute | solution.py:714
  239.4 10.2 %collective-permute-start.16 = (f32[8,384]{1,0:T(8,128)S(1)}, f32[8,384]{1,0:T(8,128)S(1)}, u32[]{:S(2)}, u32[]{:S(2)}) collective-permute-start(f32[8,384]{1,0:T(8,128)S(1)} %get-tuple-element.71), channel_id=1, source_target_pairs={{0,64},{1,65},{2,66},{3,67},{4,68},{5,69},{6,70},{7,71},{8,72},{9,... | collective-permute-start | bytes 36872 | tf_op jit(solution)/shard_map/ppermute | solution.py:714
  241.6 8.0 %collective-permute-start.17 = (f32[8,384]{1,0:T(8,128)S(1)}, f32[8,384]{1,0:T(8,128)S(1)}, u32[]{:S(2)}, u32[]{:S(2)}) collective-permute-start(f32[8,384]{1,0:T(8,128)S(1)} %get-tuple-element.72), channel_id=1, source_target_pairs={{0,96},{1,97},{2,98},{3,99},{4,100},{5,101},{6,102},{7,103},{8,104... | collective-permute-start | bytes 36872 | tf_op jit(solution)/shard_map/ppermute | solution.py:714
  (52 other events, 162.6 us)
Sparse Core Ops, SparseCore 0:
  81.7 28.2 reduce-scatter.3
  116.3 28.3 reduce-scatter.5
  147.1 29.3 reduce-scatter.7

commit v5 on v4

--- a/solution.py
+++ b/solution.py
@@ -136,7 +136,7 @@
         in_specs=vmem(3),
         out_specs=tuple(vmem(3)),
         scratch_shapes=[pltpu.VMEM((TOK, D), F32)],
-        compiler_params=params(32),
+        compiler_params=params(62),
         cost_estimate=cost(3e9, 9e6),
         name="enter",
     )(pieces, gain, pick)
@@ -239,7 +239,7 @@
             full((D // 2, 4 * GW)),
         ),
         scratch_shapes=[pltpu.VMEM((TOK, GW), BF16)] * 4 + [pltpu.VMEM((WIN, QUADS * WIN), F32)],
-        compiler_params=params(48),
+        compiler_params=params(62),
         cost_estimate=cost(8e9, 15e6),
         name="attend",
     )(scaled, scaled_t, up, qkv_weight, qkv_weight, qkv_weight, out_weight, mask, pick, z, *after)
@@ -281,7 +281,7 @@
         out_shape=jax.ShapeDtypeStruct((TOK, D), BF16),
         in_specs=vmem(6) + waits(after),
         out_specs=vmem(1)[0],
-        compiler_params=params(32),
+        compiler_params=params(62),
         cost_estimate=cost(2e9, 8e6),
         name="block_sum",
     )(*att, x, out_weight, *after)
@@ -308,7 +308,7 @@
         out_shape=jax.ShapeDtypeStruct((TOK, D), F32),
         in_specs=vmem(5) + waits(after),
         out_specs=vmem(1)[0],
-        compiler_params=params(40),
+        compiler_params=params(62),
         cost_estimate=cost(6e9, 15e6),
         name="product",
     )(*grads, qkv_weight, *after)
@@ -368,7 +368,7 @@
         in_specs=[part, part, part, full((1, D)), full((D, D))] + waits(after),
         out_specs=full((16, ROWS, 128)),
         scratch_shapes=[pltpu.VMEM((2 * WIN, D), F32), pltpu.VMEM((8, D), F32)],
-        compiler_params=params(32),
+        compiler_params=params(62),
         cost_estimate=cost(4e9, 10e6),
         name="leave",
     )(norm_grad, x, up, gain, mix, *after)
@@ -412,7 +412,7 @@
         out_specs=tuple(vmem(2) + waits(passed)),
         input_output_aliases={1 + i: 2 + i for i in range(len(passed))},
         scratch_shapes=[pltpu.VMEM((16, 6 * HALF, 128), F32), pltpu.VMEM((LON, 128), F32)],
-        compiler_params=params(32),
+        compiler_params=params(62),
         cost_estimate=cost(2e9, 4e6),
         name="join_pieces",
     )(pieces, *after)
@@ -685,8 +685,9 @@
     s2 = heads(2, (total,))
     total = s1.ring_y(y_index, (att[2],))
     s3 = heads(3, (total, s0.reduced))
-    total = s2.ring_y(y_index, (att[3],))
     norm_grad = product(grads, qkv_weight)
+    total = s2.ring_y(y_index, (norm_grad,))
+    s3.terms[-1] = (gate([newest(s3)], (norm_grad,))[0],) + s3.terms[-1][1:]
     s3, s4 = s3.columns(0, 2 * GW), s3.columns(2 * GW, 4 * GW)
     out3, _ = exchange([s3], "z", 1)
     out4, _ = exchange([s4], "z", 3)

time: 259 us -> 264 us (1.019)
  local copies, waits for them, and re-layouts: 58.4 us -> 33 us
  Pallas kernels: 97.1 us -> 120 us
  waiting for transfers between devices: 40.1 us -> 46.4 us
    unnamed x120 -> x46, local copies, waits for them, and re-layouts: 38.7 us -> 18.1 us
    all_to_all x1, waiting for transfers between devices: 10.8 us -> 17.8 us  [per_device(): lax.all_to_all(pieces, 'lon', split_axis=0, concat_axis=0, tiled=True)]
    pallas_call x4, Pallas kernels: 56.1 us -> 60.2 us  [attend(): pl.pallas_call(behind(attend_kernel, len(after), 10), grid=(1,), out_shap...]
    pallas_call x1, Pallas kernels: 2.18 us -> 6.11 us  [block_sum(): pl.pallas_call(behind(block_kernel, len(after), 6), out_shape=jax.ShapeDt...]
    pallas_call x1, Pallas kernels: 6.6 us -> 10.5 us  [leave(): pl.pallas_call(behind(leave_kernel, len(after), 5), grid=(3,), out_shape=...]
    pallas_call x1, Pallas kernels: 7.29 us -> 11.1 us  [enter(): pl.pallas_call(enter_kernel, out_shape=(jax.ShapeDtypeStruct((TOK, D), BF...]
    pallas_call x3, Pallas kernels: 4.94 us -> 8.56 us  [ordered_sum(): pl.pallas_call(add_kernel, grid_spec=pltpu.PrefetchScalarGridSpec(num_sca...]
    select_n x3, local copies, waits for them, and re-layouts: 4.57 us -> 1.04 us  [per_device(): jnp.where(window_order(mask).reshape(TOK, 1) == 1, 0.0, -1e+30).astype(F32)]
  transfers between devices with their start and end apart: 23 -> 23, of which waited for: 9 -> 9; matrix products, arithmetic and copies ran while one was open for 12% -> 10% of each run, Pallas kernels for 27% -> 33%
where the time goes in v5:
time: 264 us; the launch traced here: 263 us
  Pallas kernels  120 us (45%)
  waiting for transfers between devices  46.4 us (18%)
  starting transfers between devices  36.1 us (14%)
  local copies, waits for them, and re-layouts  33 us (12%)
  between operations  14.1 us (5%)
  other arithmetic  13.4 us (5%)
    pallas_call x4, Pallas kernels, attend(): pl.pallas_call(behind(attend_kernel, len(after), 10), grid=(1,), out_shap...  60.2 us
    unnamed x46, local copies, waits for them, and re-layouts  18.1 us
    all_to_all x1, waiting for transfers between devices, per_device(): lax.all_to_all(pieces, 'lon', split_axis=0, concat_axis=0, tiled=True)  17.8 us
    ppermute x8, waiting for transfers between devices, exchange(): got = lax.ppermute(out, AXES, swapped(**{name: by}))  13.7 us
    ppermute x8, starting transfers between devices, exchange(): got = lax.ppermute(out, AXES, swapped(**{name: by}))  13.5 us
    pallas_call x1, Pallas kernels, product(): pl.pallas_call(behind(product_kernel, len(after), 5), out_shape=jax.Shape...  12.1 us
    pallas_call x1, Pallas kernels, enter(): pl.pallas_call(enter_kernel, out_shape=(jax.ShapeDtypeStruct((TOK, D), BF...  11.1 us
    pallas_call x1, Pallas kernels, leave(): pl.pallas_call(behind(leave_kernel, len(after), 5), grid=(3,), out_shape=...  10.5 us
  transfers between devices with their start and end apart: 23, of which 9 were waited for; matrix products, arithmetic and copies ran while one was open for 10% of the time, Pallas kernels for 33%

profile of v5, /device:TPU:0, one launch (start us, length us, event | category | flops | bytes accessed | tf_op | source)
XLA Modules:
  0.0 263.1 jit_solution(9522339000263177872)
XLA Ops:
  8.7 4.2 %split_pieces.1 = bf16[16,432,128]{2,1,0:T(8,128)(2,1)} custom-call(bf16[2,12,64,576]{3,2,1,0:T(8,128)(2,1)S(1)} %bitcast.119), custom_call_target="tpu_custom_call" | custom-call | flops 200000000 | bytes 400000 | tf_op jit(solution)/shard_map/split_pieces/pallas_call | solution.py:79
  12.9 7.3 %all-to-all-start = ((bf16[16,432,128]{2,1,0:T(8,128)(2,1)}), bf16[16,432,128]{2,1,0:T(8,128)(2,1)}, u32[]{:S(2)}, u32[]{:S(2)}) async-start(bf16[16,432,128]{2,1,0:T(8,128)(2,1)} %split_pieces.1), calls=%async_computation | async-start | bytes 3538944 | tf_op jit(solution)/shard_map/all_to_all | solution.py:659
  21.7 2.1 copy.38
  28.2 17.8 %all-to-all-done.r_ref = bf16[16,432,128]{2,1,0:T(8,128)(2,1)} async-done(((bf16[16,432,128]{2,1,0:T(8,128)(2,1)}), bf16[16,432,128]{2,1,0:T(8,128)(2,1)}, u32[]{:S(2)}, u32[]{:S(2)}) %all-to-all-start) | async-done | bytes 1769504 | tf_op jit(solution)/shard_map/all_to_all | solution.py:659
  46.1 11.1 %enter.1 = (bf16[864,1024]{1,0:T(8,128)(2,1)}, bf16[864,1024]{1,0:T(8,128)(2,1)}, bf16[1024,864]{1,0:T(8,128)(2,1)}) custom-call(bf16[16,432,128]{2,1,0:T(8,128)(2,1)} %all-to-all-done.r_ref, f32[1,1024]{1,0:T(1,128)} %bitcast.140, bf16[1024,1024]{1,0:T(8,128)(2,1)} %fusion.pick_ref), custom_call_target="tpu_custom_call" | custom-call | flops 300000000 | bytes 900000 | tf_op jit(solution)/shard_map/enter/pallas_call | solution.py:129
  57.2 15.0 %attend.4 = (bf16[864,256]{1,0:T(8,128)(2,1)}, bf16[864,768]{1,0:T(8,128)(2,1)}, f32[512,1024]{1,0:T(8,128)}, f32[512,1024]{1,0:T(8,128)}) custom-call(bf16[864,1024]{1,0:T(8,128)(2,1)} %get-tuple-element.41.refs_0_, bf16[1024,864]{1,0:T(8,128)(2,1)} %get-tuple-element.42.refs_1_, bf16[864,1024]{1,0:T(8,128)(2,1)} %reshape.420.refs_2_, ...), custom_call_target="tpu_custom_call" | custom-call | flops 800000000 | bytes 1500000 | tf_op jit(solution)/shard_map/attend/pallas_call | solution.py:213
  72.1 4.4 %collective-permute-done = f32[512,1024]{1,0:T(8,128)S(1)} collective-permute-done((f32[512,1024]{1,0:T(8,128)}, f32[512,1024]{1,0:T(8,128)S(1)}, u32[]{:S(2)}, u32[]{:S(2)}) %collective-permute-start) | collective-permute-done | bytes 2097184 | tf_op jit(solution)/shard_map/ppermute | solution.py:677
  80.3 15.2 %attend.5 = (bf16[864,256]{1,0:T(8,128)(2,1)}, bf16[864,768]{1,0:T(8,128)(2,1)}, f32[512,1024]{1,0:T(8,128)}, f32[512,1024]{1,0:T(8,128)}) custom-call(bf16[864,1024]{1,0:T(8,128)(2,1)} %get-tuple-element.41.refs_0_, bf16[1024,864]{1,0:T(8,128)(2,1)} %get-tuple-element.42.refs_1_, bf16[864,1024]{1,0:T(8,128)(2,1)} %reshape.420.refs_2_, ...), custom_call_target="tpu_custom_call" | custom-call | flops 800000000 | bytes 1500000 | tf_op jit(solution)/shard_map/attend/pallas_call | solution.py:213
  95.7 15.0 %attend.6 = (bf16[864,256]{1,0:T(8,128)(2,1)}, bf16[864,768]{1,0:T(8,128)(2,1)}, f32[512,1024]{1,0:T(8,128)}, f32[512,1024]{1,0:T(8,128)}) custom-call(bf16[864,1024]{1,0:T(8,128)(2,1)} %get-tuple-element.41.refs_0_, bf16[1024,864]{1,0:T(8,128)(2,1)} %get-tuple-element.42.refs_1_, bf16[864,1024]{1,0:T(8,128)(2,1)} %reshape.420.refs_2_, ...), custom_call_target="tpu_custom_call" | custom-call | flops 800000000 | bytes 1500000 | tf_op jit(solution)/shard_map/attend/pallas_call | solution.py:213
  113.3 3.9 %ordered_sum.4.refs_10_ = f32[4,128,1024]{2,1,0:T(8,128)} custom-call(s32[1]{0:T(128)} %bitcast.6.y_ref, f32[4,128,1024]{2,1,0:T(8,128)S(1)} %bitcast.118, f32[4,128,1024]{2,1,0:T(8,128)} %bitcast.10.b_ref, bf16[864,256]{1,0:T(8,128)(2,1)S(1)} %copy-done.14), custom_call_target="tpu_custom_call" | custom-call | bytes 500000 | tf_op jit(solution)/shard_map/ordered_sum/pallas_call | solution.py:517
  118.0 15.0 %attend.7 = (bf16[864,256]{1,0:T(8,128)(2,1)}, bf16[864,768]{1,0:T(8,128)(2,1)}, f32[512,1024]{1,0:T(8,128)}, f32[512,1024]{1,0:T(8,128)}) custom-call(bf16[864,1024]{1,0:T(8,128)(2,1)} %get-tuple-element.41.refs_0_, bf16[1024,864]{1,0:T(8,128)(2,1)} %get-tuple-element.42.refs_1_, bf16[864,1024]{1,0:T(8,128)(2,1)} %reshape.420.refs_2_, ...), custom_call_target="tpu_custom_call" | custom-call | flops 800000000 | bytes 1500000 | tf_op jit(solution)/shard_map/attend/pallas_call | solution.py:213
  133.0 12.1 %product.1.refs_1_.refs_0_ = f32[864,1024]{1,0:T(8,128)} custom-call(bf16[864,768]{1,0:T(8,128)(2,1)} %get-tuple-element.52.refs_0_, bf16[864,768]{1,0:T(8,128)(2,1)} %get-tuple-element.53.refs_1_, bf16[864,768]{1,0:T(8,128)(2,1)} %get-tuple-element.54.refs_2_, bf16[864,768]{1,0:T(8,128)(2,1)} %get-tuple-element.55.refs_3_, bf16[1024,3072]{1,0:T(8,128)(2,1)} %refs_4_.9), custom_call_target="tpu_custom_call" | custom-call | flops 600000000 | bytes 1500000 | tf_op jit(solution)/shard_map/product/pallas_call | solution.py:306
  145.1 2.0 copy-done
  148.7 2.7 %ordered_sum.5.refs_8_ = f32[4,128,1024]{2,1,0:T(8,128)S(1)} custom-call(s32[1]{0:T(128)} %bitcast.6.y_ref, f32[4,128,1024]{2,1,0:T(8,128)S(1)} %bitcast.115, f32[4,128,1024]{2,1,0:T(8,128)} %bitcast.18.b_ref, f32[864,1024]{1,0:T(8,128)S(1)} %copy-done), custom_call_target="tpu_custom_call" | custom-call | bytes 500000 | tf_op jit(solution)/shard_map/ordered_sum/pallas_call | solution.py:517
  153.0 4.2 %collective-permute-done.2 = f32[512,1024]{1,0:T(8,128)S(1)} collective-permute-done((f32[512,1024]{1,0:T(8,128)}, f32[512,1024]{1,0:T(8,128)S(1)}, u32[]{:S(2)}, u32[]{:S(2)}) %collective-permute-start.2) | collective-permute-done | bytes 2097184 | tf_op jit(solution)/shard_map/ppermute | solution.py:677
  162.3 2.5 collective-permute-start.5
  164.8 2.2 fusion.1.refs_4_
  167.0 10.5 %leave.1.refs_6_.refs_2_ = bf16[16,448,128]{2,1,0:T(8,128)(2,1)} custom-call(f32[864,1024]{1,0:T(8,128)} %product.1.refs_1_.refs_0_, bf16[864,1024]{1,0:T(8,128)(2,1)} %get-tuple-element.51.refs_1_.refs_4_, bf16[864,1024]{1,0:T(8,128)(2,1)} %reshape.420.refs_2_, f32[1,1024]{1,0:T(1,128)} %bitcast.141, bf16[1024,1024]{1,0:T(8,128)(2,1)} %fusion.1.refs_4_, ...), custom_call_target="tpu_custom_call" | custom-call | flops 400000000 | bytes 1000000 | tf_op jit(solution)/shard_map/leave/pallas_call | solution.py:364
  177.5 4.5 %all-to-all-start.1 = ((bf16[16,448,128]{2,1,0:T(8,128)(2,1)}), bf16[16,448,128]{2,1,0:T(8,128)(2,1)}, u32[]{:S(2)}, u32[]{:S(2)}) async-start(bf16[16,448,128]{2,1,0:T(8,128)(2,1)} %leave.1.refs_6_.refs_2_), calls=%async_computation.3 | async-start | bytes 3670016 | tf_op jit(solution)/shard_map/all_to_all | solution.py:695
  185.3 2.1 fusion.3
  192.1 5.2 %collective-permute-done.6 = f32[16,8,512]{2,1,0:T(8,128)S(1)} collective-permute-done((f32[16,8,512]{2,1,0:T(8,128)}, f32[16,8,512]{2,1,0:T(8,128)S(1)}, u32[]{:S(2)}, u32[]{:S(2)}) %collective-permute-start.6) | collective-permute-done | bytes 262176 | tf_op jit(solution)/shard_map/ppermute | solution.py:500
  202.4 6.1 %block_sum.1.refs_2_ = bf16[864,1024]{1,0:T(8,128)(2,1)} custom-call(bf16[864,256]{1,0:T(8,128)(2,1)} %get-tuple-element.43.refs_0_, bf16[864,256]{1,0:T(8,128)(2,1)} %get-tuple-element.44.refs_1_, bf16[864,256]{1,0:T(8,128)(2,1)} %get-tuple-element.47.refs_0_.refs_2_, bf16[864,256]{1,0:T(8,128)(2,1)} %get-tuple-element.50.refs_3_, ...), custom_call_target="tpu_custom_call" | custom-call | flops 200000000 | bytes 800000 | tf_op jit(solution)/shard_map/block_sum/pallas_call | solution.py:279
  208.5 2.0 collective-permute-done.8
  210.5 3.9 %join_pieces.1 = (bf16[2,12,64,576]{3,2,1,0:T(8,128)(2,1)}, f32[1,128]{1,0:T(1,128)}, f32[2,1,4,8,1024]{4,3,2,1,0:T(8,128)}) custom-call(bf16[16,448,128]{2,1,0:T(8,128)(2,1)} %all-to-all-done.1.refs_0_, f32[2,1,4,8,1024]{4,3,2,1,0:T(8,128)} %bitcast.31.refs_1_, bf16[864,1024]{1,0:T(8,128)(2,1)} %block_sum.1.refs_2_), custom_call_target="tpu_custom_call", output_to_operand_aliasing={{2}: (1, {})} | custom-call | flops 200000000 | bytes 400000 | tf_op jit(solution)/shard_map/join_pieces/pallas_call | solution.py:404
  218.5 2.9 %collective-permute-start.11 = (f32[4,8,1024]{2,1,0:T(8,128)S(1)}, f32[4,8,1024]{2,1,0:T(8,128)S(1)}, u32[]{:S(2)}, u32[]{:S(2)}) collective-permute-start(f32[4,8,1024]{2,1,0:T(8,128)S(1)} %pad_maximum_fusion.3), channel_id=1, source_target_pairs={{0,12},{1,13},{2,14},{3,15},{4,8},{5,9},{6,10},{7,11},{8,4},{9,5},... | collective-permute-start | bytes 393224 | tf_op jit(solution)/shard_map/ppermute | solution.py:500
  221.5 3.3 %collective-permute-done.11 = f32[4,8,1024]{2,1,0:T(8,128)S(1)} collective-permute-done((f32[4,8,1024]{2,1,0:T(8,128)S(1)}, f32[4,8,1024]{2,1,0:T(8,128)S(1)}, u32[]{:S(2)}, u32[]{:S(2)}) %collective-permute-start.11) | collective-permute-done | bytes 131104 | tf_op jit(solution)/shard_map/ppermute | solution.py:500
  224.8 3.1 %collective-permute-done.10 = f32[4,8,3072]{2,1,0:T(8,128)S(1)} collective-permute-done((f32[4,8,3072]{2,1,0:T(8,128)S(1)}, f32[4,8,3072]{2,1,0:T(8,128)S(1)}, u32[]{:S(2)}, u32[]{:S(2)}) %collective-permute-start.10) | collective-permute-done | bytes 393248 | tf_op jit(solution)/shard_map/ppermute | solution.py:500
  234.4 3.6 %collective-permute-start.13 = (f32[8,4096]{1,0:T(8,128)S(1)}, f32[8,4096]{1,0:T(8,128)S(1)}, u32[]{:S(2)}, u32[]{:S(2)}) collective-permute-start(f32[8,4096]{1,0:T(8,128)S(1)} %get-tuple-element.68), channel_id=1, source_target_pairs={{0,2},{1,3},{2,0},{3,1},{4,6},{5,7},{6,4},{7,5},{8,10},{9,11},{10,... | collective-permute-start | bytes 393224 | tf_op jit(solution)/shard_map/ppermute | solution.py:713
  238.3 4.8 %collective-permute-done.13.got2 = f32[8,4096]{1,0:T(8,128)S(1)} collective-permute-done((f32[8,4096]{1,0:T(8,128)S(1)}, f32[8,4096]{1,0:T(8,128)S(1)}, u32[]{:S(2)}, u32[]{:S(2)}) %collective-permute-start.13) | collective-permute-done | bytes 131104 | tf_op jit(solution)/shard_map/ppermute | solution.py:713
  247.0 2.9 %collective-permute-start.17 = (f32[8,384]{1,0:T(8,128)S(1)}, f32[8,384]{1,0:T(8,128)S(1)}, u32[]{:S(2)}, u32[]{:S(2)}) collective-permute-start(f32[8,384]{1,0:T(8,128)S(1)} %get-tuple-element.74), channel_id=1, source_target_pairs={{0,96},{1,97},{2,98},{3,99},{4,100},{5,101},{6,102},{7,103},{8,104... | collective-permute-start | bytes 36872 | tf_op jit(solution)/shard_map/ppermute | solution.py:715
  249.9 2.4 reshape.429
  252.3 3.1 %copy.34 = bf16[2,2,6,3,12,1024]{5,0,4,3,2,1:T(2,128)(2,1)} copy(bf16[2,2,6,3,12,1024]{5,4,2,0,3,1:T(8,128)(2,1)S(1)} %bitcast.127) | data formatting | bytes 3538944 | tf_op jit(solution)/shard_map/transpose | solution.py:719
  (113 shorter events, 51.9 us)
Async XLA Ops:
  12.9 7.4 %copy-start.22 = (s32[2,12,576]{2,0,1:T(2,128)S(1)}, s32[2,12,576]{2,0,1:T(2,128)}, u32[]{:S(2)}) copy-start(s32[2,12,576]{2,0,1:T(2,128)} %param.7) | copy-start | bytes 165892
  12.9 7.6 %slice-start = ((s32[2,12,576]{2,0,1:T(2,128)}), s32[2,12,6]{2,0,1:T(2,128)S(1)}, s32[]{:S(2)}) async-start(s32[2,12,576]{2,0,1:T(2,128)} %param.7), calls=%async_computation.8 | async-start | bytes 24576 | tf_op jit(solution)/shard_map/jit(_roll_static)/slice | solution.py:662
  12.9 33.2 %all-to-all-start = ((bf16[16,432,128]{2,1,0:T(8,128)(2,1)}), bf16[16,432,128]{2,1,0:T(8,128)(2,1)}, u32[]{:S(2)}, u32[]{:S(2)}) async-start(bf16[16,432,128]{2,1,0:T(8,128)(2,1)} %split_pieces.1), calls=%async_computation | async-start | bytes 3538944 | tf_op jit(solution)/shard_map/all_to_all | solution.py:659
  20.2 97.8 %reduce-scatter.4.cloned.1.call-start = ((), (), s32[]{:S(2)}) async-start(), calls=%async_computation.5 | async-start | bytes 2621440 | tf_op jit(solution)/shard_map/reduce_scatter | solution.py:477
  72.1 4.4 %collective-permute-start = (f32[512,1024]{1,0:T(8,128)}, f32[512,1024]{1,0:T(8,128)S(1)}, u32[]{:S(2)}, u32[]{:S(2)}) collective-permute-start(f32[512,1024]{1,0:T(8,128)} %get-tuple-element.46), channel_id=1, source_target_pairs={{0,1},{1,0},{2,3},{3,2},{4,5},{5,4},{6,7},{7,6},{8,9},{9,8},{10,11... | collective-permute-start | bytes 6291464 | tf_op jit(solution)/shard_map/ppermute | solution.py:677
  80.1 86.9 %reduce-scatter.6.cloned.1.call-start = ((), (), s32[]{:S(2)}) async-start(), calls=%async_computation.6 | async-start | bytes 2621440 | tf_op jit(solution)/shard_map/reduce_scatter | solution.py:477
  95.5 15.2 %collective-permute-start.1 = (f32[512,1024]{1,0:T(8,128)}, f32[512,1024]{1,0:T(8,128)}, u32[]{:S(2)}, u32[]{:S(2)}) collective-permute-start(f32[512,1024]{1,0:T(8,128)} %get-tuple-element.49), channel_id=1, source_target_pairs={{0,1},{1,0},{2,3},{3,2},{4,5},{5,4},{6,7},{7,6},{8,9},{9,8},{10,11... | collective-permute-start | bytes 6291464 | tf_op jit(solution)/shard_map/ppermute | solution.py:677
  117.2 71.2 %reduce-scatter.8.cloned.1.call-start = ((), (), s32[]{:S(2)}) async-start(), calls=%async_computation.7 | async-start | bytes 2621440 | tf_op jit(solution)/shard_map/reduce_scatter | solution.py:477
  117.3 27.8 %collective-permute-start.3 = (f32[512,1024]{1,0:T(8,128)}, f32[512,1024]{1,0:T(8,128)}, u32[]{:S(2)}, u32[]{:S(2)}) collective-permute-start(f32[512,1024]{1,0:T(8,128)} %get-tuple-element.60), channel_id=1, source_target_pairs={{0,1},{1,0},{2,3},{3,2},{4,5},{5,4},{6,7},{7,6},{8,9},{9,8},{10,11... | collective-permute-start | bytes 6291464 | tf_op jit(solution)/shard_map/ppermute | solution.py:677
  148.7 8.5 %copy-start.1 = (f32[864,1024]{1,0:T(8,128)S(1)}, f32[864,1024]{1,0:T(8,128)}, u32[]{:S(2)}) copy-start(f32[864,1024]{1,0:T(8,128)} %product.1.refs_1_.refs_0_) | copy-start | bytes 10616836
  152.8 4.5 %collective-permute-start.2 = (f32[512,1024]{1,0:T(8,128)}, f32[512,1024]{1,0:T(8,128)S(1)}, u32[]{:S(2)}, u32[]{:S(2)}) collective-permute-start(f32[512,1024]{1,0:T(8,128)} %get-tuple-element.57), channel_id=1, source_target_pairs={{0,1},{1,0},{2,3},{3,2},{4,5},{5,4},{6,7},{7,6},{8,9},{9,8},{10,11... | collective-permute-start | bytes 6291464 | tf_op jit(solution)/shard_map/ppermute | solution.py:677
  160.4 24.3 %collective-permute-start.4 = (f32[32,8,512]{2,1,0:T(8,128)}, f32[32,8,512]{2,1,0:T(8,128)S(1)}, u32[]{:S(2)}, u32[]{:S(2)}) collective-permute-start(f32[32,8,512]{2,1,0:T(8,128)} %bitcast.14.refs_5_), channel_id=1, source_target_pairs={{0,32},{1,33},{2,34},{3,35},{4,36},{5,37},{6,38},{7,39},{8,40},{9,... | collective-permute-start | bytes 1572872 | tf_op jit(solution)/shard_map/ppermute | solution.py:500
  162.3 22.4 %collective-permute-start.5 = (f32[32,8,512]{2,1,0:T(8,128)}, f32[32,8,512]{2,1,0:T(8,128)S(1)}, u32[]{:S(2)}, u32[]{:S(2)}) collective-permute-start(f32[32,8,512]{2,1,0:T(8,128)} %bitcast.15.refs_6_), channel_id=1, source_target_pairs={{0,96},{1,97},{2,98},{3,99},{4,100},{5,101},{6,102},{7,103},{8,104... | collective-permute-start | bytes 1572872 | tf_op jit(solution)/shard_map/ppermute | solution.py:500
  177.5 7.2 %copy-start.4 = (bf16[16,448,128]{2,1,0:T(8,128)(2,1)S(1)}, bf16[16,448,128]{2,1,0:T(8,128)(2,1)}, u32[]{:S(2)}) copy-start(bf16[16,448,128]{2,1,0:T(8,128)(2,1)} %leave.1.refs_6_.refs_2_) | copy-start | bytes 5505028
  177.5 33.0 %all-to-all-start.1 = ((bf16[16,448,128]{2,1,0:T(8,128)(2,1)}), bf16[16,448,128]{2,1,0:T(8,128)(2,1)}, u32[]{:S(2)}, u32[]{:S(2)}) async-start(bf16[16,448,128]{2,1,0:T(8,128)(2,1)} %leave.1.refs_6_.refs_2_), calls=%async_computation.3 | async-start | bytes 3670016 | tf_op jit(solution)/shard_map/all_to_all | solution.py:695
  185.3 4.1 %copy-start.21 = (f32[1,2,4,8,1024]{4,3,2,1,0:T(8,128)S(1)}, f32[1,2,4,8,1024]{4,3,2,1,0:T(8,128)}, u32[]{:S(2)}) copy-start(f32[1,2,4,8,1024]{4,3,2,1,0:T(8,128)} %slice.182) | copy-start | bytes 786436
  187.4 9.9 %collective-permute-start.6 = (f32[16,8,512]{2,1,0:T(8,128)}, f32[16,8,512]{2,1,0:T(8,128)S(1)}, u32[]{:S(2)}, u32[]{:S(2)}) collective-permute-start(f32[16,8,512]{2,1,0:T(8,128)} %bitcast.23), channel_id=1, source_target_pairs={{0,96},{1,97},{2,98},{3,99},{4,100},{5,101},{6,102},{7,103},{8,104... | collective-permute-start | bytes 786440 | tf_op jit(solution)/shard_map/ppermute | solution.py:500
  188.1 9.9 %collective-permute-start.7 = (f32[16,8,512]{2,1,0:T(8,128)S(1)}, f32[16,8,512]{2,1,0:T(8,128)S(1)}, u32[]{:S(2)}, u32[]{:S(2)}) collective-permute-start(f32[16,8,512]{2,1,0:T(8,128)S(1)} %bitcast.138), channel_id=1, source_target_pairs={{0,32},{1,33},{2,34},{3,35},{4,36},{5,37},{6,38},{7,39},{8,40},{9,... | collective-permute-start | bytes 786440 | tf_op jit(solution)/shard_map/ppermute | solution.py:500
  190.4 24.0 %collective-permute-start.9 = (f32[8,8,3072]{2,1,0:T(8,128)}, f32[8,8,3072]{2,1,0:T(8,128)S(1)}, u32[]{:S(2)}, u32[]{:S(2)}) collective-permute-start(f32[8,8,3072]{2,1,0:T(8,128)} %pad_maximum_fusion), channel_id=1, source_target_pairs={{0,32},{1,33},{2,34},{3,35},{4,36},{5,37},{6,38},{7,39},{8,40},{9,... | collective-permute-start | bytes 2359304 | tf_op jit(solution)/shard_map/ppermute | solution.py:500
  200.7 9.8 %collective-permute-start.8 = (f32[8,8,1024]{2,1,0:T(8,128)}, f32[8,8,1024]{2,1,0:T(8,128)}, u32[]{:S(2)}, u32[]{:S(2)}) collective-permute-start(f32[8,8,1024]{2,1,0:T(8,128)} %pad_maximum_fusion.2), channel_id=1, source_target_pairs={{0,4},{1,5},{2,6},{3,7},{4,0},{5,1},{6,2},{7,3},{8,12},{9,13},{10,... | collective-permute-start | bytes 786440 | tf_op jit(solution)/shard_map/ppermute | solution.py:500
  214.4 13.5 %copy-start.3 = (f32[4,4,4,8,1024]{4,3,2,1,0:T(8,128)S(1)}, f32[4,4,4,8,1024]{4,3,2,1,0:T(8,128)}, u32[]{:S(2)}) copy-start(f32[4,4,4,8,1024]{4,3,2,1,0:T(8,128)} %copy-done.2) | copy-start | bytes 6291460
  214.4 13.5 %copy-start.8 = (f32[128,1024]{1,0:T(8,128)S(1)}, f32[128,1024]{1,0:T(8,128)}, u32[]{:S(2)}) copy-start(f32[128,1024]{1,0:T(8,128)} %reduce-scatter.4.cloned.1.call-done.refs_11_) | copy-start | bytes 1572868
  214.4 13.5 %copy-start.17 = (f32[16,8,512]{2,1,0:T(8,128)S(1)}, f32[16,8,512]{2,1,0:T(8,128)}, u32[]{:S(2)}) copy-start(f32[16,8,512]{2,1,0:T(8,128)} %copy-done.16) | copy-start | bytes 786436
  214.4 13.5 %copy-start.20 = (f32[1,128]{1,0:T(1,128)S(1)}, f32[1,128]{1,0:T(1,128)}, u32[]{:S(2)}) copy-start(f32[1,128]{1,0:T(1,128)} %get-tuple-element.65.refs_21_.gain_ref) | copy-start | bytes 1540
  215.7 12.2 %collective-permute-start.10 = (f32[4,8,3072]{2,1,0:T(8,128)S(1)}, f32[4,8,3072]{2,1,0:T(8,128)S(1)}, u32[]{:S(2)}, u32[]{:S(2)}) collective-permute-start(f32[4,8,3072]{2,1,0:T(8,128)S(1)} %pad_maximum_fusion.1), channel_id=1, source_target_pairs={{0,96},{1,97},{2,98},{3,99},{4,100},{5,101},{6,102},{7,103},{8,104... | collective-permute-start | bytes 1179656 | tf_op jit(solution)/shard_map/ppermute | solution.py:500
  218.5 6.3 %collective-permute-start.11 = (f32[4,8,1024]{2,1,0:T(8,128)S(1)}, f32[4,8,1024]{2,1,0:T(8,128)S(1)}, u32[]{:S(2)}, u32[]{:S(2)}) collective-permute-start(f32[4,8,1024]{2,1,0:T(8,128)S(1)} %pad_maximum_fusion.3), channel_id=1, source_target_pairs={{0,12},{1,13},{2,14},{3,15},{4,8},{5,9},{6,10},{7,11},{8,4},{9,5},... | collective-permute-start | bytes 393224 | tf_op jit(solution)/shard_map/ppermute | solution.py:500
  233.6 11.0 %collective-permute-start.12 = (f32[8,4224]{1,0:T(8,128)S(1)}, f32[8,4224]{1,0:T(8,128)S(1)}, u32[]{:S(2)}, u32[]{:S(2)}) collective-permute-start(f32[8,4224]{1,0:T(8,128)S(1)} %get-tuple-element.67), channel_id=1, source_target_pairs={{0,16},{1,17},{2,18},{3,19},{4,20},{5,21},{6,22},{7,23},{8,24},{9,... | collective-permute-start | bytes 405512 | tf_op jit(solution)/shard_map/ppermute | solution.py:713
  234.4 8.7 %collective-permute-start.13 = (f32[8,4096]{1,0:T(8,128)S(1)}, f32[8,4096]{1,0:T(8,128)S(1)}, u32[]{:S(2)}, u32[]{:S(2)}) collective-permute-start(f32[8,4096]{1,0:T(8,128)S(1)} %get-tuple-element.68), channel_id=1, source_target_pairs={{0,2},{1,3},{2,0},{3,1},{4,6},{5,7},{6,4},{7,5},{8,10},{9,11},{10,... | collective-permute-start | bytes 393224 | tf_op jit(solution)/shard_map/ppermute | solution.py:713
  238.0 6.6 %collective-permute-start.14 = (f32[8,4096]{1,0:T(8,128)S(1)}, f32[8,4096]{1,0:T(8,128)S(1)}, u32[]{:S(2)}, u32[]{:S(2)}) collective-permute-start(f32[8,4096]{1,0:T(8,128)S(1)} %get-tuple-element.69), channel_id=1, source_target_pairs={{0,18},{1,19},{2,16},{3,17},{4,22},{5,23},{6,20},{7,21},{8,26},{9,... | collective-permute-start | bytes 393224 | tf_op jit(solution)/shard_map/ppermute | solution.py:713
  245.2 10.2 %collective-permute-start.15 = (f32[8,384]{1,0:T(8,128)S(1)}, f32[8,384]{1,0:T(8,128)S(1)}, u32[]{:S(2)}, u32[]{:S(2)}) collective-permute-start(f32[8,384]{1,0:T(8,128)S(1)} %get-tuple-element.72), channel_id=1, source_target_pairs={{0,32},{1,33},{2,34},{3,35},{4,36},{5,37},{6,38},{7,39},{8,40},{9,... | collective-permute-start | bytes 36872 | tf_op jit(solution)/shard_map/ppermute | solution.py:715
  245.2 10.2 %collective-permute-start.16 = (f32[8,384]{1,0:T(8,128)S(1)}, f32[8,384]{1,0:T(8,128)S(1)}, u32[]{:S(2)}, u32[]{:S(2)}) collective-permute-start(f32[8,384]{1,0:T(8,128)S(1)} %get-tuple-element.73), channel_id=1, source_target_pairs={{0,64},{1,65},{2,66},{3,67},{4,68},{5,69},{6,70},{7,71},{8,72},{9,... | collective-permute-start | bytes 36872 | tf_op jit(solution)/shard_map/ppermute | solution.py:715
  247.0 8.4 %collective-permute-start.17 = (f32[8,384]{1,0:T(8,128)S(1)}, f32[8,384]{1,0:T(8,128)S(1)}, u32[]{:S(2)}, u32[]{:S(2)}) collective-permute-start(f32[8,384]{1,0:T(8,128)S(1)} %get-tuple-element.74), channel_id=1, source_target_pairs={{0,96},{1,97},{2,98},{3,99},{4,100},{5,101},{6,102},{7,103},{8,104... | collective-permute-start | bytes 36872 | tf_op jit(solution)/shard_map/ppermute | solution.py:715
  (15 other events, 20.1 us)
Sparse Core Ops, SparseCore 0:
  80.2 28.2 reduce-scatter.3
  117.4 28.2 reduce-scatter.5
  152.9 28.2 reduce-scatter.7

commit v6 on v5

--- a/solution.py
+++ b/solution.py
@@ -82,7 +82,7 @@
         in_specs=vmem(1),
         out_specs=vmem(1)[0],
         scratch_shapes=[pltpu.VMEM((LON, 128), F32), pltpu.VMEM((16, 6 * HALF, 128), F32)],
-        compiler_params=params(32),
+        compiler_params=params(62),
         cost_estimate=cost(2e9, 4e6),
         name="split_pieces",
     )(z)
@@ -281,7 +281,7 @@
         out_shape=jax.ShapeDtypeStruct((TOK, D), BF16),
         in_specs=vmem(6) + waits(after),
         out_specs=vmem(1)[0],
-        compiler_params=params(62),
+        compiler_params=params(32),
         cost_estimate=cost(2e9, 8e6),
         name="block_sum",
     )(*att, x, out_weight, *after)
@@ -308,7 +308,7 @@
         out_shape=jax.ShapeDtypeStruct((TOK, D), F32),
         in_specs=vmem(5) + waits(after),
         out_specs=vmem(1)[0],
-        compiler_params=params(62),
+        compiler_params=params(40),
         cost_estimate=cost(6e9, 15e6),
         name="product",
     )(*grads, qkv_weight, *after)
@@ -685,9 +685,8 @@
     s2 = heads(2, (total,))
     total = s1.ring_y(y_index, (att[2],))
     s3 = heads(3, (total, s0.reduced))
+    total = s2.ring_y(y_index, (att[3],))
     norm_grad = product(grads, qkv_weight)
-    total = s2.ring_y(y_index, (norm_grad,))
-    s3.terms[-1] = (gate([newest(s3)], (norm_grad,))[0],) + s3.terms[-1][1:]
     s3, s4 = s3.columns(0, 2 * GW), s3.columns(2 * GW, 4 * GW)
     out3, _ = exchange([s3], "z", 1)
     out4, _ = exchange([s4], "z", 3)

time: 264 us -> 264 us (level)
  local copies, waits for them, and re-layouts: 33 us -> 38.3 us
  Pallas kernels: 120 us -> 115 us
    pallas_call x1, Pallas kernels: 6.11 us -> 2.18 us  [block_sum(): pl.pallas_call(behind(block_kernel, len(after), 6), out_shape=jax.ShapeDt...]
    pallas_call x1, Pallas kernels: 12.1 us -> 8.65 us  [product(): pl.pallas_call(behind(product_kernel, len(after), 5), out_shape=jax.Shape...]
    unnamed x46 -> x68, local copies, waits for them, and re-layouts: 18.1 us -> 21.2 us
  transfers between devices with their start and end apart: 23 -> 23, of which waited for: 9 -> 10; matrix products, arithmetic and copies ran while one was open for 10% -> 11% of each run, Pallas kernels for 33% -> 30%
where the time goes in v6:
time: 264 us; the launch traced here: 263 us
  Pallas kernels  115 us (44%)
  waiting for transfers between devices  45.7 us (17%)
  local copies, waits for them, and re-layouts  38.3 us (15%)
  starting transfers between devices  35.6 us (13%)
  other arithmetic  14.1 us (5%)
  between operations  14.1 us (5%)
    pallas_call x4, Pallas kernels, attend(): pl.pallas_call(behind(attend_kernel, len(after), 10), grid=(1,), out_shap...  60.4 us
    unnamed x68, local copies, waits for them, and re-layouts  21.2 us
    all_to_all x1, waiting for transfers between devices, per_device(): lax.all_to_all(pieces, 'lon', split_axis=0, concat_axis=0, tiled=True)  17.8 us
    ppermute x8, starting transfers between devices, exchange(): got = lax.ppermute(out, AXES, swapped(**{name: by}))  13.2 us
    ppermute x8, waiting for transfers between devices, exchange(): got = lax.ppermute(out, AXES, swapped(**{name: by}))  13 us
    pallas_call x1, Pallas kernels, enter(): pl.pallas_call(enter_kernel, out_shape=(jax.ShapeDtypeStruct((TOK, D), BF...  11.1 us
    pallas_call x1, Pallas kernels, leave(): pl.pallas_call(behind(leave_kernel, len(after), 5), grid=(3,), out_shape=...  10.5 us
    pallas_call x3, Pallas kernels, ordered_sum(): pl.pallas_call(add_kernel, grid_spec=pltpu.PrefetchScalarGridSpec(num_sca...  9.64 us
  transfers between devices with their start and end apart: 23, of which 10 were waited for; matrix products, arithmetic and copies ran while one was open for 11% of the time, Pallas kernels for 30%

profile of v6, /device:TPU:0, one launch (start us, length us, event | category | flops | bytes accessed | tf_op | source)
XLA Modules:
  0.0 263.0 jit_solution(4533128493142849044)
XLA Ops:
  7.2 5.8 %split_pieces.1 = bf16[16,432,128]{2,1,0:T(8,128)(2,1)} custom-call(bf16[2,12,64,576]{3,2,1,0:T(8,128)(2,1)} %bitcast.132), custom_call_target="tpu_custom_call" | custom-call | flops 200000000 | bytes 400000 | tf_op jit(solution)/shard_map/split_pieces/pallas_call | solution.py:79
  13.0 7.3 %all-to-all-start = ((bf16[16,432,128]{2,1,0:T(8,128)(2,1)}), bf16[16,432,128]{2,1,0:T(8,128)(2,1)}, u32[]{:S(2)}, u32[]{:S(2)}) async-start(bf16[16,432,128]{2,1,0:T(8,128)(2,1)} %split_pieces.1), calls=%async_computation | async-start | bytes 3538944 | tf_op jit(solution)/shard_map/all_to_all | solution.py:659
  21.7 2.1 copy.37
  28.3 17.8 %all-to-all-done.r_ref = bf16[16,432,128]{2,1,0:T(8,128)(2,1)} async-done(((bf16[16,432,128]{2,1,0:T(8,128)(2,1)}), bf16[16,432,128]{2,1,0:T(8,128)(2,1)}, u32[]{:S(2)}, u32[]{:S(2)}) %all-to-all-start) | async-done | bytes 1769504 | tf_op jit(solution)/shard_map/all_to_all | solution.py:659
  46.1 11.1 %enter.1 = (bf16[864,1024]{1,0:T(8,128)(2,1)}, bf16[864,1024]{1,0:T(8,128)(2,1)}, bf16[1024,864]{1,0:T(8,128)(2,1)}) custom-call(bf16[16,432,128]{2,1,0:T(8,128)(2,1)} %all-to-all-done.r_ref, f32[1,1024]{1,0:T(1,128)} %bitcast.143, bf16[1024,1024]{1,0:T(8,128)(2,1)} %fusion.pick_ref), custom_call_target="tpu_custom_call" | custom-call | flops 300000000 | bytes 900000 | tf_op jit(solution)/shard_map/enter/pallas_call | solution.py:129
  57.2 15.1 %attend.4 = (bf16[864,256]{1,0:T(8,128)(2,1)}, bf16[864,768]{1,0:T(8,128)(2,1)}, f32[512,1024]{1,0:T(8,128)}, f32[512,1024]{1,0:T(8,128)}) custom-call(bf16[864,1024]{1,0:T(8,128)(2,1)} %get-tuple-element.40.refs_0_, bf16[1024,864]{1,0:T(8,128)(2,1)} %get-tuple-element.41.refs_1_, bf16[864,1024]{1,0:T(8,128)(2,1)} %reshape.416.refs_2_, ...), custom_call_target="tpu_custom_call" | custom-call | flops 800000000 | bytes 1500000 | tf_op jit(solution)/shard_map/attend/pallas_call | solution.py:213
  72.3 4.4 %collective-permute-done = f32[512,1024]{1,0:T(8,128)S(1)} collective-permute-done((f32[512,1024]{1,0:T(8,128)}, f32[512,1024]{1,0:T(8,128)S(1)}, u32[]{:S(2)}, u32[]{:S(2)}) %collective-permute-start) | collective-permute-done | bytes 2097184 | tf_op jit(solution)/shard_map/ppermute | solution.py:677
  80.5 15.1 %attend.5 = (bf16[864,256]{1,0:T(8,128)(2,1)}, bf16[864,768]{1,0:T(8,128)(2,1)}, f32[512,1024]{1,0:T(8,128)}, f32[512,1024]{1,0:T(8,128)}) custom-call(bf16[864,1024]{1,0:T(8,128)(2,1)} %get-tuple-element.40.refs_0_, bf16[1024,864]{1,0:T(8,128)(2,1)} %get-tuple-element.41.refs_1_, bf16[864,1024]{1,0:T(8,128)(2,1)} %reshape.416.refs_2_, ...), custom_call_target="tpu_custom_call" | custom-call | flops 800000000 | bytes 1500000 | tf_op jit(solution)/shard_map/attend/pallas_call | solution.py:213
  95.7 15.0 %attend.6 = (bf16[864,256]{1,0:T(8,128)(2,1)}, bf16[864,768]{1,0:T(8,128)(2,1)}, f32[512,1024]{1,0:T(8,128)}, f32[512,1024]{1,0:T(8,128)}) custom-call(bf16[864,1024]{1,0:T(8,128)(2,1)} %get-tuple-element.40.refs_0_, bf16[1024,864]{1,0:T(8,128)(2,1)} %get-tuple-element.41.refs_1_, bf16[864,1024]{1,0:T(8,128)(2,1)} %reshape.416.refs_2_, ...), custom_call_target="tpu_custom_call" | custom-call | flops 800000000 | bytes 1500000 | tf_op jit(solution)/shard_map/attend/pallas_call | solution.py:213
  113.4 3.8 %ordered_sum.4.refs_10_ = f32[4,128,1024]{2,1,0:T(8,128)} custom-call(s32[1]{0:T(128)} %bitcast.6.y_ref, f32[4,128,1024]{2,1,0:T(8,128)S(1)} %bitcast.123, f32[4,128,1024]{2,1,0:T(8,128)} %bitcast.10.b_ref, bf16[864,256]{1,0:T(8,128)(2,1)S(1)} %copy-done.19), custom_call_target="tpu_custom_call" | custom-call | bytes 500000 | tf_op jit(solution)/shard_map/ordered_sum/pallas_call | solution.py:517
  117.7 15.2 %attend.7 = (bf16[864,256]{1,0:T(8,128)(2,1)}, bf16[864,768]{1,0:T(8,128)(2,1)}, f32[512,1024]{1,0:T(8,128)}, f32[512,1024]{1,0:T(8,128)}) custom-call(bf16[864,1024]{1,0:T(8,128)(2,1)} %get-tuple-element.40.refs_0_, bf16[1024,864]{1,0:T(8,128)(2,1)} %get-tuple-element.41.refs_1_, bf16[864,1024]{1,0:T(8,128)(2,1)} %reshape.416.refs_2_, ...), custom_call_target="tpu_custom_call" | custom-call | flops 800000000 | bytes 1500000 | tf_op jit(solution)/shard_map/attend/pallas_call | solution.py:213
  135.5 3.8 %ordered_sum.5.refs_8_ = f32[4,128,1024]{2,1,0:T(8,128)} custom-call(s32[1]{0:T(128)} %bitcast.6.y_ref, f32[4,128,1024]{2,1,0:T(8,128)S(1)} %bitcast.122, f32[4,128,1024]{2,1,0:T(8,128)} %bitcast.18.b_ref, bf16[864,256]{1,0:T(8,128)(2,1)S(1)} %copy-done.21), custom_call_target="tpu_custom_call" | custom-call | bytes 500000 | tf_op jit(solution)/shard_map/ordered_sum/pallas_call | solution.py:517
  139.6 4.3 %collective-permute-done.2 = f32[512,1024]{1,0:T(8,128)S(1)} collective-permute-done((f32[512,1024]{1,0:T(8,128)}, f32[512,1024]{1,0:T(8,128)S(1)}, u32[]{:S(2)}, u32[]{:S(2)}) %collective-permute-start.2) | collective-permute-done | bytes 2097184 | tf_op jit(solution)/shard_map/ppermute | solution.py:677
  147.5 2.5 collective-permute-start.5
  150.0 2.2 fusion.1.refs_4_
  153.5 8.7 %product.1.refs_0_ = f32[864,1024]{1,0:T(8,128)S(1)} custom-call(bf16[864,768]{1,0:T(8,128)(2,1)S(1)} %copy-done.24, bf16[864,768]{1,0:T(8,128)(2,1)S(1)} %copy-done.25, bf16[864,768]{1,0:T(8,128)(2,1)S(1)} %copy-done.26, bf16[864,768]{1,0:T(8,128)(2,1)S(1)} %copy-done.27, bf16[1024,3072]{1,0:T(8,128)(2,1)} %refs_4_.9), custom_call_target="tpu_custom_call" | custom-call | flops 600000000 | bytes 1500000 | tf_op jit(solution)/shard_map/product/pallas_call | solution.py:306
  164.0 10.5 %leave.1.refs_6_.refs_2_ = bf16[16,448,128]{2,1,0:T(8,128)(2,1)} custom-call(f32[864,1024]{1,0:T(8,128)} %copy-done.8, bf16[864,1024]{1,0:T(8,128)(2,1)} %get-tuple-element.50.refs_1_.refs_4_, bf16[864,1024]{1,0:T(8,128)(2,1)} %reshape.416.refs_2_, f32[1,1024]{1,0:T(1,128)} %bitcast.144, bf16[1024,1024]{1,0:T(8,128)(2,1)} %fusion.1.refs_4_, ...), custom_call_target="tpu_custom_call" | custom-call | flops 400000000 | bytes 1000000 | tf_op jit(solution)/shard_map/leave/pallas_call | solution.py:364
  174.5 4.6 %all-to-all-start.1 = ((bf16[16,448,128]{2,1,0:T(8,128)(2,1)}), bf16[16,448,128]{2,1,0:T(8,128)(2,1)}, u32[]{:S(2)}, u32[]{:S(2)}) async-start(bf16[16,448,128]{2,1,0:T(8,128)(2,1)} %leave.1.refs_6_.refs_2_), calls=%async_computation.3 | async-start | bytes 3670016 | tf_op jit(solution)/shard_map/all_to_all | solution.py:694
  182.3 2.3 fusion.3
  186.8 2.0 pad_maximum_fusion
  190.5 4.0 %collective-permute-done.6 = f32[16,8,512]{2,1,0:T(8,128)S(1)} collective-permute-done((f32[16,8,512]{2,1,0:T(8,128)}, f32[16,8,512]{2,1,0:T(8,128)S(1)}, u32[]{:S(2)}, u32[]{:S(2)}) %collective-permute-start.6) | collective-permute-done | bytes 262176 | tf_op jit(solution)/shard_map/ppermute | solution.py:500
  202.0 2.2 block_sum.1.refs_2_
  205.4 2.0 collective-permute-done.8
  208.1 3.9 %join_pieces.1 = (bf16[2,12,64,576]{3,2,1,0:T(8,128)(2,1)}, f32[1,128]{1,0:T(1,128)}, f32[2,1,4,8,1024]{4,3,2,1,0:T(8,128)}) custom-call(bf16[16,448,128]{2,1,0:T(8,128)(2,1)} %all-to-all-done.1.refs_0_, f32[2,1,4,8,1024]{4,3,2,1,0:T(8,128)} %bitcast.117, bf16[864,1024]{1,0:T(8,128)(2,1)} %copy-done.6), custom_call_target="tpu_custom_call", output_to_operand_aliasing={{2}: (1, {})} | custom-call | flops 200000000 | bytes 400000 | tf_op jit(solution)/shard_map/join_pieces/pallas_call | solution.py:404
  215.7 3.0 %collective-permute-start.11 = (f32[4,8,1024]{2,1,0:T(8,128)S(1)}, f32[4,8,1024]{2,1,0:T(8,128)S(1)}, u32[]{:S(2)}, u32[]{:S(2)}) collective-permute-start(f32[4,8,1024]{2,1,0:T(8,128)S(1)} %pad_maximum_fusion.3), channel_id=1, source_target_pairs={{0,12},{1,13},{2,14},{3,15},{4,8},{5,9},{6,10},{7,11},{8,4},{9,5},... | collective-permute-start | bytes 393224 | tf_op jit(solution)/shard_map/ppermute | solution.py:500
  218.7 3.3 %collective-permute-done.11 = f32[4,8,1024]{2,1,0:T(8,128)S(1)} collective-permute-done((f32[4,8,1024]{2,1,0:T(8,128)S(1)}, f32[4,8,1024]{2,1,0:T(8,128)S(1)}, u32[]{:S(2)}, u32[]{:S(2)}) %collective-permute-start.11) | collective-permute-done | bytes 131104 | tf_op jit(solution)/shard_map/ppermute | solution.py:500
  221.9 3.3 %collective-permute-done.10 = f32[4,8,3072]{2,1,0:T(8,128)S(1)} collective-permute-done((f32[4,8,3072]{2,1,0:T(8,128)S(1)}, f32[4,8,3072]{2,1,0:T(8,128)S(1)}, u32[]{:S(2)}, u32[]{:S(2)}) %collective-permute-start.10) | collective-permute-done | bytes 393248 | tf_op jit(solution)/shard_map/ppermute | solution.py:500
  232.9 3.6 %collective-permute-start.13 = (f32[8,4096]{1,0:T(8,128)S(1)}, f32[8,4096]{1,0:T(8,128)S(1)}, u32[]{:S(2)}, u32[]{:S(2)}) collective-permute-start(f32[8,4096]{1,0:T(8,128)S(1)} %get-tuple-element.66), channel_id=1, source_target_pairs={{0,2},{1,3},{2,0},{3,1},{4,6},{5,7},{6,4},{7,5},{8,10},{9,11},{10,... | collective-permute-start | bytes 393224 | tf_op jit(solution)/shard_map/ppermute | solution.py:712
  236.8 4.8 %collective-permute-done.13.got2 = f32[8,4096]{1,0:T(8,128)S(1)} collective-permute-done((f32[8,4096]{1,0:T(8,128)S(1)}, f32[8,4096]{1,0:T(8,128)S(1)}, u32[]{:S(2)}, u32[]{:S(2)}) %collective-permute-start.13) | collective-permute-done | bytes 131104 | tf_op jit(solution)/shard_map/ppermute | solution.py:712
  245.5 2.9 %collective-permute-start.17 = (f32[8,384]{1,0:T(8,128)S(1)}, f32[8,384]{1,0:T(8,128)S(1)}, u32[]{:S(2)}, u32[]{:S(2)}) collective-permute-start(f32[8,384]{1,0:T(8,128)S(1)} %get-tuple-element.72), channel_id=1, source_target_pairs={{0,96},{1,97},{2,98},{3,99},{4,100},{5,101},{6,102},{7,103},{8,104... | collective-permute-start | bytes 36872 | tf_op jit(solution)/shard_map/ppermute | solution.py:714
  248.4 2.1 reshape.425
  250.5 4.7 %copy.33 = bf16[2,2,6,3,12,1024]{5,0,4,3,2,1:T(2,128)(2,1)} copy(bf16[2,2,6,3,12,1024]{5,4,2,0,3,1:T(8,128)(2,1)} %bitcast.130) | data formatting | bytes 3538944 | tf_op jit(solution)/shard_map/transpose | solution.py:718
  (134 shorter events, 55.6 us)
Async XLA Ops:
  13.0 33.2 %all-to-all-start = ((bf16[16,432,128]{2,1,0:T(8,128)(2,1)}), bf16[16,432,128]{2,1,0:T(8,128)(2,1)}, u32[]{:S(2)}, u32[]{:S(2)}) async-start(bf16[16,432,128]{2,1,0:T(8,128)(2,1)} %split_pieces.1), calls=%async_computation | async-start | bytes 3538944 | tf_op jit(solution)/shard_map/all_to_all | solution.py:659
  20.3 97.4 %reduce-scatter.4.cloned.1.call-start = ((), (), s32[]{:S(2)}) async-start(), calls=%async_computation.5 | async-start | bytes 2621440 | tf_op jit(solution)/shard_map/reduce_scatter | solution.py:477
  72.3 4.4 %collective-permute-start = (f32[512,1024]{1,0:T(8,128)}, f32[512,1024]{1,0:T(8,128)S(1)}, u32[]{:S(2)}, u32[]{:S(2)}) collective-permute-start(f32[512,1024]{1,0:T(8,128)} %get-tuple-element.45), channel_id=1, source_target_pairs={{0,1},{1,0},{2,3},{3,2},{4,5},{5,4},{6,7},{7,6},{8,9},{9,8},{10,11... | collective-permute-start | bytes 6291464 | tf_op jit(solution)/shard_map/ppermute | solution.py:677
  80.3 83.7 %reduce-scatter.6.cloned.1.call-start = ((), (), s32[]{:S(2)}) async-start(), calls=%async_computation.6 | async-start | bytes 2621440 | tf_op jit(solution)/shard_map/reduce_scatter | solution.py:477
  95.6 15.2 %collective-permute-start.1 = (f32[512,1024]{1,0:T(8,128)}, f32[512,1024]{1,0:T(8,128)}, u32[]{:S(2)}, u32[]{:S(2)}) collective-permute-start(f32[512,1024]{1,0:T(8,128)} %get-tuple-element.48), channel_id=1, source_target_pairs={{0,1},{1,0},{2,3},{3,2},{4,5},{5,4},{6,7},{7,6},{8,9},{9,8},{10,11... | collective-permute-start | bytes 6291464 | tf_op jit(solution)/shard_map/ppermute | solution.py:677
  117.2 68.5 %reduce-scatter.8.cloned.1.call-start = ((), (), s32[]{:S(2)}) async-start(), calls=%async_computation.7 | async-start | bytes 2621440 | tf_op jit(solution)/shard_map/reduce_scatter | solution.py:477
  117.3 15.6 %collective-permute-start.3 = (f32[512,1024]{1,0:T(8,128)}, f32[512,1024]{1,0:T(8,128)}, u32[]{:S(2)}, u32[]{:S(2)}) collective-permute-start(f32[512,1024]{1,0:T(8,128)} %get-tuple-element.58), channel_id=1, source_target_pairs={{0,1},{1,0},{2,3},{3,2},{4,5},{5,4},{6,7},{7,6},{8,9},{9,8},{10,11... | collective-permute-start | bytes 6291464 | tf_op jit(solution)/shard_map/ppermute | solution.py:677
  139.4 4.5 %collective-permute-start.2 = (f32[512,1024]{1,0:T(8,128)}, f32[512,1024]{1,0:T(8,128)S(1)}, u32[]{:S(2)}, u32[]{:S(2)}) collective-permute-start(f32[512,1024]{1,0:T(8,128)} %get-tuple-element.56), channel_id=1, source_target_pairs={{0,1},{1,0},{2,3},{3,2},{4,5},{5,4},{6,7},{7,6},{8,9},{9,8},{10,11... | collective-permute-start | bytes 6291464 | tf_op jit(solution)/shard_map/ppermute | solution.py:677
  143.8 8.4 %copy-start.25 = (bf16[864,768]{1,0:T(8,128)(2,1)S(1)}, bf16[864,768]{1,0:T(8,128)(2,1)}, u32[]{:S(2)}) copy-start(bf16[864,768]{1,0:T(8,128)(2,1)} %get-tuple-element.52.refs_1_) | copy-start | bytes 3981316
  145.6 36.1 %collective-permute-start.4 = (f32[32,8,512]{2,1,0:T(8,128)}, f32[32,8,512]{2,1,0:T(8,128)S(1)}, u32[]{:S(2)}, u32[]{:S(2)}) collective-permute-start(f32[32,8,512]{2,1,0:T(8,128)} %bitcast.14.refs_5_), channel_id=1, source_target_pairs={{0,32},{1,33},{2,34},{3,35},{4,36},{5,37},{6,38},{7,39},{8,40},{9,... | collective-permute-start | bytes 1572872 | tf_op jit(solution)/shard_map/ppermute | solution.py:500
  147.5 34.2 %collective-permute-start.5 = (f32[32,8,512]{2,1,0:T(8,128)}, f32[32,8,512]{2,1,0:T(8,128)S(1)}, u32[]{:S(2)}, u32[]{:S(2)}) collective-permute-start(f32[32,8,512]{2,1,0:T(8,128)} %bitcast.15.refs_6_), channel_id=1, source_target_pairs={{0,96},{1,97},{2,98},{3,99},{4,100},{5,101},{6,102},{7,103},{8,104... | collective-permute-start | bytes 1572872 | tf_op jit(solution)/shard_map/ppermute | solution.py:500
  174.5 32.9 %all-to-all-start.1 = ((bf16[16,448,128]{2,1,0:T(8,128)(2,1)}), bf16[16,448,128]{2,1,0:T(8,128)(2,1)}, u32[]{:S(2)}, u32[]{:S(2)}) async-start(bf16[16,448,128]{2,1,0:T(8,128)(2,1)} %leave.1.refs_6_.refs_2_), calls=%async_computation.3 | async-start | bytes 3670016 | tf_op jit(solution)/shard_map/all_to_all | solution.py:694
  184.7 9.9 %collective-permute-start.6 = (f32[16,8,512]{2,1,0:T(8,128)}, f32[16,8,512]{2,1,0:T(8,128)S(1)}, u32[]{:S(2)}, u32[]{:S(2)}) collective-permute-start(f32[16,8,512]{2,1,0:T(8,128)} %bitcast.23), channel_id=1, source_target_pairs={{0,96},{1,97},{2,98},{3,99},{4,100},{5,101},{6,102},{7,103},{8,104... | collective-permute-start | bytes 786440 | tf_op jit(solution)/shard_map/ppermute | solution.py:500
  185.4 9.5 %collective-permute-start.7 = (f32[16,8,512]{2,1,0:T(8,128)}, f32[16,8,512]{2,1,0:T(8,128)}, u32[]{:S(2)}, u32[]{:S(2)}) collective-permute-start(f32[16,8,512]{2,1,0:T(8,128)} %bitcast.27), channel_id=1, source_target_pairs={{0,32},{1,33},{2,34},{3,35},{4,36},{5,37},{6,38},{7,39},{8,40},{9,... | collective-permute-start | bytes 786440 | tf_op jit(solution)/shard_map/ppermute | solution.py:500
  185.7 13.2 %copy-start.20 = (bf16[864,256]{1,0:T(8,128)(2,1)S(1)}, bf16[864,256]{1,0:T(8,128)(2,1)}, u32[]{:S(2)}) copy-start(bf16[864,256]{1,0:T(8,128)(2,1)} %get-tuple-element.46.refs_0_.refs_2_) | copy-start | bytes 1327108
  186.8 12.2 %copy-start = (bf16[1024,1024]{1,0:T(8,128)(2,1)S(1)}, bf16[1024,1024]{1,0:T(8,128)(2,1)}, u32[]{:S(2)}) copy-start(bf16[1024,1024]{1,0:T(8,128)(2,1)} %refs_5_.9) | copy-start | bytes 6291460
  186.8 12.2 %copy-start.9 = (bf16[864,1024]{1,0:T(8,128)(2,1)S(1)}, bf16[864,1024]{1,0:T(8,128)(2,1)}, u32[]{:S(2)}) copy-start(bf16[864,1024]{1,0:T(8,128)(2,1)} %get-tuple-element.50.refs_1_.refs_4_) | copy-start | bytes 5308420
  188.8 23.2 %collective-permute-start.9 = (f32[8,8,3072]{2,1,0:T(8,128)}, f32[8,8,3072]{2,1,0:T(8,128)S(1)}, u32[]{:S(2)}, u32[]{:S(2)}) collective-permute-start(f32[8,8,3072]{2,1,0:T(8,128)} %pad_maximum_fusion), channel_id=1, source_target_pairs={{0,32},{1,33},{2,34},{3,35},{4,36},{5,37},{6,38},{7,39},{8,40},{9,... | collective-permute-start | bytes 2359304 | tf_op jit(solution)/shard_map/ppermute | solution.py:500
  197.1 10.3 %collective-permute-start.8 = (f32[8,8,1024]{2,1,0:T(8,128)S(1)}, f32[8,8,1024]{2,1,0:T(8,128)S(1)}, u32[]{:S(2)}, u32[]{:S(2)}) collective-permute-start(f32[8,8,1024]{2,1,0:T(8,128)S(1)} %pad_maximum_fusion.2), channel_id=1, source_target_pairs={{0,4},{1,5},{2,6},{3,7},{4,0},{5,1},{6,2},{7,3},{8,12},{9,13},{10,... | collective-permute-start | bytes 786440 | tf_op jit(solution)/shard_map/ppermute | solution.py:500
  212.0 13.2 %copy-start.3 = (f32[512,1024]{1,0:T(8,128)S(1)}, f32[512,1024]{1,0:T(8,128)}, u32[]{:S(2)}) copy-start(f32[512,1024]{1,0:T(8,128)} %get-tuple-element.55) | copy-start | bytes 6291460
  212.0 13.2 %copy-start.11 = (f32[4,2,4,8,512]{4,3,2,1,0:T(8,128)S(1)}, f32[4,2,4,8,512]{4,3,2,1,0:T(8,128)}, u32[]{:S(2)}) copy-start(f32[4,2,4,8,512]{4,3,2,1,0:T(8,128)} %copy-done.10) | copy-start | bytes 1572868
  212.0 13.2 %copy-start.15 = (f32[2,1,4,8,1024]{4,3,2,1,0:T(8,128)S(1)}, f32[2,1,4,8,1024]{4,3,2,1,0:T(8,128)}, u32[]{:S(2)}) copy-start(f32[2,1,4,8,1024]{4,3,2,1,0:T(8,128)} %get-tuple-element.62) | copy-start | bytes 786436
  212.0 13.2 %copy-start.32 = (f32[1,128]{1,0:T(1,128)S(1)}, f32[1,128]{1,0:T(1,128)}, u32[]{:S(2)}) copy-start(f32[1,128]{1,0:T(1,128)} %get-tuple-element.63.refs_21_.gain_ref) | copy-start | bytes 1540
  213.3 11.9 %collective-permute-start.10 = (f32[4,8,3072]{2,1,0:T(8,128)S(1)}, f32[4,8,3072]{2,1,0:T(8,128)S(1)}, u32[]{:S(2)}, u32[]{:S(2)}) collective-permute-start(f32[4,8,3072]{2,1,0:T(8,128)S(1)} %pad_maximum_fusion.1), channel_id=1, source_target_pairs={{0,96},{1,97},{2,98},{3,99},{4,100},{5,101},{6,102},{7,103},{8,104... | collective-permute-start | bytes 1179656 | tf_op jit(solution)/shard_map/ppermute | solution.py:500
  215.7 6.3 %collective-permute-start.11 = (f32[4,8,1024]{2,1,0:T(8,128)S(1)}, f32[4,8,1024]{2,1,0:T(8,128)S(1)}, u32[]{:S(2)}, u32[]{:S(2)}) collective-permute-start(f32[4,8,1024]{2,1,0:T(8,128)S(1)} %pad_maximum_fusion.3), channel_id=1, source_target_pairs={{0,12},{1,13},{2,14},{3,15},{4,8},{5,9},{6,10},{7,11},{8,4},{9,5},... | collective-permute-start | bytes 393224 | tf_op jit(solution)/shard_map/ppermute | solution.py:500
  230.9 17.5 %copy-start.7 = (bf16[864,1024]{1,0:T(8,128)(2,1)S(1)}, bf16[864,1024]{1,0:T(8,128)(2,1)}, u32[]{:S(2)}) copy-start(bf16[864,1024]{1,0:T(8,128)(2,1)} %copy-done.6) | copy-start | bytes 5308420
  232.0 11.0 %collective-permute-start.12 = (f32[8,4224]{1,0:T(8,128)S(1)}, f32[8,4224]{1,0:T(8,128)S(1)}, u32[]{:S(2)}, u32[]{:S(2)}) collective-permute-start(f32[8,4224]{1,0:T(8,128)S(1)} %get-tuple-element.65), channel_id=1, source_target_pairs={{0,16},{1,17},{2,18},{3,19},{4,20},{5,21},{6,22},{7,23},{8,24},{9,... | collective-permute-start | bytes 405512 | tf_op jit(solution)/shard_map/ppermute | solution.py:712
  232.9 8.7 %collective-permute-start.13 = (f32[8,4096]{1,0:T(8,128)S(1)}, f32[8,4096]{1,0:T(8,128)S(1)}, u32[]{:S(2)}, u32[]{:S(2)}) collective-permute-start(f32[8,4096]{1,0:T(8,128)S(1)} %get-tuple-element.66), channel_id=1, source_target_pairs={{0,2},{1,3},{2,0},{3,1},{4,6},{5,7},{6,4},{7,5},{8,10},{9,11},{10,... | collective-permute-start | bytes 393224 | tf_op jit(solution)/shard_map/ppermute | solution.py:712
  236.5 6.6 %collective-permute-start.14 = (f32[8,4096]{1,0:T(8,128)S(1)}, f32[8,4096]{1,0:T(8,128)S(1)}, u32[]{:S(2)}, u32[]{:S(2)}) collective-permute-start(f32[8,4096]{1,0:T(8,128)S(1)} %get-tuple-element.67), channel_id=1, source_target_pairs={{0,18},{1,19},{2,16},{3,17},{4,22},{5,23},{6,20},{7,21},{8,26},{9,... | collective-permute-start | bytes 393224 | tf_op jit(solution)/shard_map/ppermute | solution.py:712
  243.7 11.5 %collective-permute-start.15 = (f32[8,384]{1,0:T(8,128)S(1)}, f32[8,384]{1,0:T(8,128)S(1)}, u32[]{:S(2)}, u32[]{:S(2)}) collective-permute-start(f32[8,384]{1,0:T(8,128)S(1)} %get-tuple-element.70), channel_id=1, source_target_pairs={{0,32},{1,33},{2,34},{3,35},{4,36},{5,37},{6,38},{7,39},{8,40},{9,... | collective-permute-start | bytes 36872 | tf_op jit(solution)/shard_map/ppermute | solution.py:714
  243.7 11.5 %collective-permute-start.16 = (f32[8,384]{1,0:T(8,128)S(1)}, f32[8,384]{1,0:T(8,128)S(1)}, u32[]{:S(2)}, u32[]{:S(2)}) collective-permute-start(f32[8,384]{1,0:T(8,128)S(1)} %get-tuple-element.71), channel_id=1, source_target_pairs={{0,64},{1,65},{2,66},{3,67},{4,68},{5,69},{6,70},{7,71},{8,72},{9,... | collective-permute-start | bytes 36872 | tf_op jit(solution)/shard_map/ppermute | solution.py:714
  245.5 9.7 %collective-permute-start.17 = (f32[8,384]{1,0:T(8,128)S(1)}, f32[8,384]{1,0:T(8,128)S(1)}, u32[]{:S(2)}, u32[]{:S(2)}) collective-permute-start(f32[8,384]{1,0:T(8,128)S(1)} %get-tuple-element.72), channel_id=1, source_target_pairs={{0,96},{1,97},{2,98},{3,99},{4,100},{5,101},{6,102},{7,103},{8,104... | collective-permute-start | bytes 36872 | tf_op jit(solution)/shard_map/ppermute | solution.py:714
  (26 other events, 72.7 us)
Sparse Core Ops, SparseCore 0:
  80.4 28.2 reduce-scatter.3
  117.3 28.2 reduce-scatter.5
  148.1 29.3 reduce-scatter.7
